TPU v7x, 32 devices: a whole 2x2x4 slice. The times are simulated.
32 devices in a mesh: dp: 4 (over y, core), rows: 2 (over x), chan: 4 (over z).
Axes of the slice: x: 2, y: 2, z: 4, core: 2. Of those that a mesh axis runs over, the one named last changes fastest.
Arguments:
- pair: bfloat16 [16, 128, 128, 128], P('dp', 'rows', 'chan'), may hold values from -6 to 6
- node: bfloat16 [16, 128, 256], P('dp', 'rows', 'chan'), may hold values from -6 to 6
- pair_cot: bfloat16 [16, 128, 128, 128], P('dp', 'rows', 'chan'), may hold values from -6 to 6
- node_cot: bfloat16 [16, 128, 256], P('dp', 'rows', 'chan'), may hold values from -6 to 6
- lengths: int32 [16], P('dp'), may hold values from 32 to 128, as said below
- present: int32 [16, 128], P('dp'), may hold values 0 or 1
- gain_pair: float32 [128], replicated, may hold values from 0.5 to 1.5
- w_tri_in: bfloat16 [2, 4, 128, 128], P(None, None, None, 'chan'), may hold values from -0.5 to 0.5
- w_out_gate: bfloat16 [2, 128, 128], P(None, None, 'chan'), may hold values from -0.5 to 0.5
- gain_tri: float32 [2, 128], replicated, may hold values from 0.5 to 1.5
- w_tri_out: bfloat16 [2, 128, 128], P(None, None, 'chan'), may hold values from -0.75 to 0.75
- gain_trans: float32 [128], replicated, may hold values from 0.5 to 1.5
- w_trans_in: bfloat16 [128, 512], P(None, 'chan'), may hold values from -0.5 to 0.5
- w_trans_out: bfloat16 [512, 128], P('chan'), may hold values from -0.5 to 0.5
- w_bias: bfloat16 [128, 8], P(None, 'chan'), may hold values from -0.5 to 0.5
- gain_node: float32 [256], replicated, may hold values from 0.5 to 1.5
- w_qkv: bfloat16 [3, 256, 256], P(None, None, 'chan'), may hold values from -0.375 to 0.375
- w_attn_out: bfloat16 [256, 256], P(None, 'chan'), may hold values from -1.5 to 1.5
- gain_node_trans: float32 [256], replicated, may hold values from 0.5 to 1.5
- w_node_in: bfloat16 [256, 1024], P(None, 'chan'), may hold values from -0.375 to 0.375
- w_node_out: bfloat16 [1024, 256], P('chan'), may hold values from -0.375 to 0.375
Outputs:
- pair_out: bfloat16 [16, 128, 128, 128], P('dp', 'rows', 'chan')
- node_out: bfloat16 [16, 128, 256], P('dp', 'rows', 'chan')
- pair_grad: bfloat16 [16, 128, 128, 128], P('dp', 'rows', 'chan')
- node_grad: bfloat16 [16, 128, 256], P('dp', 'rows', 'chan')
- grad_gain_pair: float32 [128], P('chan')
- grad_w_tri_in: float32 [2, 4, 128, 128], P(None, None, None, 'chan')
- grad_w_out_gate: float32 [2, 128, 128], P(None, None, 'chan')
- grad_gain_tri: float32 [2, 128], P(None, 'chan')
- grad_w_tri_out: float32 [2, 128, 128], P(None, None, 'chan')
- grad_gain_trans: float32 [128], P('chan')
- grad_w_trans_in: float32 [128, 512], P(None, 'chan')
- grad_w_trans_out: float32 [512, 128], P('chan')
- grad_w_bias: float32 [128, 8], P(None, 'chan')
- grad_gain_node: float32 [256], P('chan')
- grad_w_qkv: float32 [3, 256, 256], P(None, None, 'chan')
- grad_w_attn_out: float32 [256, 256], P(None, 'chan')
- grad_gain_node_trans: float32 [256], P('chan')
- grad_w_node_in: float32 [256, 1024], P(None, 'chan')
- grad_w_node_out: float32 [1024, 256], P('chan')
Inputs may be any that keep to these rules, and one draw needn't show every extreme that they name: `lengths`: each group of 4 consecutive crops holds one crop of length 128.
All inputs are finite; a program needn't handle non-finite values. No bound on the sum of `present` on one device may be relied on, other than what follows from the above.
Results may differ from a plain program's by a relative error of at most 0.024.
Values may be sent and summed in bfloat16 or wider, within the bound.
No kernel may reach another device: no remote copies, remote signals or barrier semaphores. Data moves between devices by JAX's collectives and lax.ppermute only.
A program may use at most 384 MiB of HBM per device.

v0:
```python
import math

import jax
import jax.numpy as jnp
from jax import lax
from jax.sharding import PartitionSpec as P

epsilon = 1e-05
masked_score = -1000000000.0


def norm_parts(full):
    mean = jnp.mean(full, axis=2, keepdims=True)
    centered = full - mean
    variance = jnp.mean(centered * centered, axis=2, keepdims=True)
    inverse = lax.rsqrt(variance + epsilon)
    return (centered * inverse, inverse)


def shaped(gain, full):
    return gain.reshape(gain.shape + (1,) * (full.ndim - 3))


def normed(full, gain):
    scaled, inverse = norm_parts(full)
    return scaled * shaped(gain, full)


def stat_terms(full, gain, partial_value, groups):
    scaled, inverse = norm_parts(full)
    weighted = shaped(gain, full) * partial_value
    first_sum = jnp.sum(weighted, axis=2)
    second_sum = jnp.sum(weighted * scaled, axis=2)
    stacked = jnp.stack([first_sum, second_sum], axis=2)
    repeats = (1, 1, groups) + (1,) * (full.ndim - 3)
    return jnp.tile(stacked, repeats)


def norm_finish(full, gain, grad_here, totals, chan_index):
    width = full.shape[2]
    here = grad_here.shape[2]
    scaled, inverse = norm_parts(full)
    scaled_here = lax.dynamic_slice_in_dim(scaled, chan_index * here, here, 2)
    gain_here = lax.dynamic_slice_in_dim(gain, chan_index * here, here, 0)
    first_mean = totals[:, :, 0:1] / width
    second_mean = totals[:, :, 1:2] / width
    grad_input = inverse * (
        shaped(gain_here, full) * grad_here - first_mean - scaled_here * second_mean
    )
    summed_axes = (0, 1) + tuple(range(3, full.ndim))
    grad_gain = jnp.sum(grad_here * scaled_here, axis=summed_axes)
    return (grad_input, grad_gain)


def gelu_exact(value):
    return jax.nn.gelu(value, approximate=False)


def softmax_rows(scores):
    top = jnp.max(scores, axis=-1, keepdims=True)
    exps = jnp.exp(scores - top)
    return exps / jnp.sum(exps, axis=-1, keepdims=True)


def shards(
    pair,
    node,
    pair_cot,
    node_cot,
    lengths,
    present,
    gain_pair,
    w_tri_in,
    w_out_gate,
    gain_tri,
    w_tri_out,
    gain_trans,
    w_trans_in,
    w_trans_out,
    w_bias,
    gain_node,
    w_qkv,
    w_attn_out,
    gain_node_trans,
    w_node_in,
    w_node_out,
):
    batch = pair.shape[0]
    rows_here = pair.shape[1]
    crop_len = pair.shape[3]
    groups = lax.axis_size("chan")
    chan_index = lax.axis_index("chan")
    row_start = lax.axis_index("rows") * rows_here
    heads_here = w_bias.shape[1]
    head_dim = w_qkv.shape[2] // heads_here
    scale = 1.0 / math.sqrt(head_dim)
    positions = jnp.arange(crop_len, dtype=jnp.int32)
    mask_all = present.astype(jnp.float32) * (positions[None, :] < lengths[:, None]).astype(
        jnp.float32
    )
    mask_rows = lax.dynamic_slice_in_dim(mask_all, row_start, rows_here, 1)
    pair_mask = mask_rows[:, :, None, None] * mask_all[:, None, None, :]
    key_live = mask_all[:, None, None, :] > 0.5

    def gating(gate, value):
        return jax.nn.sigmoid(gate) * value * pair_mask

    pair_whole, node_whole = (
        lax.all_gather(pair, "chan", axis=2, tiled=True),
        lax.all_gather(node, "chan", axis=2, tiled=True),
    )
    full_in = pair_whole.astype(jnp.float32)
    node_full = node_whole.astype(jnp.float32)
    stream_in = pair.astype(jnp.float32)
    node_in = node.astype(jnp.float32)
    normed_in = normed(full_in, gain_pair).astype(jnp.bfloat16)
    projected = jnp.einsum(
        "bicj,dgch->dgbihj", normed_in, w_tri_in, preferred_element_type=jnp.float32
    )
    gate_pre = jnp.einsum(
        "bicj,dcx->dbixj", normed_in, w_out_gate, preferred_element_type=jnp.float32
    )
    bias = jnp.einsum("bicj,ch->bhij", normed_in, w_bias, preferred_element_type=jnp.float32)
    left_out = gating(projected[0, 0], projected[0, 1]).astype(jnp.bfloat16)
    right_out = gating(projected[0, 2], projected[0, 3]).astype(jnp.bfloat16)
    left_in = gating(projected[1, 0], projected[1, 1]).astype(jnp.bfloat16)
    right_in = gating(projected[1, 2], projected[1, 3]).astype(jnp.bfloat16)
    normed_node = normed(node_full, gain_node).astype(jnp.bfloat16)
    qkv = jnp.einsum(
        "bin,gna->gbia", normed_node, w_qkv, preferred_element_type=jnp.float32
    ).astype(jnp.bfloat16)
    whole_right_out, whole_right_in, whole_keys, whole_values = (
        lax.all_gather(right_out, "rows", axis=1, tiled=True),
        lax.all_gather(right_in, "rows", axis=1, tiled=True),
        lax.all_gather(qkv[1], "rows", axis=1, tiled=True),
        lax.all_gather(qkv[2], "rows", axis=1, tiled=True),
    )
    left_cols = lax.all_to_all(left_in, "rows", split_axis=3, concat_axis=1, tiled=True)
    queries = qkv[0].reshape(batch, rows_here, heads_here, head_dim)
    keys = whole_keys.reshape(batch, crop_len, heads_here, head_dim)
    values = whole_values.reshape(batch, crop_len, heads_here, head_dim)
    raw = (
        jnp.einsum("bihd,bjhd->bhij", queries, keys, preferred_element_type=jnp.float32) * scale
        + bias
    )
    probs = softmax_rows(jnp.where(key_live, raw, masked_score))
    probs_low = probs.astype(jnp.bfloat16)
    attn = jnp.einsum(
        "bhij,bjhd->bihd", probs_low, values, preferred_element_type=jnp.float32
    ).astype(jnp.bfloat16)
    attn = attn.reshape(batch, rows_here, heads_here * head_dim)
    tri_out = jnp.einsum(
        "bihk,bjhk->bihj", left_out, whole_right_out, preferred_element_type=jnp.float32
    )
    tri_in = jnp.einsum(
        "bkhi,bkhj->bihj", left_cols, whole_right_in, preferred_element_type=jnp.float32
    )
    tri_full_out, tri_full_in, attn_whole = (
        lax.all_gather(tri_out.astype(jnp.bfloat16), "chan", axis=2, tiled=True).astype(
            tri_out.dtype
        ),
        lax.all_gather(tri_in.astype(jnp.bfloat16), "chan", axis=2, tiled=True).astype(
            tri_in.dtype
        ),
        lax.all_gather(
            attn.astype(jnp.float32).astype(jnp.bfloat16), "chan", axis=2, tiled=True
        ).astype(jnp.float32),
    )
    normed_out = normed(tri_full_out, gain_tri[0]).astype(jnp.bfloat16)
    normed_inc = normed(tri_full_in, gain_tri[1]).astype(jnp.bfloat16)
    branch_out = jnp.einsum(
        "bihj,hc->bicj", normed_out, w_tri_out[0], preferred_element_type=jnp.float32
    )
    branch_inc = jnp.einsum(
        "bihj,hc->bicj", normed_inc, w_tri_out[1], preferred_element_type=jnp.float32
    )
    gate_sig = jax.nn.sigmoid(gate_pre)
    stream_mid = stream_in + gate_sig[0] * branch_out + gate_sig[1] * branch_inc
    attn_low = attn_whole.astype(jnp.bfloat16)
    node_mid = node_in + jnp.einsum(
        "bia,an->bin", attn_low, w_attn_out, preferred_element_type=jnp.float32
    )
    full_mid, node_full_mid = (
        lax.all_gather(stream_mid.astype(jnp.bfloat16), "chan", axis=2, tiled=True).astype(
            stream_mid.dtype
        ),
        lax.all_gather(node_mid.astype(jnp.bfloat16), "chan", axis=2, tiled=True).astype(
            node_mid.dtype
        ),
    )
    normed_mid = normed(full_mid, gain_trans).astype(jnp.bfloat16)
    pre_hidden = jnp.einsum(
        "bicj,cf->bifj", normed_mid, w_trans_in, preferred_element_type=jnp.float32
    )
    hidden, gelu_pull = jax.vjp(gelu_exact, pre_hidden)
    hidden_low = hidden.astype(jnp.bfloat16)
    out_terms = jnp.einsum(
        "bifj,fc->bicj", hidden_low, w_trans_out, preferred_element_type=jnp.float32
    )
    normed_node_mid = normed(node_full_mid, gain_node_trans).astype(jnp.bfloat16)
    node_pre = jnp.einsum(
        "bin,nf->bif", normed_node_mid, w_node_in, preferred_element_type=jnp.float32
    )
    node_hidden, node_gelu_pull = jax.vjp(gelu_exact, node_pre)
    node_hidden_low = node_hidden.astype(jnp.bfloat16)
    node_terms = jnp.einsum(
        "bif,fn->bin", node_hidden_low, w_node_out, preferred_element_type=jnp.float32
    )
    pair_sum, node_sum = (
        lax.psum_scatter(
            out_terms.astype(jnp.bfloat16), "chan", scatter_dimension=2, tiled=True
        ).astype(jnp.float32),
        lax.psum_scatter(
            node_terms.astype(jnp.bfloat16), "chan", scatter_dimension=2, tiled=True
        ).astype(jnp.float32),
    )
    stream_out = stream_mid + pair_sum
    node_out = node_mid + node_sum
    cot_full, node_cot_full = (
        lax.all_gather(pair_cot, "chan", axis=2, tiled=True),
        lax.all_gather(node_cot, "chan", axis=2, tiled=True),
    )
    grad_trans_out = jnp.einsum(
        "bifj,bicj->fc", hidden_low, cot_full, preferred_element_type=jnp.float32
    )
    grad_hidden = jnp.einsum(
        "bicj,fc->bifj", cot_full, w_trans_out, preferred_element_type=jnp.float32
    )
    grad_pre = gelu_pull(grad_hidden)[0].astype(jnp.bfloat16)
    grad_trans_in = jnp.einsum(
        "bicj,bifj->cf", normed_mid, grad_pre, preferred_element_type=jnp.float32
    )
    grad_normed_mid = jnp.einsum(
        "bifj,cf->bicj", grad_pre, w_trans_in, preferred_element_type=jnp.float32
    )
    mid_terms = stat_terms(full_mid, gain_trans, grad_normed_mid, groups)
    grad_node_out_w = jnp.einsum(
        "bif,bin->fn", node_hidden_low, node_cot_full, preferred_element_type=jnp.float32
    )
    grad_node_hidden = jnp.einsum(
        "bin,fn->bif", node_cot_full, w_node_out, preferred_element_type=jnp.float32
    )
    grad_node_pre = node_gelu_pull(grad_node_hidden)[0].astype(jnp.bfloat16)
    grad_node_in_w = jnp.einsum(
        "bin,bif->nf", normed_node_mid, grad_node_pre, preferred_element_type=jnp.float32
    )
    grad_normed_node_mid = jnp.einsum(
        "bif,nf->bin", grad_node_pre, w_node_in, preferred_element_type=jnp.float32
    )
    node_mid_terms = stat_terms(node_full_mid, gain_node_trans, grad_normed_node_mid, groups)
    mid_here, mid_totals, node_mid_here, node_mid_totals = (
        lax.psum_scatter(
            grad_normed_mid.astype(jnp.bfloat16), "chan", scatter_dimension=2, tiled=True
        ).astype(jnp.float32),
        lax.psum_scatter(
            mid_terms.astype(jnp.bfloat16), "chan", scatter_dimension=2, tiled=True
        ).astype(jnp.float32),
        lax.psum_scatter(
            grad_normed_node_mid.astype(jnp.bfloat16), "chan", scatter_dimension=2, tiled=True
        ).astype(jnp.float32),
        lax.psum_scatter(
            node_mid_terms.astype(jnp.bfloat16), "chan", scatter_dimension=2, tiled=True
        ).astype(jnp.float32),
    )
    mid_extra, grad_gain_trans = norm_finish(full_mid, gain_trans, mid_here, mid_totals, chan_index)
    node_mid_extra, grad_gain_node_trans = norm_finish(
        node_full_mid, gain_node_trans, node_mid_here, node_mid_totals, chan_index
    )
    grad_mid = pair_cot.astype(jnp.float32) + mid_extra
    grad_node_mid = node_cot.astype(jnp.float32) + node_mid_extra
    branches = jnp.stack([branch_out, branch_inc])
    grad_branch = (gate_sig * grad_mid[None]).astype(jnp.bfloat16)
    grad_gate = (grad_mid[None] * branches * gate_sig * (1.0 - gate_sig)).astype(jnp.bfloat16)
    tri_normed_both = jnp.stack([normed_out, normed_inc])
    grad_w_tri_out = jnp.einsum(
        "dbihj,dbicj->dhc", tri_normed_both, grad_branch, preferred_element_type=jnp.float32
    )
    grad_out_gate = jnp.einsum(
        "bicj,dbixj->dcx", normed_in, grad_gate, preferred_element_type=jnp.float32
    )
    grad_tri_normed = jnp.einsum(
        "dbicj,dhc->dbihj", grad_branch, w_tri_out, preferred_element_type=jnp.float32
    )
    out_stats = stat_terms(tri_full_out, gain_tri[0], grad_tri_normed[0], groups)
    inc_stats = stat_terms(tri_full_in, gain_tri[1], grad_tri_normed[1], groups)
    grad_attn_branch = grad_node_mid.astype(jnp.bfloat16)
    grad_w_attn_out = jnp.einsum(
        "bia,bin->an", attn_low, grad_attn_branch, preferred_element_type=jnp.float32
    )
    attn_terms = jnp.einsum(
        "bin,an->bia", grad_attn_branch, w_attn_out, preferred_element_type=jnp.float32
    )
    out_here, out_totals, inc_here, inc_totals, attn_here = (
        lax.psum_scatter(
            grad_tri_normed[0].astype(jnp.bfloat16), "chan", scatter_dimension=2, tiled=True
        ).astype(jnp.float32),
        lax.psum_scatter(
            out_stats.astype(jnp.bfloat16), "chan", scatter_dimension=2, tiled=True
        ).astype(jnp.float32),
        lax.psum_scatter(
            grad_tri_normed[1].astype(jnp.bfloat16), "chan", scatter_dimension=2, tiled=True
        ).astype(jnp.float32),
        lax.psum_scatter(
            inc_stats.astype(jnp.bfloat16), "chan", scatter_dimension=2, tiled=True
        ).astype(jnp.float32),
        lax.psum_scatter(
            attn_terms.astype(jnp.bfloat16), "chan", scatter_dimension=2, tiled=True
        ).astype(jnp.float32),
    )
    grad_tri_a, gain_grad_out = norm_finish(
        tri_full_out, gain_tri[0], out_here, out_totals, chan_index
    )
    grad_tri_b, gain_grad_inc = norm_finish(
        tri_full_in, gain_tri[1], inc_here, inc_totals, chan_index
    )
    grad_gain_tri = jnp.stack([gain_grad_out, gain_grad_inc])
    grad_out_low = grad_tri_a.astype(jnp.bfloat16)
    grad_inc_low = grad_tri_b.astype(jnp.bfloat16)
    grad_attn = attn_here.astype(jnp.bfloat16).reshape(batch, rows_here, heads_here, head_dim)
    grad_probs = jnp.einsum(
        "bihd,bjhd->bhij", grad_attn, values, preferred_element_type=jnp.float32
    )
    delta = jnp.sum(probs * grad_probs, axis=3, keepdims=True)
    grad_scores = (probs * (grad_probs - delta)).astype(jnp.bfloat16)
    grad_queries = (
        jnp.einsum("bhij,bjhd->bihd", grad_scores, keys, preferred_element_type=jnp.float32) * scale
    )
    key_terms = (
        jnp.einsum("bhij,bihd->bjhd", grad_scores, queries, preferred_element_type=jnp.float32)
        * scale
    )
    value_terms = jnp.einsum(
        "bhij,bihd->bjhd", probs_low, grad_attn, preferred_element_type=jnp.float32
    )
    grad_w_bias = jnp.einsum(
        "bicj,bhij->ch", normed_in, grad_scores, preferred_element_type=jnp.float32
    )
    bias_back = jnp.einsum("bhij,ch->bicj", grad_scores, w_bias, preferred_element_type=jnp.float32)
    grad_left_out = jnp.einsum(
        "bihj,bjhk->bihk", grad_out_low, whole_right_out, preferred_element_type=jnp.float32
    )
    right_terms = jnp.einsum(
        "bihj,bihk->bjhk", grad_out_low, left_out, preferred_element_type=jnp.float32
    )
    grad_right_out, key_grads, value_grads = (
        lax.psum_scatter(
            right_terms.astype(jnp.bfloat16), "rows", scatter_dimension=1, tiled=True
        ).astype(jnp.float32),
        lax.psum_scatter(
            key_terms.astype(jnp.bfloat16), "rows", scatter_dimension=1, tiled=True
        ).astype(jnp.float32),
        lax.psum_scatter(
            value_terms.astype(jnp.bfloat16), "rows", scatter_dimension=1, tiled=True
        ).astype(jnp.float32),
    )
    whole_grad_in = lax.all_gather(grad_inc_low, "rows", axis=1, tiled=True)
    grad_left_in = jnp.einsum(
        "bihj,bkhj->bkhi", whole_grad_in, right_in, preferred_element_type=jnp.float32
    )
    grad_right_in = jnp.einsum(
        "bkhi,bihj->bkhj", left_in, whole_grad_in, preferred_element_type=jnp.float32
    )

    def gate_back(first, second, grad):
        kept_value, pull = jax.vjp(gating, first, second)
        return pull(grad)

    left_gate_out, left_value_out = gate_back(projected[0, 0], projected[0, 1], grad_left_out)
    right_gate_out, right_value_out = gate_back(projected[0, 2], projected[0, 3], grad_right_out)
    left_gate_in, left_value_in = gate_back(projected[1, 0], projected[1, 1], grad_left_in)
    right_gate_in, right_value_in = gate_back(projected[1, 2], projected[1, 3], grad_right_in)
    grad_proj = jnp.stack(
        [
            jnp.stack([left_gate_out, left_value_out, right_gate_out, right_value_out]),
            jnp.stack([left_gate_in, left_value_in, right_gate_in, right_value_in]),
        ]
    ).astype(jnp.bfloat16)
    grad_tri_in_w = jnp.einsum(
        "bicj,dgbihj->dgch", normed_in, grad_proj, preferred_element_type=jnp.float32
    )
    grad_normed_in = jnp.einsum(
        "dgbihj,dgch->bicj", grad_proj, w_tri_in, preferred_element_type=jnp.float32
    )
    grad_normed_in = grad_normed_in + jnp.einsum(
        "dbixj,dcx->bicj", grad_gate, w_out_gate, preferred_element_type=jnp.float32
    )
    grad_normed_in = grad_normed_in + bias_back
    grad_qkv = jnp.stack(
        [
            grad_queries.reshape(batch, rows_here, heads_here * head_dim),
            key_grads.reshape(batch, rows_here, heads_here * head_dim),
            value_grads.reshape(batch, rows_here, heads_here * head_dim),
        ]
    ).astype(jnp.bfloat16)
    grad_w_qkv = jnp.einsum(
        "bin,gbia->gna", normed_node, grad_qkv, preferred_element_type=jnp.float32
    )
    grad_normed_node = jnp.einsum(
        "gbia,gna->bin", grad_qkv, w_qkv, preferred_element_type=jnp.float32
    )
    in_terms = stat_terms(full_in, gain_pair, grad_normed_in, groups)
    node_in_terms = stat_terms(node_full, gain_node, grad_normed_node, groups)
    in_here, in_totals, node_in_here, node_in_totals = (
        lax.psum_scatter(
            grad_normed_in.astype(jnp.bfloat16), "chan", scatter_dimension=2, tiled=True
        ).astype(jnp.float32),
        lax.psum_scatter(
            in_terms.astype(jnp.bfloat16), "chan", scatter_dimension=2, tiled=True
        ).astype(jnp.float32),
        lax.psum_scatter(
            grad_normed_node.astype(jnp.bfloat16), "chan", scatter_dimension=2, tiled=True
        ).astype(jnp.float32),
        lax.psum_scatter(
            node_in_terms.astype(jnp.bfloat16), "chan", scatter_dimension=2, tiled=True
        ).astype(jnp.float32),
    )
    in_extra, grad_gain_pair = norm_finish(full_in, gain_pair, in_here, in_totals, chan_index)
    node_in_extra, grad_gain_node = norm_finish(
        node_full, gain_node, node_in_here, node_in_totals, chan_index
    )
    grad_stream = grad_mid + in_extra
    node_grad = grad_node_mid + node_in_extra
    summed = lax.psum(
        (
            grad_gain_pair,
            grad_tri_in_w,
            grad_out_gate,
            grad_gain_tri,
            grad_w_tri_out,
            grad_gain_trans,
            grad_trans_in,
            grad_trans_out,
            grad_w_bias,
            grad_gain_node,
            grad_w_qkv,
            grad_w_attn_out,
            grad_gain_node_trans,
            grad_node_in_w,
            grad_node_out_w,
        ),
        ("dp", "rows"),
    )
    return (
        stream_out.astype(jnp.bfloat16),
        node_out.astype(jnp.bfloat16),
        grad_stream.astype(jnp.bfloat16),
        node_grad.astype(jnp.bfloat16),
        summed[0],
        summed[1],
        summed[2],
        summed[3],
        summed[4],
        summed[5],
        summed[6],
        summed[7],
        summed[8],
        summed[9],
        summed[10],
        summed[11],
        summed[12],
        summed[13],
        summed[14],
    )


def solution(mesh):
    in_specs = (
        P("dp", "rows", "chan", None),
        P("dp", "rows", "chan"),
        P("dp", "rows", "chan", None),
        P("dp", "rows", "chan"),
        P("dp"),
        P("dp", None),
        P(),
        P(None, None, None, "chan"),
        P(None, None, "chan"),
        P(),
        P(None, None, "chan"),
        P(),
        P(None, "chan"),
        P("chan", None),
        P(None, "chan"),
        P(),
        P(None, None, "chan"),
        P(None, "chan"),
        P(),
        P(None, "chan"),
        P("chan", None),
    )
    out_specs = (
        P("dp", "rows", "chan", None),
        P("dp", "rows", "chan"),
        P("dp", "rows", "chan", None),
        P("dp", "rows", "chan"),
        P("chan"),
        P(None, None, None, "chan"),
        P(None, None, "chan"),
        P(None, "chan"),
        P(None, None, "chan"),
        P("chan"),
        P(None, "chan"),
        P("chan", None),
        P(None, "chan"),
        P("chan"),
        P(None, None, "chan"),
        P(None, "chan"),
        P("chan"),
        P(None, "chan"),
        P("chan", None),
    )
    return jax.shard_map(shards, mesh=mesh, in_specs=in_specs, out_specs=out_specs, check_vma=False)
```

profile of v0, /device:TPU:8, one launch (start us, length us, event | category | flops | bytes accessed | tf_op | source)
XLA Modules:
  0.0 2315.7 jit_solution(10990880924844850911)
XLA Ops:
  9.0 148.5 %all-gather.11.cloned.1.call-done = bf16[4,64,128,128]{3,2,1,0:T(8,128)(2,1)} async-done(((bf16[4,64,32,128]{3,2,1,0:T(8,128)(2,1)}), bf16[4,64,128,128]{3,2,1,0:T(8,128)(2,1)}) %all-gather.11.cloned.1.call-update) | async-done | bytes 8388624 | tf_op jit(solution)/shard_map/all_gather | solution.py:109
  179.1 16.9 convolution_bitcast_fusion
  195.9 15.5 multiply_convert_fusion.10
  226.3 54.4 %all_to_all.18 = bf16[2,2,262144]{2,1,0:T(2,128)(2,1)} all-to-all(bf16[2,2,262144]{2,1,0:T(2,128)(2,1)} %reshape.263), channel_id=1, replica_groups=mesh['dp'=4,'rows'=2,'chan'=4] {'rows'}, dimensions={0} | all-to-all | bytes 4194304 | tf_op jit(solution)/shard_map/all_to_all | solution.py:138
  309.7 41.2 %all-gather.13.cloned.1.call-done = bf16[4,128,32,128]{3,2,1,0:T(8,128)(2,1)} async-done(((bf16[4,64,32,128]{3,2,1,0:T(8,128)(2,1)}), bf16[4,128,32,128]{3,2,1,0:T(8,128)(2,1)}) %all-gather.13.cloned.1.call-update) | async-done | bytes 4194320 | tf_op jit(solution)/shard_map/all_gather | solution.py:133
  368.9 130.1 %all-gather.19.cloned.1.call-done = bf16[4,64,128,128]{3,1,2,0:T(8,128)(2,1)} async-done(((bf16[4,64,32,128]{3,1,2,0:T(8,128)(2,1)}), bf16[4,64,128,128]{3,1,2,0:T(8,128)(2,1)}) %all-gather.19.cloned.1.call-update) | async-done | bytes 8388624 | tf_op jit(solution)/shard_map/all_gather | solution.py:162
  507.0 141.8 %all-gather.15.cloned.1.call-done = bf16[4,64,128,128]{3,1,2,0:T(8,128)(2,1)} async-done(((bf16[4,64,32,128]{3,1,2,0:T(8,128)(2,1)}), bf16[4,64,128,128]{3,1,2,0:T(8,128)(2,1)}) %all-gather.15.cloned.1.call-update) | async-done | bytes 8388624 | tf_op jit(solution)/shard_map/all_gather | solution.py:159
  696.3 18.0 all_gather.48
  725.9 18.0 all_gather.55
  750.9 24.1 %all_gather.51 = bf16[4,64,256]{1,0,2:T(4,128)(2,1)S(1)} all-gather(bf16[4,64,64]{1,0,2:T(4,128)(2,1)S(1)} %copy.289), channel_id=1, replica_groups=mesh['dp'=4,'rows'=2,'chan'=4] {'chan'}, dimensions={2}, use_global_device_ids=true | all-gather | bytes 163840 | tf_op jit(solution)/shard_map/all_gather | solution.py:165
  776.2 20.6 all_gather.52
  801.8 55.8 %all-gather.21.cloned.1.call-done = bf16[4,64,128,128]{3,2,1,0:T(8,128)(2,1)} async-done(((bf16[4,64,32,128]{3,2,1,0:T(8,128)(2,1)}), bf16[4,64,128,128]{3,2,1,0:T(8,128)(2,1)}) %all-gather.21.cloned.1.call-update) | async-done | bytes 8388624 | tf_op jit(solution)/shard_map/all_gather | solution.py:184
  868.4 42.3 %fusion.25 = (bf16[4,64,128,128]{2,3,1,0:T(8,128)(2,1)}, f32[4,64,128,128]{2,3,1,0:T(8,128)}, f32[4,64,128,128]{3,2,1,0:T(8,128)}) fusion(bf16[128,128]{1,0:T(8,128)(2,1)S(1)} %copy-done.72, f32[128]{0:T(128)S(1)} %copy-done.86, f32[4,64,128]{2,1,0:T(8,128)S(1)} %add_rsqrt_fusion, f32[4,64,128]{2,1,0:T(8,128)S(1)} %broadcast_multiply_fusion.1, ...), kind=kOutput, calls=%fused_computation.51 | convolution fusion | flops 1367343104 | bytes 50627072 | tf_op jit(solution)/shard_map/bicj,cf->bifj/dot_general | solution.py:192
  910.7 95.9 %all-gather.23.cloned.1.call-done = bf16[4,64,128,128]{3,2,1,0:T(8,128)(2,1)} async-done(((bf16[4,64,32,128]{3,2,1,0:T(8,128)(2,1)}), bf16[4,64,128,128]{3,2,1,0:T(8,128)(2,1)}) %all-gather.23.cloned.1.call-update) | async-done | bytes 8388624 | tf_op jit(solution)/shard_map/all_gather | solution.py:220
  1006.5 16.3 fusion.22
  1062.0 146.9 %reduce-scatter.40.cloned.1.call-done = bf16[4,64,32,128]{3,2,1,0:T(8,128)(2,1)} async-done(((bf16[4,64,128,128]{3,2,1,0:T(8,128)(2,1)}), bf16[4,64,32,128]{3,2,1,0:T(8,128)(2,1)}) %reduce-scatter.40.cloned.1.call-update) | async-done | bytes 2097168 | tf_op jit(solution)/shard_map/reduce_scatter | solution.py:252
  1223.0 17.9 fusion.118
  1240.9 31.9 %copy.465 = f32[2,4,64,128,128]{3,2,4,1,0:T(8,128)} copy(f32[2,4,64,128,128]{3,4,2,1,0:T(8,128)} %fusion.118) | data formatting | bytes 67108864 | tf_op jit(solution)/shard_map/dbicj,dhc->dbihj/dot_general | solution.py:281
  1272.9 21.1 fusion.45
  1295.0 17.4 fusion.41
  1368.4 112.9 %reduce-scatter.58.cloned.1.call-done = bf16[32,32768]{1,0:T(8,128)(2,1)} async-done(((bf16[128,32768]{1,0:T(8,128)(2,1)}), bf16[32,32768]{1,0:T(8,128)(2,1)}) %reduce-scatter.58.cloned.1.call-update) | async-done | bytes 2097168
  1489.0 14.1 reduce-scatter.44.cloned.1.call-done
  1504.1 146.8 %reduce-scatter.54.cloned.1.call-done = bf16[32,32768]{1,0:T(8,128)(2,1)} async-done(((bf16[128,32768]{1,0:T(8,128)(2,1)}), bf16[32,32768]{1,0:T(8,128)(2,1)}) %reduce-scatter.54.cloned.1.call-update) | async-done | bytes 2097168
  1707.7 28.0 %all-gather.25.cloned.1.call-done = bf16[4,128,32,128]{3,1,2,0:T(8,128)(2,1)} async-done(((bf16[4,64,32,128]{3,1,2,0:T(8,128)(2,1)}), bf16[4,128,32,128]{3,1,2,0:T(8,128)(2,1)}) %all-gather.25.cloned.1.call-update) | async-done | bytes 4194320 | tf_op jit(solution)/shard_map/all_gather | solution.py:356
  1747.0 45.3 %reduce-scatter.56.cloned.1.call-done = bf16[64,16384]{1,0:T(8,128)(2,1)} async-done(((bf16[128,16384]{1,0:T(8,128)(2,1)}), bf16[64,16384]{1,0:T(8,128)(2,1)}) %reduce-scatter.56.cloned.1.call-update) | async-done | bytes 2097168
  1794.5 19.0 fusion.133
  1821.3 29.5 %bitcast_reduce_fusion = (bf16[4,64,128]{2,1,0:T(8,128)(2,1)S(1)}, bf16[4,64,128]{2,1,0:T(8,128)(2,1)S(1)}, f32[4,64,128,128]{3,2,1,0:T(8,128)}, bf16[4,64,128,128]{2,3,1,0:T(8,128)(2,1)}) fusion(f32[128]{0:T(128)S(1)} %copy-done.85, f32[4,64,128]{2,1,0:T(8,128)S(1)} %copy-done.21, f32[4,64,128]{2,1,0:T(8,128)S(1)} %copy-done.23, ...), kind=kOutput, calls=%fused_computation.31 | convolution fusion | flops 2197749760 | bytes 84345344 | tf_op jit(solution)/shard_map/dgbihj,dgch->bicj/dot_general | solution.py:381
  1922.0 21.2 fusion.159
  1956.9 61.7 %reduce-scatter.48.cloned.1.call-done = bf16[4,64,32,128]{3,2,1,0:T(8,128)(2,1)} async-done(((bf16[4,64,128,128]{3,2,1,0:T(8,128)(2,1)}), bf16[4,64,32,128]{3,2,1,0:T(8,128)(2,1)}) %reduce-scatter.48.cloned.1.call-update) | async-done | bytes 2097168 | tf_op jit(solution)/shard_map/reduce_scatter | solution.py:404
  2026.1 139.9 %reduce-scatter.38.cloned.1.call-done = bf16[4,64,32,128]{3,2,1,0:T(8,128)(2,1)} async-done(((bf16[4,64,128,128]{3,2,1,0:T(8,128)(2,1)}), bf16[4,64,32,128]{3,2,1,0:T(8,128)(2,1)}) %reduce-scatter.38.cloned.1.call-update) | async-done | bytes 2097168 | tf_op jit(solution)/shard_map/reduce_scatter | solution.py:210
  2170.8 60.7 %all-reduce.9.cloned.1.call-done = (f32[2,4,128,32]{2,3,1,0:T(8,128)}, f32[128,128]{1,0:T(8,128)}, f32[128,128]{1,0:T(8,128)}, f32[3,256,64]{1,2,0:T(8,128)}, f3...) async-done(((f32[2,4,128,32]{2,3,1,0:T(8,128)}, f32[128,128]{1,0:T(8,128)}, f32[128,128]{1,0:T(8,128)}, f32[3,256,64]{1,2,0:T(8,128)}, f32[256,64]{0,1:T(8,128)}, ...) | async-done | bytes 1048592 | tf_op jit(solution)/shard_map/psum | solution.py:423
  2231.5 56.5 %all-reduce.7.cloned.1.call-done = (f32[32]{0:T(128)}, f32[2,128,32]{1,2,0:T(8,128)}, f32[2,32]{1,0:T(2,128)}, f32[2,128,32]{1,2,0:T(8,128)}, f32[32]{0:T(128)},...) async-done(((f32[32]{0:T(128)}, f32[2,128,32]{1,2,0:T(8,128)}, f32[2,32]{1,0:T(2,128)}, f32[2,128,32]{1,2,0:T(8,128)}, f32[32]{0:T(128)}, /*index=5*/f32[128,2]{0,1:T(2,128)}, ...) | async-done | bytes 67600 | tf_op jit(solution)/shard_map/psum | solution.py:423
  (485 shorter events, 488.3 us)
Async XLA Ops:
  7.2 790.1 %copy-start = (bf16[256,256]{1,0:T(8,128)(2,1)S(1)}, bf16[256,256]{1,0:T(8,128)(2,1)}, u32[]{:S(2)}) copy-start(bf16[256,256]{1,0:T(8,128)(2,1)} %param.40) | copy-start | bytes 393220
  7.2 150.3 %all-gather.11.cloned.1.call-start = ((), (), s32[]{:S(2)}) async-start(), calls=%async_computation.17 | async-start | bytes 10485760 | tf_op jit(solution)/shard_map/all_gather | solution.py:109
  7.9 295.0 %all-gather.17.cloned.1.call-start = ((), (), s32[]{:S(2)}) async-start(), calls=%async_computation.20 | async-start | bytes 6291456 | tf_op jit(solution)/shard_map/all_gather | solution.py:134
  8.9 187.0 %copy-start.24 = (f32[4,64,128]{2,1,0:T(8,128)}, f32[4,64,128]{2,1,0:T(8,128)S(1)}, u32[]{:S(2)}) copy-start(f32[4,64,128]{2,1,0:T(8,128)S(1)} %broadcast_multiply_fusion) | copy-start | bytes 393220
  211.5 139.5 %all-gather.13.cloned.1.call-start = ((), (), s32[]{:S(2)}) async-start(), calls=%async_computation.18 | async-start | bytes 6291456 | tf_op jit(solution)/shard_map/all_gather | solution.py:133
  212.2 286.8 %all-gather.19.cloned.1.call-start = ((), (), s32[]{:S(2)}) async-start(), calls=%async_computation.21 | async-start | bytes 10485760 | tf_op jit(solution)/shard_map/all_gather | solution.py:162
  309.6 339.3 %all-gather.15.cloned.1.call-start = ((), (), s32[]{:S(2)}) async-start(), calls=%async_computation.19 | async-start | bytes 10485760 | tf_op jit(solution)/shard_map/all_gather | solution.py:159
  357.5 500.1 %all-gather.21.cloned.1.call-start = ((), (), s32[]{:S(2)}) async-start(), calls=%async_computation.22 | async-start | bytes 10485760 | tf_op jit(solution)/shard_map/all_gather | solution.py:184
  358.2 302.4 %copy-start.92 = (f32[128]{0:T(128)}, f32[128]{0:T(128)S(1)}, u32[]{:S(2)}) copy-start(f32[128]{0:T(128)S(1)} %get-tuple-element.117) | copy-start | bytes 1540
  358.2 302.4 %copy-start.94 = (f32[128]{0:T(128)}, f32[128]{0:T(128)S(1)}, u32[]{:S(2)}) copy-start(f32[128]{0:T(128)S(1)} %get-tuple-element.118) | copy-start | bytes 1540
  695.4 311.1 %all-gather.23.cloned.1.call-start = ((), (), s32[]{:S(2)}) async-start(), calls=%async_computation.24 | async-start | bytes 10485760 | tf_op jit(solution)/shard_map/all_gather | solution.py:220
  696.2 358.8 %reduce-scatter.60.cloned.1.call-start = ((), (), s32[]{:S(2)}) async-start(), calls=%async_computation.36 | async-start | bytes 163840
  801.8 259.3 %reduce-scatter.42.cloned.1.call-start = ((), (), s32[]{:S(2)}) async-start(), calls=%async_computation.26 | async-start | bytes 655360 | tf_op jit(solution)/shard_map/reduce_scatter | solution.py:255
  868.3 340.6 %copy-start.40 = (f32[4,64,128]{2,1,0:T(8,128)}, f32[4,64,128]{2,1,0:T(8,128)S(1)}, u32[]{:S(2)}) copy-start(f32[4,64,128]{2,1,0:T(8,128)S(1)} %add_rsqrt_fusion) | copy-start | bytes 393220
  1040.8 168.1 %reduce-scatter.40.cloned.1.call-start = ((), (), s32[]{:S(2)}) async-start(), calls=%async_computation.25 | async-start | bytes 10485760 | tf_op jit(solution)/shard_map/reduce_scatter | solution.py:252
  1041.4 320.0 %reduce-scatter.62.cloned.1.call-start = ((), (), s32[]{:S(2)}) async-start(), calls=%async_computation.37 | async-start | bytes 163840
  1058.0 309.5 %reduce-scatter.46.cloned.1.call-start = ((), (), s32[]{:S(2)}) async-start(), calls=%async_computation.28 | async-start | bytes 655360 | tf_op jit(solution)/shard_map/reduce_scatter | solution.py:303
  1295.0 186.4 %reduce-scatter.58.cloned.1.call-start = ((), (), s32[]{:S(2)}) async-start(), calls=%async_computation.35 | async-start | bytes 10485760
  1336.0 167.1 %reduce-scatter.44.cloned.1.call-start = ((), (), s32[]{:S(2)}) async-start(), calls=%async_computation.27 | async-start | bytes 655360 | tf_op jit(solution)/shard_map/reduce_scatter | solution.py:297
  1337.0 313.9 %reduce-scatter.54.cloned.1.call-start = ((), (), s32[]{:S(2)}) async-start(), calls=%async_computation.33 | async-start | bytes 10485760
  1360.7 328.7 %reduce-scatter.66.cloned.1.call-start = ((), (), s32[]{:S(2)}) async-start(), calls=%async_computation.39 | async-start | bytes 98304
  1365.7 324.9 %reduce-scatter.64.cloned.1.call-start = ((), (), s32[]{:S(2)}) async-start(), calls=%async_computation.38 | async-start | bytes 98304
  1367.2 368.6 %all-gather.25.cloned.1.call-start = ((), (), s32[]{:S(2)}) async-start(), calls=%async_computation.29 | async-start | bytes 6291456 | tf_op jit(solution)/shard_map/all_gather | solution.py:356
  1488.8 303.5 %reduce-scatter.56.cloned.1.call-start = ((), (), s32[]{:S(2)}) async-start(), calls=%async_computation.34 | async-start | bytes 6291456
  1677.8 186.6 %reduce-scatter.52.cloned.1.call-start = ((), (), s32[]{:S(2)}) async-start(), calls=%async_computation.32 | async-start | bytes 163840
  1679.2 203.9 %reduce-scatter.68.cloned.1.call-start = ((), (), s32[]{:S(2)}) async-start(), calls=%async_computation.40 | async-start | bytes 163840
  1693.2 262.7 %reduce-scatter.50.cloned.1.call-start = ((), (), s32[]{:S(2)}) async-start(), calls=%async_computation.31 | async-start | bytes 655360 | tf_op jit(solution)/shard_map/reduce_scatter | solution.py:407
  1851.7 166.8 %reduce-scatter.48.cloned.1.call-start = ((), (), s32[]{:S(2)}) async-start(), calls=%async_computation.30 | async-start | bytes 10485760 | tf_op jit(solution)/shard_map/reduce_scatter | solution.py:404
  1852.4 313.5 %reduce-scatter.38.cloned.1.call-start = ((), (), s32[]{:S(2)}) async-start(), calls=%async_computation.23 | async-start | bytes 10485760 | tf_op jit(solution)/shard_map/reduce_scatter | solution.py:210
  1861.5 370.0 %all-reduce.9.cloned.1.call-start = ((), (), s32[]{:S(2)}) async-start(), calls=%async_computation.42 | async-start | bytes 2097152 | tf_op jit(solution)/shard_map/psum | solution.py:423
  1955.5 332.4 %all-reduce.7.cloned.1.call-start = ((), (), s32[]{:S(2)}) async-start(), calls=%async_computation.41 | async-start | bytes 139264 | tf_op jit(solution)/shard_map/psum | solution.py:423
  2018.5 290.1 %copy-start.1 = (bf16[256,256]{1,0:T(8,128)(2,1)S(1)}, bf16[256,256]{1,0:T(8,128)(2,1)}, u32[]{:S(2)}) copy-start(bf16[256,256]{1,0:T(8,128)(2,1)} %param.40) | copy-start | bytes 393220
  (111 other events, 3481.7 us)
Sparse Core Ops, SparseCore 0:
  9.6 147.8 all-gather.10
  211.6 80.3 all-gather.16
  294.1 56.7 all-gather.12
  352.3 146.6 all-gather.18
  501.0 147.8 all-gather.14
  695.5 162.0 all-gather.20
  859.2 147.3 all-gather.22
  1008.8 17.4 reduce-scatter.59
  1041.0 20.0 reduce-scatter.41
  1063.4 145.4 reduce-scatter.39
  1211.8 17.3 reduce-scatter.61
  1295.1 19.5 reduce-scatter.45
  1336.1 145.1 reduce-scatter.57
  1483.5 19.5 reduce-scatter.43
  1505.3 145.4 reduce-scatter.53
  1653.5 10.9 reduce-scatter.65
  1667.0 9.8 reduce-scatter.63
  1678.9 56.7 all-gather.24
  1738.0 54.2 reduce-scatter.55
  1795.1 16.3 reduce-scatter.51
  1813.7 17.3 reduce-scatter.67
  1851.8 18.5 reduce-scatter.49
  1872.9 145.5 reduce-scatter.47
  2020.8 145.0 reduce-scatter.37
  2172.1 59.3 all-reduce.8
  2237.5 50.4 all-reduce.6
where the time goes:
time: 2330 us; the launch traced here: 2320 us
  waiting for transfers between devices  1430 us (61%)
  matrix products  309 us (13%)
  local copies, waits for them, and re-layouts  200 us (9%)
  other arithmetic  188 us (8%)
  blocking collectives  166 us (7%)
    unnamed x35, waiting for transfers between devices  309 us
    all_gather x1, waiting for transfers between devices, shards(): lax.all_gather(pair, 'chan', axis=2, tiled=True)  149 us
    reduce_scatter x1, waiting for transfers between devices, shards(): lax.psum_scatter(grad_normed_mid.astype(jnp.bfloat16), 'chan', scatter_di...  147 us
    all_gather x1, waiting for transfers between devices, shards(): lax.all_gather(tri_out.astype(jnp.bfloat16), 'chan', axis=2, tiled=True)  142 us
    reduce_scatter x1, waiting for transfers between devices, shards(): lax.psum_scatter(out_terms.astype(jnp.bfloat16), 'chan', scatter_dimensio...  140 us
    all_gather x1, waiting for transfers between devices, shards(): lax.all_gather(tri_in.astype(jnp.bfloat16), 'chan', axis=2, tiled=True)  130 us
    unnamed x286, local copies, waits for them, and re-layouts  120 us
    psum x2, waiting for transfers between devices, shards(): lax.psum((grad_gain_pair, grad_tri_in_w, grad_out_gate, grad_gain_tri, gr...  117 us
  transfers between devices with their start and end apart: 26, of which 17 were waited for; matrix products, arithmetic and copies ran while one was open for 24% of the time, Pallas kernels for 0%

commit v1 on v0

--- a/solution.py
+++ b/solution.py
@@ -1,11 +1,16 @@
+import functools
 import math
 
 import jax
 import jax.numpy as jnp
 from jax import lax
+from jax.experimental import pallas as pl
+from jax.experimental.pallas import tpu as pltpu
 from jax.sharding import PartitionSpec as P
 
+f32, bf16 = jnp.float32, jnp.bfloat16
 epsilon = 1e-05
+DP, ROWS, CHAN = "dp", "rows", "chan"
 masked_score = -1000000000.0
 
 
@@ -88,9 +93,9 @@
     batch = pair.shape[0]
     rows_here = pair.shape[1]
     crop_len = pair.shape[3]
-    groups = lax.axis_size("chan")
-    chan_index = lax.axis_index("chan")
-    row_start = lax.axis_index("rows") * rows_here
+    groups = lax.axis_size(CHAN)
+    chan_index = lax.axis_index(CHAN)
+    row_start = lax.axis_index(ROWS) * rows_here
     heads_here = w_bias.shape[1]
     head_dim = w_qkv.shape[2] // heads_here
     scale = 1.0 / math.sqrt(head_dim)
@@ -106,8 +111,8 @@
         return jax.nn.sigmoid(gate) * value * pair_mask
 
     pair_whole, node_whole = (
-        lax.all_gather(pair, "chan", axis=2, tiled=True),
-        lax.all_gather(node, "chan", axis=2, tiled=True),
+        lax.all_gather(pair, CHAN, axis=2, tiled=True),
+        lax.all_gather(node, CHAN, axis=2, tiled=True),
     )
     full_in = pair_whole.astype(jnp.float32)
     node_full = node_whole.astype(jnp.float32)
@@ -130,12 +135,12 @@
         "bin,gna->gbia", normed_node, w_qkv, preferred_element_type=jnp.float32
     ).astype(jnp.bfloat16)
     whole_right_out, whole_right_in, whole_keys, whole_values = (
-        lax.all_gather(right_out, "rows", axis=1, tiled=True),
-        lax.all_gather(right_in, "rows", axis=1, tiled=True),
-        lax.all_gather(qkv[1], "rows", axis=1, tiled=True),
-        lax.all_gather(qkv[2], "rows", axis=1, tiled=True),
-    )
-    left_cols = lax.all_to_all(left_in, "rows", split_axis=3, concat_axis=1, tiled=True)
+        lax.all_gather(right_out, ROWS, axis=1, tiled=True),
+        lax.all_gather(right_in, ROWS, axis=1, tiled=True),
+        lax.all_gather(qkv[1], ROWS, axis=1, tiled=True),
+        lax.all_gather(qkv[2], ROWS, axis=1, tiled=True),
+    )
+    left_cols = lax.all_to_all(left_in, ROWS, split_axis=3, concat_axis=1, tiled=True)
     queries = qkv[0].reshape(batch, rows_here, heads_here, head_dim)
     keys = whole_keys.reshape(batch, crop_len, heads_here, head_dim)
     values = whole_values.reshape(batch, crop_len, heads_here, head_dim)
@@ -156,14 +161,14 @@
         "bkhi,bkhj->bihj", left_cols, whole_right_in, preferred_element_type=jnp.float32
     )
     tri_full_out, tri_full_in, attn_whole = (
-        lax.all_gather(tri_out.astype(jnp.bfloat16), "chan", axis=2, tiled=True).astype(
+        lax.all_gather(tri_out.astype(jnp.bfloat16), CHAN, axis=2, tiled=True).astype(
             tri_out.dtype
         ),
-        lax.all_gather(tri_in.astype(jnp.bfloat16), "chan", axis=2, tiled=True).astype(
+        lax.all_gather(tri_in.astype(jnp.bfloat16), CHAN, axis=2, tiled=True).astype(
             tri_in.dtype
         ),
         lax.all_gather(
-            attn.astype(jnp.float32).astype(jnp.bfloat16), "chan", axis=2, tiled=True
+            attn.astype(jnp.float32).astype(jnp.bfloat16), CHAN, axis=2, tiled=True
         ).astype(jnp.float32),
     )
     normed_out = normed(tri_full_out, gain_tri[0]).astype(jnp.bfloat16)
@@ -181,10 +186,10 @@
         "bia,an->bin", attn_low, w_attn_out, preferred_element_type=jnp.float32
     )
     full_mid, node_full_mid = (
-        lax.all_gather(stream_mid.astype(jnp.bfloat16), "chan", axis=2, tiled=True).astype(
+        lax.all_gather(stream_mid.astype(jnp.bfloat16), CHAN, axis=2, tiled=True).astype(
             stream_mid.dtype
         ),
-        lax.all_gather(node_mid.astype(jnp.bfloat16), "chan", axis=2, tiled=True).astype(
+        lax.all_gather(node_mid.astype(jnp.bfloat16), CHAN, axis=2, tiled=True).astype(
             node_mid.dtype
         ),
     )
@@ -208,17 +213,17 @@
     )
     pair_sum, node_sum = (
         lax.psum_scatter(
-            out_terms.astype(jnp.bfloat16), "chan", scatter_dimension=2, tiled=True
-        ).astype(jnp.float32),
-        lax.psum_scatter(
-            node_terms.astype(jnp.bfloat16), "chan", scatter_dimension=2, tiled=True
+            out_terms.astype(jnp.bfloat16), CHAN, scatter_dimension=2, tiled=True
+        ).astype(jnp.float32),
+        lax.psum_scatter(
+            node_terms.astype(jnp.bfloat16), CHAN, scatter_dimension=2, tiled=True
         ).astype(jnp.float32),
     )
     stream_out = stream_mid + pair_sum
     node_out = node_mid + node_sum
     cot_full, node_cot_full = (
-        lax.all_gather(pair_cot, "chan", axis=2, tiled=True),
-        lax.all_gather(node_cot, "chan", axis=2, tiled=True),
+        lax.all_gather(pair_cot, CHAN, axis=2, tiled=True),
+        lax.all_gather(node_cot, CHAN, axis=2, tiled=True),
     )
     grad_trans_out = jnp.einsum(
         "bifj,bicj->fc", hidden_low, cot_full, preferred_element_type=jnp.float32
@@ -250,16 +255,16 @@
     node_mid_terms = stat_terms(node_full_mid, gain_node_trans, grad_normed_node_mid, groups)
     mid_here, mid_totals, node_mid_here, node_mid_totals = (
         lax.psum_scatter(
-            grad_normed_mid.astype(jnp.bfloat16), "chan", scatter_dimension=2, tiled=True
-        ).astype(jnp.float32),
-        lax.psum_scatter(
-            mid_terms.astype(jnp.bfloat16), "chan", scatter_dimension=2, tiled=True
-        ).astype(jnp.float32),
-        lax.psum_scatter(
-            grad_normed_node_mid.astype(jnp.bfloat16), "chan", scatter_dimension=2, tiled=True
-        ).astype(jnp.float32),
-        lax.psum_scatter(
-            node_mid_terms.astype(jnp.bfloat16), "chan", scatter_dimension=2, tiled=True
+            grad_normed_mid.astype(jnp.bfloat16), CHAN, scatter_dimension=2, tiled=True
+        ).astype(jnp.float32),
+        lax.psum_scatter(
+            mid_terms.astype(jnp.bfloat16), CHAN, scatter_dimension=2, tiled=True
+        ).astype(jnp.float32),
+        lax.psum_scatter(
+            grad_normed_node_mid.astype(jnp.bfloat16), CHAN, scatter_dimension=2, tiled=True
+        ).astype(jnp.float32),
+        lax.psum_scatter(
+            node_mid_terms.astype(jnp.bfloat16), CHAN, scatter_dimension=2, tiled=True
         ).astype(jnp.float32),
     )
     mid_extra, grad_gain_trans = norm_finish(full_mid, gain_trans, mid_here, mid_totals, chan_index)
@@ -292,19 +297,19 @@
     )
     out_here, out_totals, inc_here, inc_totals, attn_here = (
         lax.psum_scatter(
-            grad_tri_normed[0].astype(jnp.bfloat16), "chan", scatter_dimension=2, tiled=True
-        ).astype(jnp.float32),
-        lax.psum_scatter(
-            out_stats.astype(jnp.bfloat16), "chan", scatter_dimension=2, tiled=True
-        ).astype(jnp.float32),
-        lax.psum_scatter(
-            grad_tri_normed[1].astype(jnp.bfloat16), "chan", scatter_dimension=2, tiled=True
-        ).astype(jnp.float32),
-        lax.psum_scatter(
-            inc_stats.astype(jnp.bfloat16), "chan", scatter_dimension=2, tiled=True
-        ).astype(jnp.float32),
-        lax.psum_scatter(
-            attn_terms.astype(jnp.bfloat16), "chan", scatter_dimension=2, tiled=True
+            grad_tri_normed[0].astype(jnp.bfloat16), CHAN, scatter_dimension=2, tiled=True
+        ).astype(jnp.float32),
+        lax.psum_scatter(
+            out_stats.astype(jnp.bfloat16), CHAN, scatter_dimension=2, tiled=True
+        ).astype(jnp.float32),
+        lax.psum_scatter(
+            grad_tri_normed[1].astype(jnp.bfloat16), CHAN, scatter_dimension=2, tiled=True
+        ).astype(jnp.float32),
+        lax.psum_scatter(
+            inc_stats.astype(jnp.bfloat16), CHAN, scatter_dimension=2, tiled=True
+        ).astype(jnp.float32),
+        lax.psum_scatter(
+            attn_terms.astype(jnp.bfloat16), CHAN, scatter_dimension=2, tiled=True
         ).astype(jnp.float32),
     )
     grad_tri_a, gain_grad_out = norm_finish(
@@ -344,16 +349,16 @@
     )
     grad_right_out, key_grads, value_grads = (
         lax.psum_scatter(
-            right_terms.astype(jnp.bfloat16), "rows", scatter_dimension=1, tiled=True
-        ).astype(jnp.float32),
-        lax.psum_scatter(
-            key_terms.astype(jnp.bfloat16), "rows", scatter_dimension=1, tiled=True
-        ).astype(jnp.float32),
-        lax.psum_scatter(
-            value_terms.astype(jnp.bfloat16), "rows", scatter_dimension=1, tiled=True
-        ).astype(jnp.float32),
-    )
-    whole_grad_in = lax.all_gather(grad_inc_low, "rows", axis=1, tiled=True)
+            right_terms.astype(jnp.bfloat16), ROWS, scatter_dimension=1, tiled=True
+        ).astype(jnp.float32),
+        lax.psum_scatter(
+            key_terms.astype(jnp.bfloat16), ROWS, scatter_dimension=1, tiled=True
+        ).astype(jnp.float32),
+        lax.psum_scatter(
+            value_terms.astype(jnp.bfloat16), ROWS, scatter_dimension=1, tiled=True
+        ).astype(jnp.float32),
+    )
+    whole_grad_in = lax.all_gather(grad_inc_low, ROWS, axis=1, tiled=True)
     grad_left_in = jnp.einsum(
         "bihj,bkhj->bkhi", whole_grad_in, right_in, preferred_element_type=jnp.float32
     )
@@ -402,16 +407,16 @@
     node_in_terms = stat_terms(node_full, gain_node, grad_normed_node, groups)
     in_here, in_totals, node_in_here, node_in_totals = (
         lax.psum_scatter(
-            grad_normed_in.astype(jnp.bfloat16), "chan", scatter_dimension=2, tiled=True
-        ).astype(jnp.float32),
-        lax.psum_scatter(
-            in_terms.astype(jnp.bfloat16), "chan", scatter_dimension=2, tiled=True
-        ).astype(jnp.float32),
-        lax.psum_scatter(
-            grad_normed_node.astype(jnp.bfloat16), "chan", scatter_dimension=2, tiled=True
-        ).astype(jnp.float32),
-        lax.psum_scatter(
-            node_in_terms.astype(jnp.bfloat16), "chan", scatter_dimension=2, tiled=True
+            grad_normed_in.astype(jnp.bfloat16), CHAN, scatter_dimension=2, tiled=True
+        ).astype(jnp.float32),
+        lax.psum_scatter(
+            in_terms.astype(jnp.bfloat16), CHAN, scatter_dimension=2, tiled=True
+        ).astype(jnp.float32),
+        lax.psum_scatter(
+            grad_normed_node.astype(jnp.bfloat16), CHAN, scatter_dimension=2, tiled=True
+        ).astype(jnp.float32),
+        lax.psum_scatter(
+            node_in_terms.astype(jnp.bfloat16), CHAN, scatter_dimension=2, tiled=True
         ).astype(jnp.float32),
     )
     in_extra, grad_gain_pair = norm_finish(full_in, gain_pair, in_here, in_totals, chan_index)
@@ -438,7 +443,7 @@
             grad_node_in_w,
             grad_node_out_w,
         ),
-        ("dp", "rows"),
+        (DP, ROWS),
     )
     return (
         stream_out.astype(jnp.bfloat16),
@@ -463,49 +468,751 @@
     )
 
 
+def dot(a, b, ca=1, cb=0):
+    return lax.dot_general(a, b, (((ca,), (cb,)), ((), ())), preferred_element_type=f32)
+
+def sigmoid(v):
+    return 0.5 * jnp.tanh(0.5 * v) + 0.5
+
+def sub_norm(full):
+    mean = jnp.mean(full, axis=0, keepdims=True)
+    centered = full - mean
+    inverse = lax.rsqrt(jnp.mean(centered * centered, axis=0, keepdims=True) + epsilon)
+    return centered * inverse, inverse
+
+def project_kernel(zc_ref, p0, p1, p2, p3, mask_ref, gain_ref, w_ref, wb_ref,
+                   lo_ref, ro_ref, li_ref, ri_ref, norm_ref, pair_ref, bias_ref, xs, *scratch):
+    pieces = (p0, p1, p2, p3)
+    outs = (lo_ref, ro_ref, li_ref, ri_ref)
+    rows, quarter, width = p0.shape
+    chans = 4 * quarter
+    z = zc_ref[0]
+    gain = gain_ref[...]
+
+    @pl.loop(0, rows // 2)
+    def _(step):
+        for half in range(2):
+            row = 2 * step + half
+            for m in range(4):
+                at = pl.multiple_of(lax.bitwise_xor(z, m) * quarter, quarter)
+                piece = pieces[m][row]
+                pair_ref[row, pl.ds(at, quarter), :] = piece
+                xs[pl.ds(at, quarter), half * width:(half + 1) * width] = piece.astype(f32)
+        scaled, _ = sub_norm(xs[...])
+        low = (scaled * gain).astype(bf16)
+        for half in range(2):
+            norm_ref[2 * step + half] = low[:, half * width:(half + 1) * width]
+        mask = jnp.concatenate([mask_ref[pl.ds(2 * step + half, 1), :] for half in range(2)], axis=1)
+        b = dot(wb_ref[...], low)
+        for half in range(2):
+            bias_ref[2 * step + half] = b[:, half * width:(half + 1) * width]
+        for block in range(4):
+            proj = dot(w_ref[block], low)
+            for k in range(4):
+                gate = proj[(2 * k) * quarter:(2 * k + 1) * quarter]
+                value = proj[(2 * k + 1) * quarter:(2 * k + 2) * quarter]
+                kept = sigmoid(gate) * value * mask
+                for half in range(2):
+                    at = pl.multiple_of((2 * step + half) * chans + block * quarter, quarter)
+                    scratch[k][pl.ds(at, quarter), :] = kept[:, half * width:(half + 1) * width]
+
+    @pl.loop(0, chans, unroll=8)
+    def _(h):
+        for k in range(4):
+            outs[k][h] = scratch[k][pl.ds(h, rows, stride=chans), :].astype(bf16)
+
+def project(zc, pieces, mask_rows, gain, w, wb, step_rows=16):
+    rows, quarter, width = pieces[0].shape
+    chans = 4 * quarter
+    heads = wb.shape[0]
+    grid = (rows // step_rows,)
+    tri = jax.ShapeDtypeStruct((chans, rows, width), bf16)
+    tri_spec = pl.BlockSpec((chans, step_rows, width), lambda i: (0, i, 0))
+    row_spec = pl.BlockSpec((step_rows, chans, width), lambda i: (i, 0, 0))
+    pair = jax.ShapeDtypeStruct((rows, chans, width), bf16)
+    return pl.pallas_call(
+        project_kernel,
+        grid=grid,
+        in_specs=[pl.BlockSpec(memory_space=pltpu.SMEM)]
+        + [pl.BlockSpec((step_rows, quarter, width), lambda i: (i, 0, 0))] * 4
+        + [pl.BlockSpec((step_rows, width), lambda i: (i, 0)),
+           pl.BlockSpec(gain.shape, lambda i: (0, 0)),
+           pl.BlockSpec(w.shape, lambda i: (0, 0, 0)),
+           pl.BlockSpec(wb.shape, lambda i: (0, 0))],
+        out_specs=[tri_spec] * 4 + [row_spec, row_spec,
+                                    pl.BlockSpec((step_rows, heads, width), lambda i: (i, 0, 0))],
+        out_shape=[tri] * 4 + [pair, pair, jax.ShapeDtypeStruct((rows, heads, width), f32)],
+        scratch_shapes=[pltpu.VMEM((chans, 2 * width), f32)]
+        + [pltpu.VMEM((step_rows * chans, width), f32)] * 4,
+        compiler_params=pltpu.CompilerParams(vmem_limit_bytes=48 * 2**20),
+        cost_estimate=pl.CostEstimate(flops=2 * rows * width * chans * 8 * chans, bytes_accessed=20 * 2**20, transcendentals=rows * width * chans * 4),
+        name="project",
+    )(zc, *pieces, mask_rows, gain, w, wb)
+
+def gelu_both(value):
+    cdf = 0.5 * (1.0 + lax.erf(value * (0.5 ** 0.5)))
+    density = jnp.exp(-0.5 * value * value) * (1.0 / math.sqrt(2.0 * math.pi))
+    return value * cdf, cdf + value * density
+
+def norm_back(gain, scaled, inverse, grad):
+    weighted = gain * grad
+    first = jnp.mean(weighted, axis=0, keepdims=True)
+    second = jnp.mean(weighted * scaled, axis=0, keepdims=True)
+    return inverse * (weighted - first - scaled * second)
+
+def middle_kernel(h_steps, place_ref, lo, ro, ro_far, li, li_far, ri, ri_far,
+                  pair_ref, norm_ref, c0, c1, c2, c3,
+                  gain_tri_ref, gain_trans_ref, wg_ref, wto_ref, wti_ref, wout_ref,
+                  p0, p1, p2, p3, mid_ref, gate_ref, go_ref, gi_ref,
+                  gw_in_ref, gw_out_ref, gw_tri_ref, gg_trans_ref, gg_tri_ref,
+                  tri0, tri1, wout_t, wti_t, wto_t, right_s, xs, cot_s, po_s, tn0, tn1, nm, hid, gp, gb0, gb1, gs0, gs1):
+    z, core = place_ref[0], place_ref[1]
+    step = pl.program_id(0)
+    half_rows = lo.shape[1]
+    width = lo.shape[2]
+    chans = wg_ref.shape[1]
+    tris = (tri0, tri1)
+
+    @pl.when(step == 0)
+    def _():
+        for f in range(4):
+            wout_t[:, f * 128:(f + 1) * 128] = wout_ref[f * 128:(f + 1) * 128].astype(f32).T.astype(bf16)
+            wti_t[:, f * 128:(f + 1) * 128] = wti_ref[f * 128:(f + 1) * 128].astype(f32).T.astype(bf16)
+        for d in range(2):
+            wto_t[d] = wto_ref[d].astype(f32).T.astype(bf16)
+        for ref in (gw_in_ref, gw_out_ref, gw_tri_ref, gg_trans_ref, gg_tri_ref):
+            ref[...] = jnp.zeros_like(ref)
+
+    @pl.when(step < h_steps)
+    def _():
+        here = lo.shape[0]
+        first = core == 0
+
+        @pl.loop(0, here, unroll=4)
+        def _(h):
+            at = pl.multiple_of((step * here + h) * half_rows, half_rows)
+            mine, far = ro[h], ro_far[h]
+            right = jnp.concatenate([jnp.where(first, mine, far), jnp.where(first, far, mine)], axis=0)
+            tri0[pl.ds(at, half_rows), :] = dot(lo[h], right, 1, 1)
+            left = jnp.concatenate([li[h], li_far[h]], axis=0)
+            right = jnp.concatenate([ri[h], ri_far[h]], axis=0)
+            both = dot(left, right, 0, 0)
+            tri1[pl.ds(at, half_rows), :] = jnp.where(first, both[:half_rows], both[half_rows:])
+
+    @pl.when(step >= h_steps)
+    def _():
+        rows = pair_ref.shape[0]
+        quarter = chans // 4
+        first_row = (step - h_steps) * rows
+        cots, outs = (c0, c1, c2, c3), (p0, p1, p2, p3)
+        tns, gbs, gss, grads = (tn0, tn1), (gb0, gb1), (gs0, gs1), (go_ref, gi_ref)
+        gain_trans = gain_trans_ref[...]
+
+        @pl.loop(0, rows // 2)
+        def _(s2):
+            lanes = pl.ds(pl.multiple_of(s2 * 2 * width, 2 * width), 2 * width)
+
+            def wide(get):
+                return jnp.concatenate([get(2 * s2), get(2 * s2 + 1)], axis=1)
+
+            inner = wide(lambda r: norm_ref[r])
+            gate = sigmoid(dot(wg_ref[...].reshape(2 * chans, chans), inner))
+            total = wide(lambda r: pair_ref[r]).astype(f32)
+            kept = []
+            for d in range(2):
+                tri = wide(lambda r: tris[d][pl.ds(first_row + r, chans, stride=half_rows), :])
+                scaled, inverse = sub_norm(tri)
+                low = (scaled * gain_tri_ref[d]).astype(bf16)
+                tns[d][:, lanes] = low
+                branch = dot(wto_ref[d], low)
+                total = total + gate[d * chans:(d + 1) * chans] * branch
+                kept.append((scaled, inverse, branch))
+            scaled, inverse = sub_norm(total)
+            low = (scaled * gain_trans).astype(bf16)
+            nm[:, lanes] = low
+            for half in range(2):
+                for m in range(4):
+                    at = pl.multiple_of(lax.bitwise_xor(z, m) * quarter, quarter)
+                    cot_s[pl.ds(at, quarter), pl.ds(pl.multiple_of((2 * s2 + half) * width, width), width)] = cots[m][2 * s2 + half]
+            cot = cot_s[:, lanes]
+            for f in range(4):
+                block = slice(f * 128, (f + 1) * 128)
+                act, slope = gelu_both(dot(wti_ref[block], low))
+                hid[block, lanes] = act.astype(bf16)
+                gp[block, lanes] = (dot(wout_ref[block], cot) * slope).astype(bf16)
+            po_s[...] = (total + dot(wout_t[...], hid[:, lanes])).astype(bf16)
+            for half in range(2):
+                for m in range(4):
+                    at = pl.multiple_of(lax.bitwise_xor(z, m) * quarter, quarter)
+                    outs[m][2 * s2 + half] = po_s[pl.ds(at, quarter), half * width:(half + 1) * width]
+            back = dot(wti_t[...], gp[:, lanes])
+            gg_trans_ref[...] += back * scaled
+            grad = cot.astype(f32) + norm_back(gain_trans, scaled, inverse, back)
+            for half in range(2):
+                mid_ref[2 * s2 + half] = grad[:, half * width:(half + 1) * width]
+            for d in range(2):
+                scaled, inverse, branch = kept[d]
+                sig = gate[d * chans:(d + 1) * chans]
+                grad_branch = sig * grad
+                grad_gate = (grad_branch * branch * (1.0 - sig)).astype(bf16)
+                grad_branch = grad_branch.astype(bf16)
+                for half in range(2):
+                    gate_ref[2 * s2 + half, d * chans:(d + 1) * chans] = grad_gate[:, half * width:(half + 1) * width]
+                gbs[d][:, lanes] = grad_branch
+                back = dot(wto_t[d], grad_branch)
+                gg_tri_ref[d] += back * scaled
+                out = norm_back(gain_tri_ref[d], scaled, inverse, back)
+                for half in range(2):
+                    gss[d][pl.ds(2 * s2 + half, chans, stride=rows), :] = out[:, half * width:(half + 1) * width]
+
+        gw_out_ref[...] += dot(hid[...], cot_s[...], 1, 1)
+        gw_in_ref[...] += dot(gp[...], nm[...], 1, 1)
+        for d in range(2):
+            gw_tri_ref[d] += dot(gbs[d][...], tns[d][...], 1, 1)
+
+            @pl.loop(0, chans, unroll=8)
+            def _(h):
+                grads[d][h] = gss[d][pl.ds(pl.multiple_of(h * rows, rows), rows), :].astype(bf16)
+
+def middle(place, tri_in, pair, norm, cots, gain_tri, gain_trans, wg, wto, wti, wout, step_rows=16, step_h=16):
+    chans, rows, width = tri_in[0].shape
+    hidden = wti.shape[0]
+    quarter = chans // 4
+    h_steps, i_steps = chans // step_h, rows // step_rows
+    h_spec = pl.BlockSpec((step_h, rows, width), lambda s: (jnp.minimum(s, h_steps - 1), 0, 0))
+
+    def at(s):
+        return jnp.maximum(s - h_steps, 0)
+
+    def whole(a):
+        zeros = (0,) * len(a.shape)
+        return pl.BlockSpec(a.shape, lambda s: zeros)
+
+    row_spec = pl.BlockSpec((step_rows, chans, width), lambda s: (at(s), 0, 0))
+    piece_spec = pl.BlockSpec((step_rows, quarter, width), lambda s: (at(s), 0, 0))
+    tri_spec = pl.BlockSpec((chans, step_rows, width), lambda s: (0, at(s), 0))
+    piece = jax.ShapeDtypeStruct((rows, quarter, width), bf16)
+    tri = jax.ShapeDtypeStruct((chans, rows, width), bf16)
+    sums = [jax.ShapeDtypeStruct(s, f32) for s in ((hidden, chans), (hidden, chans), (2, chans, chans), (chans, 2 * width), (2, chans, 2 * width))]
+    lanes = step_rows * width
+    return pl.pallas_call(
+        functools.partial(middle_kernel, h_steps),
+        grid=(h_steps + i_steps,),
+        in_specs=[pl.BlockSpec(memory_space=pltpu.SMEM)] + [h_spec] * 7 + [row_spec, row_spec] + [piece_spec] * 4
+        + [whole(a) for a in (gain_tri, gain_trans, wg, wto, wti, wout)],
+        out_specs=[piece_spec] * 4 + [row_spec, pl.BlockSpec((step_rows, 2 * chans, width), lambda s: (at(s), 0, 0)), tri_spec, tri_spec]
+        + [whole(a) for a in sums],
+        out_shape=[piece] * 4 + [jax.ShapeDtypeStruct((rows, chans, width), f32), jax.ShapeDtypeStruct((rows, 2 * chans, width), bf16), tri, tri] + sums,
+        scratch_shapes=[pltpu.VMEM((chans * rows, width), f32)] * 2
+        + [pltpu.VMEM((chans, hidden), bf16)] * 2 + [pltpu.VMEM((2, chans, chans), bf16), pltpu.VMEM((width, width), bf16),
+           pltpu.VMEM((chans, 2 * width), f32), pltpu.VMEM((chans, lanes), bf16), pltpu.VMEM((chans, 2 * width), bf16)]
+        + [pltpu.VMEM((chans, lanes), bf16)] * 3 + [pltpu.VMEM((hidden, lanes), bf16)] * 2 + [pltpu.VMEM((chans, lanes), bf16)] * 2
+        + [pltpu.VMEM((chans * step_rows, width), f32)] * 2,
+        compiler_params=pltpu.CompilerParams(vmem_limit_bytes=60 * 2**20),
+        cost_estimate=pl.CostEstimate(flops=11 * 10**9, bytes_accessed=40 * 2**20, transcendentals=rows * width * hidden * 2),
+        name="middle",
+    )(place, *tri_in, pair, norm, *cots, gain_tri, gain_trans, wg, wto, wti, wout)
+
+def finish_kernel(h_steps, place_ref, lo, lo_far, ro, ro_far, li, ri, go, go_far, gi, gi_far,
+                  pair_ref, norm_ref, mid_ref, gate_ref, score_ref, mask_ref, gain_ref, w_ref, wall_ref,
+                  p0, p1, p2, p3, gw_ref, gg_ref,
+                  s0, s1, s2_, s3, wall_t, gall, nb, po_s):
+    z, core = place_ref[0], place_ref[1]
+    step = pl.program_id(0)
+    half_rows, width = lo.shape[1:]
+    chans = norm_ref.shape[1]
+    sums = (s0, s1, s2_, s3)
+    packed = wall_ref.shape[0]
+
+    @pl.when(step == 0)
+    def _():
+        for f in range(packed // 128):
+            wall_t[:, f * 128:(f + 1) * 128] = wall_ref[f * 128:(f + 1) * 128].astype(f32).T.astype(bf16)
+        for ref in (gw_ref, gg_ref):
+            ref[...] = jnp.zeros_like(ref)
+
+    @pl.when(step < h_steps)
+    def _():
+        here = lo.shape[0]
+        first = core == 0
+
+        def ordered(mine, far):
+            return jnp.concatenate([jnp.where(first, mine, far), jnp.where(first, far, mine)], axis=0)
+
+        @pl.loop(0, here, unroll=4)
+        def _(h):
+            at = pl.ds(pl.multiple_of((step * here + h) * half_rows, half_rows), half_rows)
+            s0[at, :] = dot(go[h], ordered(ro[h], ro_far[h]))
+            both = dot(jnp.concatenate([go[h], go_far[h]], axis=0), jnp.concatenate([lo[h], lo_far[h]], axis=0), 0, 0)
+            s1[at, :] = jnp.where(first, both[:half_rows], both[half_rows:])
+            inc = ordered(gi[h], gi_far[h])
+            s2_[at, :] = dot(ri[h], inc, 1, 1)
+            s3[at, :] = dot(li[h], inc)
+
+    @pl.when(step >= h_steps)
+    def _():
+        rows = pair_ref.shape[0]
+        quarter = chans // 4
+        first_row = (step - h_steps) * rows
+        outs = (p0, p1, p2, p3)
+        gain = gain_ref[...]
+        heads = score_ref.shape[1]
+        gall[packed - 128:, :] = jnp.zeros((128, gall.shape[1]), bf16)
+
+        @pl.loop(0, rows // 2)
+        def _(s2):
+            lanes = pl.ds(pl.multiple_of(s2 * 2 * width, 2 * width), 2 * width)
+
+            def wide(get):
+                return jnp.concatenate([get(2 * s2), get(2 * s2 + 1)], axis=1)
+
+            inner = wide(lambda r: norm_ref[r])
+            nb[:, lanes] = inner
+            mask = wide(lambda r: mask_ref[pl.ds(r, 1), :])
+            for block in range(4):
+                proj = dot(w_ref[block], inner)
+                for k in range(4):
+                    gate = proj[(2 * k) * quarter:(2 * k + 1) * quarter]
+                    value = proj[(2 * k + 1) * quarter:(2 * k + 2) * quarter]
+                    grad = wide(lambda r: sums[k][pl.ds(block * quarter * half_rows + first_row + r, quarter, stride=half_rows), :])
+                    sig = sigmoid(gate)
+                    back = grad * mask * sig
+                    base = block * 8 * quarter + 2 * k * quarter
+                    gall[base:base + quarter, lanes] = (back * value * (1.0 - sig)).astype(bf16)
+                    gall[base + quarter:base + 2 * quarter, lanes] = back.astype(bf16)
+            gall[8 * chans:10 * chans, lanes] = wide(lambda r: gate_ref[r])
+            gall[10 * chans:10 * chans + 2 * heads, lanes] = jnp.concatenate([wide(lambda r: score_ref[r]), jnp.zeros((heads, 2 * width), f32)], axis=0).astype(bf16)
+            back = dot(wall_t[...], gall[:, lanes])
+            scaled, inverse = sub_norm(wide(lambda r: pair_ref[r]).astype(f32))
+            gg_ref[...] += back * scaled
+            out = wide(lambda r: mid_ref[r]) + norm_back(gain, scaled, inverse, back)
+            po_s[...] = out.astype(bf16)
+            for half in range(2):
+                for m in range(4):
+                    at = pl.multiple_of(lax.bitwise_xor(z, m) * quarter, quarter)
+                    outs[m][2 * s2 + half] = po_s[pl.ds(at, quarter), half * width:(half + 1) * width]
+
+        gw_ref[...] += dot(gall[...], nb[...], 1, 1)
+
+def finish(place, tri_in, pair, norm, mid, gate, scores, mask_rows, gain, w, wall, step_rows=16, step_h=16):
+    chans, rows, width = tri_in[0].shape
+    quarter = chans // 4
+    heads = scores.shape[1]
+    packed = wall.shape[0]
+    h_steps, i_steps = chans // step_h, rows // step_rows
+    h_spec = pl.BlockSpec((step_h, rows, width), lambda s: (jnp.minimum(s, h_steps - 1), 0, 0))
+
+    def at(s):
+        return jnp.maximum(s - h_steps, 0)
+
+    def whole(a):
+        zeros = (0,) * len(a.shape)
+        return pl.BlockSpec(a.shape, lambda s: zeros)
+
+    row_spec = pl.BlockSpec((step_rows, chans, width), lambda s: (at(s), 0, 0))
+    piece_spec = pl.BlockSpec((step_rows, quarter, width), lambda s: (at(s), 0, 0))
+    piece = jax.ShapeDtypeStruct((rows, quarter, width), bf16)
+    sums = [jax.ShapeDtypeStruct(s, f32) for s in ((packed, chans), (chans, 2 * width))]
+    lanes = step_rows * width
+    return pl.pallas_call(
+        functools.partial(finish_kernel, h_steps),
+        grid=(h_steps + i_steps,),
+        in_specs=[pl.BlockSpec(memory_space=pltpu.SMEM)] + [h_spec] * 10 + [row_spec] * 3
+        + [pl.BlockSpec((step_rows, 2 * chans, width), lambda s: (at(s), 0, 0)),
+           pl.BlockSpec((step_rows, heads, width), lambda s: (at(s), 0, 0)),
+           pl.BlockSpec((step_rows, width), lambda s: (at(s), 0))]
+        + [whole(a) for a in (gain, w, wall)],
+        out_specs=[piece_spec] * 4 + [whole(a) for a in sums],
+        out_shape=[piece] * 4 + sums,
+        scratch_shapes=[pltpu.VMEM((chans * rows, width), f32)] * 4
+        + [pltpu.VMEM((chans, packed), bf16), pltpu.VMEM((packed, lanes), bf16), pltpu.VMEM((chans, lanes), bf16), pltpu.VMEM((chans, 2 * width), bf16)],
+        compiler_params=pltpu.CompilerParams(vmem_limit_bytes=60 * 2**20),
+        cost_estimate=pl.CostEstimate(flops=8 * 10**9, bytes_accessed=40 * 2**20, transcendentals=rows * width * chans * 4),
+        name="finish",
+    )(place, *tri_in, pair, norm, mid, gate, scores, mask_rows, gain, w, wall)
+
+
+def shards_by_crop(
+    pair,
+    node,
+    pair_cot,
+    node_cot,
+    lengths,
+    present,
+    gain_pair,
+    w_tri_in,
+    w_out_gate,
+    gain_tri,
+    w_tri_out,
+    gain_trans,
+    w_trans_in,
+    w_trans_out,
+    w_bias,
+    gain_node,
+    w_qkv,
+    w_attn_out,
+    gain_node_trans,
+    w_node_in,
+    w_node_out,
+):
+    groups = lax.axis_size(CHAN)
+    rows_here = pair.shape[1]
+    chans = groups * pair.shape[2]
+    crop_len = pair.shape[3]
+    nodes = groups * node.shape[2]
+    z = lax.axis_index(CHAN)
+    core = lax.axis_index(DP) % 2
+    x = lax.axis_index(ROWS)
+    place = jnp.stack([z, core]).astype(jnp.int32)
+    mesh_shape = (lax.axis_size(DP), lax.axis_size(ROWS), groups)
+
+    def device(d, r, c):
+        return (d * mesh_shape[1] + r) * groups + c
+
+    def home_perm(m):
+        return [
+            (device(d, r, c), device(d - d % 2 + r, d % 2, c ^ m))
+            for d in range(mesh_shape[0])
+            for r in range(mesh_shape[1])
+            for c in range(groups)
+        ]
+
+    core_pairs = [(d, d ^ 1) for d in range(mesh_shape[0])]
+    row_pairs = [(0, 1), (1, 0)]
+
+    def send_home(pieces):
+        return [
+            lax.ppermute(piece, (DP, ROWS, CHAN), home_perm(m))
+            for m, piece in enumerate(pieces)
+        ]
+
+    def crops_home(value):
+        return send_home(
+            [lax.dynamic_index_in_dim(value, z ^ m, 0, keepdims=False) for m in range(groups)]
+        )
+
+    def swap_core(value):
+        return lax.ppermute(value, DP, core_pairs)
+
+    def in_order(pieces, axis):
+        stacked = jnp.stack(pieces)
+        return jnp.concatenate(
+            [lax.dynamic_index_in_dim(stacked, z ^ m, 0, keepdims=False) for m in range(groups)],
+            axis=axis,
+        )
+
+    def own_and_far(value, axis):
+        far = swap_core(value)
+        return jnp.concatenate(
+            [jnp.where(core == 0, value, far), jnp.where(core == 0, far, value)], axis=axis
+        )
+
+    def own_rows(value, axis):
+        return lax.dynamic_slice_in_dim(value, core * rows_here, rows_here, axis)
+
+    def gather(parts):
+        packed = jnp.concatenate([part.reshape(-1, chans) for part in parts])
+        whole = lax.all_gather(packed, CHAN, axis=0)
+        cuts, at = [], 0
+        for part in parts:
+            size = part.size // chans
+            cuts.append(whole[:, at : at + size])
+            at += size
+        return cuts
+
+    w8, wg, wb = gather(
+        [w_tri_in.transpose(0, 1, 3, 2), w_out_gate.transpose(0, 2, 1), w_bias.T]
+    )
+    wg = wg.reshape(groups, 2, -1, chans).transpose(1, 0, 2, 3).reshape(2, chans, chans)
+    heads = groups * w_bias.shape[1]
+    wb = wb.reshape(heads, chans)
+    pieces = crops_home(pair)
+    positions = jnp.arange(crop_len, dtype=jnp.int32)
+    live = present.astype(jnp.float32) * (positions[None, :] < lengths[:, None]).astype(jnp.float32)
+    live = lax.dynamic_index_in_dim(live, z, 0, keepdims=False)
+    live = jnp.where(x == core, live, swap_core(live))
+    live_rows = own_rows(live, 0)
+    mask_rows = live_rows[:, None] * live[None, :]
+    node_pieces = crops_home(node)
+
+    lo, ro, li, ri, norm_in, pair_home, bias = project(
+        place, pieces, mask_rows, gain_pair.reshape(-1, 1), w8, wb
+    )
+    ro_far, ri_far, li_far, lo_far = swap_core(ro), swap_core(ri), swap_core(li), swap_core(lo)
+
+    wto, wti, wout, wq, wa, wni, wno = gather(
+        [
+            w_tri_out.transpose(0, 2, 1),
+            w_trans_in.T,
+            w_trans_out,
+            w_qkv.transpose(0, 2, 1),
+            w_attn_out.T,
+            w_node_in.T,
+            w_node_out,
+        ]
+    )
+    wto = wto.reshape(groups, 2, -1, chans).transpose(1, 0, 2, 3).reshape(2, chans, chans)
+    wti, wout = wti.reshape(-1, chans), wout.reshape(-1, chans)
+    cot_pieces = crops_home(pair_cot)
+    node_cot_pieces = crops_home(node_cot)
+
+    out0, out1, out2, out3, grad_mid, grad_gate, go, gi, gw_in, gw_out, gw_tri, gg_trans, gg_tri = middle(
+        place,
+        (lo, ro, ro_far, li, li_far, ri, ri_far),
+        pair_home,
+        norm_in,
+        cot_pieces,
+        gain_tri.reshape(2, -1, 1),
+        gain_trans.reshape(-1, 1),
+        wg,
+        wto,
+        wti,
+        wout,
+    )
+    go_far, gi_far = swap_core(go), swap_core(gi)
+    out_back = send_home([out0, out1, out2, out3])
+
+    wq = wq.reshape(groups, 3, -1, nodes).transpose(1, 0, 2, 3).reshape(3, -1, nodes)
+    wa, wni, wno = wa.reshape(nodes, -1), wni.reshape(-1, nodes), wno.reshape(-1, nodes)
+    node_in = own_and_far(in_order(node_pieces, 1), 0).astype(jnp.float32)
+    cot = own_and_far(in_order(node_cot_pieces, 1), 0)
+    bias = own_and_far(bias, 0).transpose(1, 0, 2)
+    node_outs = node_track(node_in, cot, bias, live, wq, wa, wni, wno, gain_node, gain_node_trans)
+    node_out, node_grad, scores, gw_node, gg_node = node_outs
+    scores = own_rows(scores, 1).transpose(1, 0, 2).astype(jnp.float32)
+
+    def node_back(value):
+        value = own_rows(value.astype(jnp.bfloat16), 0)
+        width = nodes // groups
+        return send_home(
+            [lax.dynamic_slice_in_dim(value, (z ^ m) * width, width, 1) for m in range(groups)]
+        )
+
+    node_out_back, node_grad_back = node_back(node_out), node_back(node_grad)
+
+    wall = jnp.concatenate([w8.reshape(-1, chans), wg.reshape(-1, chans), wb])
+    wall = jnp.pad(wall, ((0, -wall.shape[0] % 128), (0, 0)))
+    g0, g1, g2, g3, gw, gg_pair = finish(
+        place,
+        (lo, lo_far, ro, ro_far, li, ri, go, go_far, gi, gi_far),
+        pair_home,
+        norm_in,
+        grad_mid,
+        grad_gate,
+        scores,
+        mask_rows,
+        gain_pair.reshape(-1, 1),
+        w8,
+        wall,
+    )
+    grad_back = send_home([g0, g1, g2, g3])
+
+    def reduce(parts):
+        packed = jnp.concatenate(parts, axis=1).astype(jnp.float32)
+        count = packed.shape[1]
+        packed = jnp.pad(packed, ((0, 0), (0, -count % 128), (0, 0)))
+        y = lax.axis_index(DP) // 2
+        rounds = (
+            (core, DP, core_pairs),
+            (x, ROWS, row_pairs),
+            (y, DP, [(d, d ^ 2) for d in range(mesh_shape[0])]),
+        )
+        for side, axis, pairs in rounds:
+            half = packed.shape[1] // 2
+            low, high = packed[:, :half], packed[:, half:]
+            sent = jnp.where(side == 0, high, low).astype(jnp.bfloat16)
+            kept = jnp.where(side == 0, low, high)
+            packed = kept + lax.ppermute(sent, axis, pairs).astype(jnp.float32)
+        low = packed.astype(jnp.bfloat16)
+        total = lax.dynamic_index_in_dim(packed, z, 0, keepdims=False)
+        for m in range(1, groups):
+            sent = lax.dynamic_index_in_dim(low, z ^ m, 0, keepdims=False)
+            total = total + lax.ppermute(
+                sent, CHAN, [(c, c ^ m) for c in range(groups)]
+            ).astype(jnp.float32)
+        total = total.astype(jnp.bfloat16)
+        for side, axis, pairs in rounds[::-1]:
+            far = lax.ppermute(total, axis, pairs)
+            total = jnp.concatenate(
+                [jnp.where(side == 0, total, far), jnp.where(side == 0, far, total)]
+            )
+        total = total.astype(jnp.float32)
+        cuts, at = [], 0
+        for part in parts:
+            cuts.append(total[at : at + part.shape[1]])
+            at += part.shape[1]
+        return cuts
+
+    def by_chan(value):
+        a, b, c = value.shape
+        return value.reshape(a, groups, b // groups, c).transpose(1, 0, 2, 3).reshape(groups, -1, c)
+
+    def gains(*values):
+        return jnp.concatenate(
+            [value.reshape(-1, groups, value.shape[-1] // groups).transpose(1, 0, 2).reshape(groups, -1) for value in values],
+            axis=1,
+        ).reshape(groups, -1, chans)
+
+    gq, ga, gni, gno = gw_node
+    early = reduce(
+        [
+            gw_in.reshape(groups, -1, chans),
+            gw_out.reshape(groups, -1, chans),
+            by_chan(gw_tri),
+            by_chan(gq).reshape(groups, -1, chans),
+            ga.reshape(groups, -1, chans),
+            gni.reshape(groups, -1, chans),
+            gno.reshape(groups, -1, chans),
+            gains(*gg_node),
+            gains(jnp.sum(gg_trans, axis=-1), jnp.sum(gg_tri, axis=-1), jnp.zeros_like(gain_trans)),
+        ]
+    )
+    tri_rows, gate_rows = 8 * chans, 10 * chans
+    late = reduce(
+        [
+            gw[:tri_rows].reshape(groups, -1, chans),
+            by_chan(gw[tri_rows:gate_rows].reshape(2, chans, chans)),
+            gw[gate_rows : gate_rows + heads].reshape(groups, -1, chans),
+            gains(jnp.sum(gg_pair, axis=-1), jnp.zeros((3, chans), jnp.float32)),
+        ]
+    )
+    quarter = chans // groups
+
+    def assemble(pieces):
+        return jnp.stack(
+            [lax.dynamic_index_in_dim(jnp.stack(pieces), z ^ k, 0, keepdims=False) for k in range(groups)]
+        )
+
+    node_quarter = nodes // groups
+    return (
+        assemble(out_back),
+        assemble(node_out_back),
+        assemble(grad_back),
+        assemble(node_grad_back),
+        late[3].reshape(4, quarter)[0],
+        late[0].reshape(2, 4, quarter, chans).transpose(0, 1, 3, 2),
+        late[1].reshape(2, quarter, chans).transpose(0, 2, 1),
+        early[8].reshape(4, quarter)[1:3],
+        early[2].reshape(2, quarter, chans).transpose(0, 2, 1),
+        early[8].reshape(4, quarter)[0],
+        early[0].T,
+        early[1],
+        late[2].T,
+        early[7].reshape(2, node_quarter)[0],
+        early[3].reshape(3, node_quarter, nodes).transpose(0, 2, 1),
+        early[4].reshape(node_quarter, nodes).T,
+        early[7].reshape(2, node_quarter)[1],
+        early[5].reshape(-1, nodes).T,
+        early[6].reshape(-1, nodes),
+    )
+
+
+def node_track(node_in, cot, bias, live, wq, wa, wni, wno, gain_node, gain_node_trans):
+    length, nodes = node_in.shape
+    heads = bias.shape[0]
+    head_dim = wq.shape[1] // heads
+    scale = 1.0 / math.sqrt(head_dim)
+    key_live = live[None, None, :] > 0.5
+
+    def parts(value):
+        centered = value - jnp.mean(value, axis=-1, keepdims=True)
+        inverse = lax.rsqrt(jnp.mean(centered * centered, axis=-1, keepdims=True) + epsilon)
+        return centered * inverse, inverse
+
+    def back(gain, scaled, inverse, grad):
+        weighted = gain * grad
+        first = jnp.mean(weighted, axis=-1, keepdims=True)
+        second = jnp.mean(weighted * scaled, axis=-1, keepdims=True)
+        return inverse * (weighted - first - scaled * second)
+
+    def mul(spec, a, b):
+        return jnp.einsum(spec, a, b, preferred_element_type=jnp.float32)
+
+    scaled_in, inverse_in = parts(node_in)
+    low_in = (scaled_in * gain_node).astype(jnp.bfloat16)
+    qkv = mul("in,gan->gia", low_in, wq).astype(jnp.bfloat16)
+    queries, keys, values = (qkv[g].reshape(length, heads, head_dim) for g in range(3))
+    raw = mul("ihd,jhd->hij", queries, keys) * scale + bias
+    probs = softmax_rows(jnp.where(key_live, raw, masked_score))
+    probs_low = probs.astype(jnp.bfloat16)
+    attn = mul("hij,jhd->ihd", probs_low, values).astype(jnp.bfloat16).reshape(length, -1)
+    mid = node_in + mul("ia,na->in", attn, wa)
+    scaled_mid, inverse_mid = parts(mid)
+    low_mid = (scaled_mid * gain_node_trans).astype(jnp.bfloat16)
+    pre = mul("in,fn->if", low_mid, wni)
+    act, slope = gelu_both(pre)
+    act = act.astype(jnp.bfloat16)
+    node_out = mid + mul("if,fn->in", act, wno)
+    grad_pre = (mul("in,fn->if", cot, wno) * slope).astype(jnp.bfloat16)
+    gno = mul("if,in->fn", act, cot)
+    gni = mul("if,in->fn", grad_pre, low_mid)
+    grad = mul("if,fn->in", grad_pre, wni)
+    gg_mid = jnp.sum(grad * scaled_mid, axis=0)
+    grad_mid = cot.astype(jnp.float32) + back(gain_node_trans, scaled_mid, inverse_mid, grad)
+    grad_low = grad_mid.astype(jnp.bfloat16)
+    ga = mul("in,ia->na", grad_low, attn)
+    grad_attn = mul("in,na->ia", grad_low, wa).astype(jnp.bfloat16).reshape(length, heads, head_dim)
+    grad_probs = mul("ihd,jhd->hij", grad_attn, values)
+    delta = jnp.sum(probs * grad_probs, axis=2, keepdims=True)
+    scores = (probs * (grad_probs - delta)).astype(jnp.bfloat16)
+    grad_q = mul("hij,jhd->ihd", scores, keys) * scale
+    grad_k = mul("hij,ihd->jhd", scores, queries) * scale
+    grad_v = mul("hij,ihd->jhd", probs_low, grad_attn)
+    grad_qkv = jnp.stack([v.reshape(length, -1) for v in (grad_q, grad_k, grad_v)]).astype(jnp.bfloat16)
+    gq = mul("gia,in->gan", grad_qkv, low_in)
+    grad = mul("gia,gan->in", grad_qkv, wq)
+    gg_in = jnp.sum(grad * scaled_in, axis=0)
+    node_grad = grad_mid + back(gain_node, scaled_in, inverse_in, grad)
+    halves = [0.5 * v for v in (gq, ga, gni, gno)]
+    return node_out, node_grad, scores, halves, (0.5 * gg_in, 0.5 * gg_mid)
+
+
 def solution(mesh):
     in_specs = (
-        P("dp", "rows", "chan", None),
-        P("dp", "rows", "chan"),
-        P("dp", "rows", "chan", None),
-        P("dp", "rows", "chan"),
-        P("dp"),
-        P("dp", None),
+        P(DP, ROWS, CHAN, None),
+        P(DP, ROWS, CHAN),
+        P(DP, ROWS, CHAN, None),
+        P(DP, ROWS, CHAN),
+        P(DP),
+        P(DP, None),
         P(),
-        P(None, None, None, "chan"),
-        P(None, None, "chan"),
+        P(None, None, None, CHAN),
+        P(None, None, CHAN),
         P(),
-        P(None, None, "chan"),
+        P(None, None, CHAN),
         P(),
-        P(None, "chan"),
-        P("chan", None),
-        P(None, "chan"),
+        P(None, CHAN),
+        P(CHAN, None),
+        P(None, CHAN),
         P(),
-        P(None, None, "chan"),
-        P(None, "chan"),
+        P(None, None, CHAN),
+        P(None, CHAN),
         P(),
-        P(None, "chan"),
-        P("chan", None),
+        P(None, CHAN),
+        P(CHAN, None),
     )
     out_specs = (
-        P("dp", "rows", "chan", None),
-        P("dp", "rows", "chan"),
-        P("dp", "rows", "chan", None),
-        P("dp", "rows", "chan"),
-        P("chan"),
-        P(None, None, None, "chan"),
-        P(None, None, "chan"),
-        P(None, "chan"),
-        P(None, None, "chan"),
-        P("chan"),
-        P(None, "chan"),
-        P("chan", None),
-        P(None, "chan"),
-        P("chan"),
-        P(None, None, "chan"),
-        P(None, "chan"),
-        P("chan"),
-        P(None, "chan"),
-        P("chan", None),
-    )
-    return jax.shard_map(shards, mesh=mesh, in_specs=in_specs, out_specs=out_specs, check_vma=False)
+        P(DP, ROWS, CHAN, None),
+        P(DP, ROWS, CHAN),
+        P(DP, ROWS, CHAN, None),
+        P(DP, ROWS, CHAN),
+        P(CHAN),
+        P(None, None, None, CHAN),
+        P(None, None, CHAN),
+        P(None, CHAN),
+        P(None, None, CHAN),
+        P(CHAN),
+        P(None, CHAN),
+        P(CHAN, None),
+        P(None, CHAN),
+        P(CHAN),
+        P(None, None, CHAN),
+        P(None, CHAN),
+        P(CHAN),
+        P(None, CHAN),
+        P(CHAN, None),
+    )
+    sizes = dict(mesh.shape)
+    by_crop = sizes[ROWS] == 2 and sizes[DP] == 4 and sizes[CHAN] == 4
+    body = shards_by_crop if by_crop else shards
+    return jax.shard_map(body, mesh=mesh, in_specs=in_specs, out_specs=out_specs, check_vma=False)

time: 2330 us -> 562 us (0.24)
  waiting for transfers between devices: 1430 us -> 189 us
  matrix products: 309 us -> 9.26 us
  blocking collectives: 166 us -> 16.5 us
  other arithmetic: 188 us -> 39.7 us
  Pallas kernels: 0 us -> 148 us
  local copies, waits for them, and re-layouts: 200 us -> 61.2 us
  starting transfers between devices: 2.31 us -> 80.8 us
    all_gather x8 -> x1, waiting for transfers between devices: 641 us -> 0.02 us  [gather(): whole = lax.all_gather(packed, CHAN, axis=0)]
    reduce_scatter x7 -> x0, waiting for transfers between devices: 366 us -> none  [the longest x1 147 us: shards(): lax.psum_scatter(grad_normed_mid.astype(jnp.bfloat16), 'chan', scatter_di...]
    unnamed x35 -> x1, waiting for transfers between devices: 309 us -> 0.02 us
    dot_general x43 -> x18, matrix products: 309 us -> 9.26 us  [mul(): return jnp.einsum(spec, a, b, preferred_element_type=jnp.float32)]
    ppermute x0 -> x60, waiting for transfers between devices: none -> 189 us  [the longest x32 147 us: send_home(): lax.ppermute(piece, (DP, ROWS, CHAN), home_perm(m))]
    pallas_call x0 -> x3, Pallas kernels: none -> 148 us  [the longest x1 73 us: middle(): pl.pallas_call(functools.partial(middle_kernel, h_steps), grid=(h_steps +...]
    psum x2 -> x0, waiting for transfers between devices: 117 us -> none  [shards(): lax.psum((grad_gain_pair, grad_tri_in_w, grad_out_gate, grad_gain_tri, gr...]
    unnamed x286 -> x170, local copies, waits for them, and re-layouts: 120 us -> 15.8 us
  transfers between devices with their start and end apart: 26 -> 61, of which waited for: 17 -> 21; matrix products, arithmetic and copies ran while one was open for 24% -> 12% of each run, Pallas kernels for 0% -> 13%
where the time goes in v1:
time: 562 us; the launch traced here: 560 us
  waiting for transfers between devices  189 us (34%)
  Pallas kernels  148 us (26%)
  starting transfers between devices  80.8 us (14%)
  local copies, waits for them, and re-layouts  61.2 us (11%)
  other arithmetic  39.7 us (7%)
  blocking collectives  16.5 us (3%)
  between operations  15.9 us (3%)
  matrix products  9.26 us (2%)
    ppermute x32, waiting for transfers between devices, send_home(): lax.ppermute(piece, (DP, ROWS, CHAN), home_perm(m))  147 us
    pallas_call x1, Pallas kernels, middle(): pl.pallas_call(functools.partial(middle_kernel, h_steps), grid=(h_steps +...  73 us
    pallas_call x1, Pallas kernels, finish(): pl.pallas_call(functools.partial(finish_kernel, h_steps), grid=(h_steps +...  49.5 us
    ppermute x32, starting transfers between devices, send_home(): lax.ppermute(piece, (DP, ROWS, CHAN), home_perm(m))  41.8 us
    ppermute x6, waiting for transfers between devices, reduce(): packed = kept + lax.ppermute(sent, axis, pairs).astype(jnp.float32)  28 us
    pallas_call x1, Pallas kernels, project(): pl.pallas_call(project_kernel, grid=grid, in_specs=[pl.BlockSpec(memory_s...  25 us
    ppermute x10, starting transfers between devices, swap_core(): return lax.ppermute(value, DP, core_pairs)  22.2 us
    all_gather x1, blocking collectives, gather(): whole = lax.all_gather(packed, CHAN, axis=0)  16.5 us
  transfers between devices with their start and end apart: 61, of which 21 were waited for; matrix products, arithmetic and copies ran while one was open for 12% of the time, Pallas kernels for 13%

profile of v1, /device:TPU:8, one launch (start us, length us, event | category | flops | bytes accessed | tf_op | source)
XLA Modules:
  0.0 559.6 jit_solution(10877146473946371619)
XLA Ops:
  9.0 3.0 collective-permute-start.18
  19.6 3.2 collective-permute-start.4
  22.7 16.5 %all-gather.2 = bf16[4,322,128]{2,1,0:T(8,128)(2,1)S(1)} all-gather(bf16[1,322,128]{2,1,0:T(8,128)(2,1)S(1)} %maximum_bitcast_fusion.1), channel_id=2, replica_groups=mesh['dp'=4,'rows'=2,'chan'=4] {'chan'}, dimensions={0}, use_global_device_ids=true | all-gather | bytes 412160 | tf_op jit(solution)/shard_map/all_gather | solution.py:915
  41.6 3.2 dynamic-slice_bitcast_fusion
  53.7 3.1 collective-permute-start.2
  56.9 6.6 %collective-permute-start.20 = (bf16[64,256]{1,0:T(8,128)(2,1)S(1)}, bf16[64,256]{1,0:T(8,128)(2,1)S(1)}, u32[]{:S(2)}, u32[]{:S(2)}) collective-permute-start(bf16[64,256]{1,0:T(8,128)(2,1)S(1)} %pad_maximum_fusion.18), channel_id=1, source_target_pairs={{0,8},{8,0},{16,24},{24,16},{1,9},{9,1},{17,25},{25,17},{2,10},{10... | collective-permute-start | bytes 98312 | tf_op jit(solution)/shard_map/ppermute | solution.py:895
  64.3 3.5 collective-permute-start.10
  68.4 19.2 %collective-permute-done.1.p1 = bf16[64,32,128]{2,1,0:T(8,128)(2,1)S(1)} collective-permute-done((bf16[64,32,128]{2,1,0:T(8,128)(2,1)S(1)}, bf16[64,32,128]{2,1,0:T(8,128)(2,1)S(1)}, u32[]{:S(2)}, u32[]{:S(2)}) %collective-permute-start.1) | collective-permute-done | bytes 524320 | tf_op jit(solution)/shard_map/ppermute | solution.py:885
  89.5 45.3 %collective-permute-done.3.p3 = bf16[64,32,128]{2,1,0:T(8,128)(2,1)S(1)} collective-permute-done((bf16[64,32,128]{2,1,0:T(8,128)(2,1)S(1)}, bf16[64,32,128]{2,1,0:T(8,128)(2,1)S(1)}, u32[]{:S(2)}, u32[]{:S(2)}) %collective-permute-start.3) | collective-permute-done | bytes 524320 | tf_op jit(solution)/shard_map/ppermute | solution.py:885
  134.9 25.0 %project.1 = (bf16[128,64,128]{2,1,0:T(8,128)(2,1)S(1)}, bf16[128,64,128]{2,1,0:T(8,128)(2,1)}, bf16[128,64,128]{2,1,0:T(8,128)(2,1)}, bf16[128,64,128]{2,1,0:T(...) custom-call(s32[2]{0:T(128)S(1)} %pad_add_fusion.zc_ref.place_ref, ...), custom_call_target="tpu_custom_call" | custom-call | flops 2147483648 | bytes 20971520 | tf_op jit(solution)/shard_map/project/pallas_call | solution.py:533
  161.3 4.2 collective-permute-start.21
  172.5 8.3 %fusion.78 = (f32[8,128]{0,1:T(8,128)S(1)}, f32[8,128,128]{2,0,1:T(8,128)S(1)}) fusion(f32[64,8,128]{2,1,0:T(8,128)S(1)} %get-tuple-element.181, f32[64,8,128]{2,1,0:T(8,128)S(1)} %get-tuple-element.180, f32[8,128,128]{2,1,0:T(8,128)S(1)} %fusion.80, pred[128]{0:T(512)(128)(4,1)S(1)} %get-tuple-element.157), kind=kOutput, calls=%fused_computation.260 | output fusion | flops 786559 | bytes 1577088 | tf_op jit(solution)/shard_map/sub | solution.py:66
  186.2 6.4 %fusion.6 = bf16[8,128,128]{2,0,1:T(8,128)(2,1)S(1)} fusion(f32[8,128,128]{2,1,0:T(8,128)S(1)} %fusion.81, f32[8,128,128]{2,0,1:T(8,128)S(1)} %get-tuple-element.247, f32[8,128]{0,1:T(8,128)} %copy-done.45), kind=kOutput, calls=%fused_computation.17 | output fusion | flops 787583 | bytes 1314816 | tf_op jit(solution)/shard_map/sub | solution.py:1157
  195.5 5.4 collective-permute-start.8
  205.4 8.2 %collective-permute-done.9.c1 = bf16[64,32,128]{2,1,0:T(8,128)(2,1)} collective-permute-done((bf16[64,32,128]{2,1,0:T(8,128)(2,1)}, bf16[64,32,128]{2,1,0:T(8,128)(2,1)}, u32[]{:S(2)}, u32[]{:S(2)}) %collective-permute-start.9) | collective-permute-done | bytes 524320 | tf_op jit(solution)/shard_map/ppermute | solution.py:885
  213.6 73.0 %middle.1 = (bf16[64,32,128]{2,1,0:T(8,128)(2,1)}, bf16[64,32,128]{2,1,0:T(8,128)(2,1)}, bf16[64,32,128]{2,1,0:T(8,128)(2,1)}, bf16[64,32,128]{2,1,0:T(8,128)(2,...) custom-call(s32[2]{0:T(128)} %copy-done.5, ...), custom_call_target="tpu_custom_call" | custom-call | flops 11000000512 | bytes 41943040 | tf_op jit(solution)/shard_map/middle/pallas_call | solution.py:698
  301.3 11.0 %concatenate.76 = f32[4,1858,128]{2,1,0:T(8,128)} concatenate(f32[4,128,128]{2,1,0:T(8,128)} %bitcast.271, f32[4,128,128]{2,1,0:T(8,128)} %bitcast.273, f32[4,64,128]{2,1,0:T(8,128)} %bitcast.267, f32[4,384,128]{2,1,0:T(8,128)S(1)} %reshape_reshape.11, f32[4,128,128]{2,1,0:T(8,128)S(1)} %reshape.290, f32[4,512,128]{2,1,0:T(8,128)S(1)} %reshape.291, f32[4,512,128]{2,1,0:T(8,128)S(1)} %reshape.292, ...), dimensions={1} | concatenate | bytes 7610368 | tf_op jit(solution)/shard_map/concatenate | solution.py:1011
  323.3 10.1 %collective-permute-done.52 = bf16[4,480,128]{2,1,0:T(8,128)(2,1)S(1)} collective-permute-done((bf16[4,480,128]{2,1,0:T(8,128)(2,1)S(1)}, bf16[4,480,128]{2,1,0:T(8,128)(2,1)S(1)}, u32[]{:S(2)}, u32[]{:S(2)}) %collective-permute-start.52) | collective-permute-done | bytes 491552 | tf_op jit(solution)/shard_map/ppermute | solution.py:1025
  344.4 5.8 %collective-permute-start.26 = (bf16[128,64,128]{2,1,0:T(8,128)(2,1)S(1)}, bf16[128,64,128]{2,1,0:T(8,128)(2,1)S(1)}, u32[]{:S(2)}, u32[]{:S(2)}) collective-permute-start(bf16[128,64,128]{2,1,0:T(8,128)(2,1)S(1)} %copy-done.2), channel_id=1, source_target_pairs={{0,8},{8,0},{16,24},{24,16},{1,9},{9,1},{17,25},{25,17},{2,10},{10... | collective-permute-start | bytes 6291464 | tf_op jit(solution)/shard_map/ppermute | solution.py:895
  351.2 3.2 collective-permute-start.54
  357.7 2.8 collective-permute-done.55
  363.5 32.1 %collective-permute-done.14 = bf16[64,32,128]{2,1,0:T(8,128)(2,1)S(1)} collective-permute-done((bf16[64,32,128]{2,1,0:T(8,128)(2,1)S(1)}, bf16[64,32,128]{2,1,0:T(8,128)(2,1)S(1)}, u32[]{:S(2)}, u32[]{:S(2)}) %collective-permute-start.14) | collective-permute-done | bytes 524320 | tf_op jit(solution)/shard_map/ppermute | solution.py:885
  396.1 11.1 %collective-permute-done.15 = bf16[64,32,128]{2,1,0:T(8,128)(2,1)S(1)} collective-permute-done((bf16[64,32,128]{2,1,0:T(8,128)(2,1)S(1)}, bf16[64,32,128]{2,1,0:T(8,128)(2,1)S(1)}, u32[]{:S(2)}, u32[]{:S(2)}) %collective-permute-start.15) | collective-permute-done | bytes 524320 | tf_op jit(solution)/shard_map/ppermute | solution.py:885
  407.5 4.5 collective-permute-start.58
  418.6 49.5 %finish.1 = (bf16[64,32,128]{2,1,0:T(8,128)(2,1)}, bf16[64,32,128]{2,1,0:T(8,128)(2,1)}, bf16[64,32,128]{2,1,0:T(8,128)(2,1)}, bf16[64,32,128]{2,1,0:T(8,128)(2,...) custom-call(s32[2]{0:T(128)} %copy-done.5, bf16[128,64,128]{2,1,0:T(8,128)(2,1)} %copy-done.1, ...), custom_call_target="tpu_custom_call" | custom-call | flops 8000000000 | bytes 41943040 | tf_op jit(solution)/shard_map/finish/pallas_call | solution.py:817
  472.5 5.4 collective-permute-start.34
  479.2 12.0 %collective-permute-done.43 = bf16[4,96,128]{2,1,0:T(8,128)(2,1)S(1)} collective-permute-done((bf16[4,96,128]{2,1,0:T(8,128)(2,1)S(1)}, bf16[4,96,128]{2,1,0:T(8,128)(2,1)S(1)}, u32[]{:S(2)}, u32[]{:S(2)}) %collective-permute-start.43) | collective-permute-done | bytes 98336 | tf_op jit(solution)/shard_map/ppermute | solution.py:1025
  491.9 3.5 collective-permute-done.44
  503.3 2.6 collective-permute-done.48
  506.9 3.1 collective-permute-done.49
  518.4 16.8 %collective-permute-done.36 = bf16[64,32,128]{2,1,0:T(8,128)(2,1)} collective-permute-done((bf16[64,32,128]{2,1,0:T(8,128)(2,1)}, bf16[64,32,128]{2,1,0:T(8,128)(2,1)}, u32[]{:S(2)}, u32[]{:S(2)}) %collective-permute-start.36) | collective-permute-done | bytes 524320 | tf_op jit(solution)/shard_map/ppermute | solution.py:885
  535.3 12.3 %collective-permute-done.37 = bf16[64,32,128]{2,1,0:T(8,128)(2,1)} collective-permute-done((bf16[64,32,128]{2,1,0:T(8,128)(2,1)}, bf16[64,32,128]{2,1,0:T(8,128)(2,1)}, u32[]{:S(2)}, u32[]{:S(2)}) %collective-permute-start.37) | collective-permute-done | bytes 524320 | tf_op jit(solution)/shard_map/ppermute | solution.py:885
  (434 shorter events, 123.9 us)
Async XLA Ops:
  7.3 159.9 %all-gather.5.cloned.1.call-start = ((), (), s32[]{:S(2)}) async-start(), calls=%async_computation | async-start | bytes 2375680 | tf_op jit(solution)/shard_map/all_gather | solution.py:915
  8.2 39.6 %collective-permute-start.16 = (bf16[64,64]{1,0:T(8,128)(2,1)S(1)}, bf16[64,64]{1,0:T(8,128)(2,1)S(1)}, u32[]{:S(2)}, u32[]{:S(2)}) collective-permute-start(bf16[64,64]{1,0:T(8,128)(2,1)S(1)} %get-tuple-element.235), channel_id=1, source_target_pairs={{0,0},{1,1},{2,2},{3,3},{4,8},{5,9},{6,10},{7,11},{8,4},{9,5},{10,... | collective-permute-start | bytes 24584 | tf_op jit(solution)/shard_map/ppermute | solution.py:885
  8.9 39.6 %collective-permute-start.17 = (bf16[64,64]{1,0:T(8,128)(2,1)S(1)}, bf16[64,64]{1,0:T(8,128)(2,1)S(1)}, u32[]{:S(2)}, u32[]{:S(2)}) collective-permute-start(bf16[64,64]{1,0:T(8,128)(2,1)S(1)} %get-tuple-element.236), channel_id=1, source_target_pairs={{0,1},{1,0},{2,3},{3,2},{4,9},{5,8},{6,11},{7,10},{8,5},{9,4},{10,... | collective-permute-start | bytes 24584 | tf_op jit(solution)/shard_map/ppermute | solution.py:885
  9.0 40.1 %collective-permute-start.18 = (bf16[64,64]{1,0:T(8,128)(2,1)S(1)}, bf16[64,64]{1,0:T(8,128)(2,1)S(1)}, u32[]{:S(2)}, u32[]{:S(2)}) collective-permute-start(bf16[64,64]{1,0:T(8,128)(2,1)S(1)} %get-tuple-element.238), channel_id=1, source_target_pairs={{0,2},{1,3},{2,0},{3,1},{4,10},{5,11},{6,8},{7,9},{8,6},{9,7},{10,... | collective-permute-start | bytes 24584 | tf_op jit(solution)/shard_map/ppermute | solution.py:885
  12.0 39.4 %collective-permute-start.19 = (bf16[64,64]{1,0:T(8,128)(2,1)S(1)}, bf16[64,64]{1,0:T(8,128)(2,1)S(1)}, u32[]{:S(2)}, u32[]{:S(2)}) collective-permute-start(bf16[64,64]{1,0:T(8,128)(2,1)S(1)} %get-tuple-element.237), channel_id=1, source_target_pairs={{0,3},{1,2},{2,1},{3,0},{4,11},{5,10},{6,9},{7,8},{8,7},{9,6},{10,... | collective-permute-start | bytes 24584 | tf_op jit(solution)/shard_map/ppermute | solution.py:885
  19.6 27.4 %collective-permute-start.4 = (f32[128]{0:T(128)S(1)}, f32[128]{0:T(128)S(1)}, u32[]{:S(2)}, u32[]{:S(2)}) collective-permute-start(f32[128]{0:T(128)S(1)} %fusion.61), channel_id=1, source_target_pairs={{0,8},{8,0},{16,24},{24,16},{1,9},{9,1},{17,25},{25,17},{2,10},{10... | collective-permute-start | bytes 1544 | tf_op jit(solution)/shard_map/ppermute | solution.py:895
  47.0 21.3 %collective-permute-start = (bf16[64,32,128]{2,1,0:T(8,128)(2,1)S(1)}, bf16[64,32,128]{2,1,0:T(8,128)(2,1)S(1)}, u32[]{:S(2)}, u32[]{:S(2)}) collective-permute-start(bf16[64,32,128]{2,1,0:T(8,128)(2,1)S(1)} %copy-done.39), channel_id=1, source_target_pairs={{0,0},{1,1},{2,2},{3,3},{4,8},{5,9},{6,10},{7,11},{8,4},{9,5},{10,... | collective-permute-start | bytes 1572872 | tf_op jit(solution)/shard_map/ppermute | solution.py:885
  52.3 35.3 %collective-permute-start.1 = (bf16[64,32,128]{2,1,0:T(8,128)(2,1)S(1)}, bf16[64,32,128]{2,1,0:T(8,128)(2,1)S(1)}, u32[]{:S(2)}, u32[]{:S(2)}) collective-permute-start(bf16[64,32,128]{2,1,0:T(8,128)(2,1)S(1)} %copy-done.38), channel_id=1, source_target_pairs={{0,1},{1,0},{2,3},{3,2},{4,9},{5,8},{6,11},{7,10},{8,5},{9,4},{10,... | collective-permute-start | bytes 1572872 | tf_op jit(solution)/shard_map/ppermute | solution.py:885
  53.7 35.8 %collective-permute-start.2 = (bf16[64,32,128]{2,1,0:T(8,128)(2,1)S(1)}, bf16[64,32,128]{2,1,0:T(8,128)(2,1)S(1)}, u32[]{:S(2)}, u32[]{:S(2)}) collective-permute-start(bf16[64,32,128]{2,1,0:T(8,128)(2,1)S(1)} %copy-done.37), channel_id=1, source_target_pairs={{0,2},{1,3},{2,0},{3,1},{4,10},{5,11},{6,8},{7,9},{8,6},{9,7},{10,... | collective-permute-start | bytes 1572872 | tf_op jit(solution)/shard_map/ppermute | solution.py:885
  56.8 78.1 %collective-permute-start.3 = (bf16[64,32,128]{2,1,0:T(8,128)(2,1)S(1)}, bf16[64,32,128]{2,1,0:T(8,128)(2,1)S(1)}, u32[]{:S(2)}, u32[]{:S(2)}) collective-permute-start(bf16[64,32,128]{2,1,0:T(8,128)(2,1)S(1)} %get-tuple-element.171), channel_id=1, source_target_pairs={{0,3},{1,2},{2,1},{3,0},{4,11},{5,10},{6,9},{7,8},{8,7},{9,6},{10,... | collective-permute-start | bytes 1572872 | tf_op jit(solution)/shard_map/ppermute | solution.py:885
  64.3 131.2 %collective-permute-start.10 = (bf16[64,32,128]{2,1,0:T(8,128)(2,1)}, bf16[64,32,128]{2,1,0:T(8,128)(2,1)}, u32[]{:S(2)}, u32[]{:S(2)}) collective-permute-start(bf16[64,32,128]{2,1,0:T(8,128)(2,1)} %get-tuple-element.170), channel_id=1, source_target_pairs={{0,2},{1,3},{2,0},{3,1},{4,10},{5,11},{6,8},{7,9},{8,6},{9,7},{10,... | collective-permute-start | bytes 1572872 | tf_op jit(solution)/shard_map/ppermute | solution.py:885
  68.3 132.6 %collective-permute-start.11 = (bf16[64,32,128]{2,1,0:T(8,128)(2,1)}, bf16[64,32,128]{2,1,0:T(8,128)(2,1)}, u32[]{:S(2)}, u32[]{:S(2)}) collective-permute-start(bf16[64,32,128]{2,1,0:T(8,128)(2,1)} %get-tuple-element.167), channel_id=1, source_target_pairs={{0,3},{1,2},{2,1},{3,0},{4,11},{5,10},{6,9},{7,8},{8,7},{9,6},{10,... | collective-permute-start | bytes 1572872 | tf_op jit(solution)/shard_map/ppermute | solution.py:885
  87.6 77.9 %collective-permute-start.33 = (bf16[64,256]{1,0:T(8,128)(2,1)S(1)}, bf16[64,256]{1,0:T(8,128)(2,1)S(1)}, u32[]{:S(2)}, u32[]{:S(2)}) collective-permute-start(bf16[64,256]{1,0:T(8,128)(2,1)S(1)} %pad_maximum_fusion.19), channel_id=1, source_target_pairs={{0,8},{8,0},{16,24},{24,16},{1,9},{9,1},{17,25},{25,17},{2,10},{10... | collective-permute-start | bytes 98312 | tf_op jit(solution)/shard_map/ppermute | solution.py:895
  166.3 47.3 %collective-permute-start.5 = (bf16[128,64,128]{2,1,0:T(8,128)(2,1)}, bf16[128,64,128]{2,1,0:T(8,128)(2,1)}, u32[]{:S(2)}, u32[]{:S(2)}) collective-permute-start(bf16[128,64,128]{2,1,0:T(8,128)(2,1)} %get-tuple-element.46.ro), channel_id=1, source_target_pairs={{0,8},{8,0},{16,24},{24,16},{1,9},{9,1},{17,25},{25,17},{2,10},{10... | collective-permute-start | bytes 6291464 | tf_op jit(solution)/shard_map/ppermute | solution.py:895
  166.3 47.3 %collective-permute-start.6 = (bf16[128,64,128]{2,1,0:T(8,128)(2,1)}, bf16[128,64,128]{2,1,0:T(8,128)(2,1)}, u32[]{:S(2)}, u32[]{:S(2)}) collective-permute-start(bf16[128,64,128]{2,1,0:T(8,128)(2,1)} %get-tuple-element.47.li), channel_id=1, source_target_pairs={{0,8},{8,0},{16,24},{24,16},{1,9},{9,1},{17,25},{25,17},{2,10},{10... | collective-permute-start | bytes 6291464 | tf_op jit(solution)/shard_map/ppermute | solution.py:895
  166.8 46.8 %collective-permute-start.7 = (bf16[128,64,128]{2,1,0:T(8,128)(2,1)}, bf16[128,64,128]{2,1,0:T(8,128)(2,1)}, u32[]{:S(2)}, u32[]{:S(2)}) collective-permute-start(bf16[128,64,128]{2,1,0:T(8,128)(2,1)} %get-tuple-element.48.ri), channel_id=1, source_target_pairs={{0,8},{8,0},{16,24},{24,16},{1,9},{9,1},{17,25},{25,17},{2,10},{10... | collective-permute-start | bytes 6291464 | tf_op jit(solution)/shard_map/ppermute | solution.py:895
  319.8 13.7 %collective-permute-start.52 = (bf16[4,480,128]{2,1,0:T(8,128)(2,1)S(1)}, bf16[4,480,128]{2,1,0:T(8,128)(2,1)S(1)}, u32[]{:S(2)}, u32[]{:S(2)}) collective-permute-start(bf16[4,480,128]{2,1,0:T(8,128)(2,1)S(1)} %select_convert_fusion.1), channel_id=1, source_target_pairs={{0,4},{4,0},{1,5},{5,1},{2,6},{6,2},{3,7},{7,3},{8,12},{12,8},{9,1... | collective-permute-start | bytes 1474568 | tf_op jit(solution)/shard_map/ppermute | solution.py:1025
  320.5 15.9 %collective-permute-start.38 = (bf16[64,64]{1,0:T(8,128)(2,1)S(1)}, bf16[64,64]{1,0:T(8,128)(2,1)S(1)}, u32[]{:S(2)}, u32[]{:S(2)}) collective-permute-start(bf16[64,64]{1,0:T(8,128)(2,1)S(1)} %get-tuple-element.207), channel_id=1, source_target_pairs={{0,0},{1,1},{2,2},{3,3},{4,8},{5,9},{6,10},{7,11},{8,4},{9,5},{10,... | collective-permute-start | bytes 24584 | tf_op jit(solution)/shard_map/ppermute | solution.py:885
  321.3 15.8 %collective-permute-start.39 = (bf16[64,64]{1,0:T(8,128)(2,1)S(1)}, bf16[64,64]{1,0:T(8,128)(2,1)S(1)}, u32[]{:S(2)}, u32[]{:S(2)}) collective-permute-start(bf16[64,64]{1,0:T(8,128)(2,1)S(1)} %get-tuple-element.210), channel_id=1, source_target_pairs={{0,1},{1,0},{2,3},{3,2},{4,9},{5,8},{6,11},{7,10},{8,5},{9,4},{10,... | collective-permute-start | bytes 24584 | tf_op jit(solution)/shard_map/ppermute | solution.py:885
  321.9 15.8 %collective-permute-start.40 = (bf16[64,64]{1,0:T(8,128)(2,1)S(1)}, bf16[64,64]{1,0:T(8,128)(2,1)S(1)}, u32[]{:S(2)}, u32[]{:S(2)}) collective-permute-start(bf16[64,64]{1,0:T(8,128)(2,1)S(1)} %get-tuple-element.209), channel_id=1, source_target_pairs={{0,2},{1,3},{2,0},{3,1},{4,10},{5,11},{6,8},{7,9},{8,6},{9,7},{10,... | collective-permute-start | bytes 24584 | tf_op jit(solution)/shard_map/ppermute | solution.py:885
  333.7 17.3 %collective-permute-start.53 = (bf16[4,240,128]{2,1,0:T(8,128)(2,1)S(1)}, bf16[4,240,128]{2,1,0:T(8,128)(2,1)S(1)}, u32[]{:S(2)}, u32[]{:S(2)}) collective-permute-start(bf16[4,240,128]{2,1,0:T(8,128)(2,1)S(1)} %select_convert_fusion.2), channel_id=1, source_target_pairs={{0,16},{8,24},{16,0},{24,8},{1,17},{9,25},{17,1},{25,9},{2,18},{10... | collective-permute-start | bytes 737288 | tf_op jit(solution)/shard_map/ppermute | solution.py:1025
  337.6 13.5 %collective-permute-start.12 = (bf16[64,32,128]{2,1,0:T(8,128)(2,1)S(1)}, bf16[64,32,128]{2,1,0:T(8,128)(2,1)S(1)}, u32[]{:S(2)}, u32[]{:S(2)}) collective-permute-start(bf16[64,32,128]{2,1,0:T(8,128)(2,1)S(1)} %copy-done.75), channel_id=1, source_target_pairs={{0,0},{1,1},{2,2},{3,3},{4,8},{5,9},{6,10},{7,11},{8,4},{9,5},{10,... | collective-permute-start | bytes 1572872 | tf_op jit(solution)/shard_map/ppermute | solution.py:885
  344.4 71.4 %collective-permute-start.26 = (bf16[128,64,128]{2,1,0:T(8,128)(2,1)S(1)}, bf16[128,64,128]{2,1,0:T(8,128)(2,1)S(1)}, u32[]{:S(2)}, u32[]{:S(2)}) collective-permute-start(bf16[128,64,128]{2,1,0:T(8,128)(2,1)S(1)} %copy-done.2), channel_id=1, source_target_pairs={{0,8},{8,0},{16,24},{24,16},{1,9},{9,1},{17,25},{25,17},{2,10},{10... | collective-permute-start | bytes 6291464 | tf_op jit(solution)/shard_map/ppermute | solution.py:895
  350.2 65.7 %collective-permute-start.27 = (bf16[128,64,128]{2,1,0:T(8,128)(2,1)S(1)}, bf16[128,64,128]{2,1,0:T(8,128)(2,1)S(1)}, u32[]{:S(2)}, u32[]{:S(2)}) collective-permute-start(bf16[128,64,128]{2,1,0:T(8,128)(2,1)S(1)} %copy-done.8), channel_id=1, source_target_pairs={{0,8},{8,0},{16,24},{24,16},{1,9},{9,1},{17,25},{25,17},{2,10},{10... | collective-permute-start | bytes 6291464 | tf_op jit(solution)/shard_map/ppermute | solution.py:895
  350.9 65.0 %collective-permute-start.28 = (bf16[128,64,128]{2,1,0:T(8,128)(2,1)S(1)}, bf16[128,64,128]{2,1,0:T(8,128)(2,1)S(1)}, u32[]{:S(2)}, u32[]{:S(2)}) collective-permute-start(bf16[128,64,128]{2,1,0:T(8,128)(2,1)S(1)} %copy-done.9), channel_id=1, source_target_pairs={{0,8},{8,0},{16,24},{24,16},{1,9},{9,1},{17,25},{25,17},{2,10},{10... | collective-permute-start | bytes 6291464 | tf_op jit(solution)/shard_map/ppermute | solution.py:895
  360.5 35.1 %collective-permute-start.14 = (bf16[64,32,128]{2,1,0:T(8,128)(2,1)S(1)}, bf16[64,32,128]{2,1,0:T(8,128)(2,1)S(1)}, u32[]{:S(2)}, u32[]{:S(2)}) collective-permute-start(bf16[64,32,128]{2,1,0:T(8,128)(2,1)S(1)} %copy-done.73), channel_id=1, source_target_pairs={{0,2},{1,3},{2,0},{3,1},{4,10},{5,11},{6,8},{7,9},{8,6},{9,7},{10,... | collective-permute-start | bytes 1572872 | tf_op jit(solution)/shard_map/ppermute | solution.py:885
  361.8 45.4 %collective-permute-start.15 = (bf16[64,32,128]{2,1,0:T(8,128)(2,1)S(1)}, bf16[64,32,128]{2,1,0:T(8,128)(2,1)S(1)}, u32[]{:S(2)}, u32[]{:S(2)}) collective-permute-start(bf16[64,32,128]{2,1,0:T(8,128)(2,1)S(1)} %copy-done.72), channel_id=1, source_target_pairs={{0,3},{1,2},{2,1},{3,0},{4,11},{5,10},{6,9},{7,8},{8,7},{9,6},{10,... | collective-permute-start | bytes 1572872 | tf_op jit(solution)/shard_map/ppermute | solution.py:885
  415.8 62.1 %collective-permute-start.59 = (bf16[960,128]{1,0:T(8,128)(2,1)S(1)}, bf16[960,128]{1,0:T(8,128)(2,1)}, u32[]{:S(2)}, u32[]{:S(2)}) collective-permute-start(bf16[960,128]{1,0:T(8,128)(2,1)S(1)} %pad_maximum_fusion.4), channel_id=1, source_target_pairs={{0,8},{8,0},{16,24},{24,16},{1,9},{9,1},{17,25},{25,17},{2,10},{10... | collective-permute-start | bytes 737288 | tf_op jit(solution)/shard_map/ppermute | solution.py:1035
  472.5 45.9 %collective-permute-start.34 = (bf16[64,32,128]{2,1,0:T(8,128)(2,1)}, bf16[64,32,128]{2,1,0:T(8,128)(2,1)}, u32[]{:S(2)}, u32[]{:S(2)}) collective-permute-start(bf16[64,32,128]{2,1,0:T(8,128)(2,1)} %get-tuple-element.60), channel_id=1, source_target_pairs={{0,0},{1,1},{2,2},{3,3},{4,8},{5,9},{6,10},{7,11},{8,4},{9,5},{10,... | collective-permute-start | bytes 1572872 | tf_op jit(solution)/shard_map/ppermute | solution.py:885
  477.9 40.5 %collective-permute-start.35 = (bf16[64,32,128]{2,1,0:T(8,128)(2,1)}, bf16[64,32,128]{2,1,0:T(8,128)(2,1)}, u32[]{:S(2)}, u32[]{:S(2)}) collective-permute-start(bf16[64,32,128]{2,1,0:T(8,128)(2,1)} %get-tuple-element.61), channel_id=1, source_target_pairs={{0,1},{1,0},{2,3},{3,2},{4,9},{5,8},{6,11},{7,10},{8,5},{9,4},{10,... | collective-permute-start | bytes 1572872 | tf_op jit(solution)/shard_map/ppermute | solution.py:885
  499.6 35.6 %collective-permute-start.36 = (bf16[64,32,128]{2,1,0:T(8,128)(2,1)}, bf16[64,32,128]{2,1,0:T(8,128)(2,1)}, u32[]{:S(2)}, u32[]{:S(2)}) collective-permute-start(bf16[64,32,128]{2,1,0:T(8,128)(2,1)} %get-tuple-element.62), channel_id=1, source_target_pairs={{0,2},{1,3},{2,0},{3,1},{4,10},{5,11},{6,8},{7,9},{8,6},{9,7},{10,... | collective-permute-start | bytes 1572872 | tf_op jit(solution)/shard_map/ppermute | solution.py:885
  501.1 46.4 %collective-permute-start.37 = (bf16[64,32,128]{2,1,0:T(8,128)(2,1)}, bf16[64,32,128]{2,1,0:T(8,128)(2,1)}, u32[]{:S(2)}, u32[]{:S(2)}) collective-permute-start(bf16[64,32,128]{2,1,0:T(8,128)(2,1)} %get-tuple-element.63), channel_id=1, source_target_pairs={{0,3},{1,2},{2,1},{3,0},{4,11},{5,10},{6,9},{7,8},{8,7},{9,6},{10,... | collective-permute-start | bytes 1572872 | tf_op jit(solution)/shard_map/ppermute | solution.py:885
  (107 other events, 1954.0 us)
Sparse Core Ops, SparseCore 0:
  19.6 61.6 all-gather.4

commit v2 on v0

--- a/solution.py
+++ b/solution.py
@@ -1,11 +1,16 @@
+import functools
 import math
 
 import jax
 import jax.numpy as jnp
 from jax import lax
+from jax.experimental import pallas as pl
+from jax.experimental.pallas import tpu as pltpu
 from jax.sharding import PartitionSpec as P
 
+f32, bf16 = jnp.float32, jnp.bfloat16
 epsilon = 1e-05
+DP, ROWS, CHAN = "dp", "rows", "chan"
 masked_score = -1000000000.0
 
 
@@ -88,9 +93,9 @@
     batch = pair.shape[0]
     rows_here = pair.shape[1]
     crop_len = pair.shape[3]
-    groups = lax.axis_size("chan")
-    chan_index = lax.axis_index("chan")
-    row_start = lax.axis_index("rows") * rows_here
+    groups = lax.axis_size(CHAN)
+    chan_index = lax.axis_index(CHAN)
+    row_start = lax.axis_index(ROWS) * rows_here
     heads_here = w_bias.shape[1]
     head_dim = w_qkv.shape[2] // heads_here
     scale = 1.0 / math.sqrt(head_dim)
@@ -106,8 +111,8 @@
         return jax.nn.sigmoid(gate) * value * pair_mask
 
     pair_whole, node_whole = (
-        lax.all_gather(pair, "chan", axis=2, tiled=True),
-        lax.all_gather(node, "chan", axis=2, tiled=True),
+        lax.all_gather(pair, CHAN, axis=2, tiled=True),
+        lax.all_gather(node, CHAN, axis=2, tiled=True),
     )
     full_in = pair_whole.astype(jnp.float32)
     node_full = node_whole.astype(jnp.float32)
@@ -130,12 +135,12 @@
         "bin,gna->gbia", normed_node, w_qkv, preferred_element_type=jnp.float32
     ).astype(jnp.bfloat16)
     whole_right_out, whole_right_in, whole_keys, whole_values = (
-        lax.all_gather(right_out, "rows", axis=1, tiled=True),
-        lax.all_gather(right_in, "rows", axis=1, tiled=True),
-        lax.all_gather(qkv[1], "rows", axis=1, tiled=True),
-        lax.all_gather(qkv[2], "rows", axis=1, tiled=True),
-    )
-    left_cols = lax.all_to_all(left_in, "rows", split_axis=3, concat_axis=1, tiled=True)
+        lax.all_gather(right_out, ROWS, axis=1, tiled=True),
+        lax.all_gather(right_in, ROWS, axis=1, tiled=True),
+        lax.all_gather(qkv[1], ROWS, axis=1, tiled=True),
+        lax.all_gather(qkv[2], ROWS, axis=1, tiled=True),
+    )
+    left_cols = lax.all_to_all(left_in, ROWS, split_axis=3, concat_axis=1, tiled=True)
     queries = qkv[0].reshape(batch, rows_here, heads_here, head_dim)
     keys = whole_keys.reshape(batch, crop_len, heads_here, head_dim)
     values = whole_values.reshape(batch, crop_len, heads_here, head_dim)
@@ -156,14 +161,14 @@
         "bkhi,bkhj->bihj", left_cols, whole_right_in, preferred_element_type=jnp.float32
     )
     tri_full_out, tri_full_in, attn_whole = (
-        lax.all_gather(tri_out.astype(jnp.bfloat16), "chan", axis=2, tiled=True).astype(
+        lax.all_gather(tri_out.astype(jnp.bfloat16), CHAN, axis=2, tiled=True).astype(
             tri_out.dtype
         ),
-        lax.all_gather(tri_in.astype(jnp.bfloat16), "chan", axis=2, tiled=True).astype(
+        lax.all_gather(tri_in.astype(jnp.bfloat16), CHAN, axis=2, tiled=True).astype(
             tri_in.dtype
         ),
         lax.all_gather(
-            attn.astype(jnp.float32).astype(jnp.bfloat16), "chan", axis=2, tiled=True
+            attn.astype(jnp.float32).astype(jnp.bfloat16), CHAN, axis=2, tiled=True
         ).astype(jnp.float32),
     )
     normed_out = normed(tri_full_out, gain_tri[0]).astype(jnp.bfloat16)
@@ -181,10 +186,10 @@
         "bia,an->bin", attn_low, w_attn_out, preferred_element_type=jnp.float32
     )
     full_mid, node_full_mid = (
-        lax.all_gather(stream_mid.astype(jnp.bfloat16), "chan", axis=2, tiled=True).astype(
+        lax.all_gather(stream_mid.astype(jnp.bfloat16), CHAN, axis=2, tiled=True).astype(
             stream_mid.dtype
         ),
-        lax.all_gather(node_mid.astype(jnp.bfloat16), "chan", axis=2, tiled=True).astype(
+        lax.all_gather(node_mid.astype(jnp.bfloat16), CHAN, axis=2, tiled=True).astype(
             node_mid.dtype
         ),
     )
@@ -208,17 +213,17 @@
     )
     pair_sum, node_sum = (
         lax.psum_scatter(
-            out_terms.astype(jnp.bfloat16), "chan", scatter_dimension=2, tiled=True
-        ).astype(jnp.float32),
-        lax.psum_scatter(
-            node_terms.astype(jnp.bfloat16), "chan", scatter_dimension=2, tiled=True
+            out_terms.astype(jnp.bfloat16), CHAN, scatter_dimension=2, tiled=True
+        ).astype(jnp.float32),
+        lax.psum_scatter(
+            node_terms.astype(jnp.bfloat16), CHAN, scatter_dimension=2, tiled=True
         ).astype(jnp.float32),
     )
     stream_out = stream_mid + pair_sum
     node_out = node_mid + node_sum
     cot_full, node_cot_full = (
-        lax.all_gather(pair_cot, "chan", axis=2, tiled=True),
-        lax.all_gather(node_cot, "chan", axis=2, tiled=True),
+        lax.all_gather(pair_cot, CHAN, axis=2, tiled=True),
+        lax.all_gather(node_cot, CHAN, axis=2, tiled=True),
     )
     grad_trans_out = jnp.einsum(
         "bifj,bicj->fc", hidden_low, cot_full, preferred_element_type=jnp.float32
@@ -250,16 +255,16 @@
     node_mid_terms = stat_terms(node_full_mid, gain_node_trans, grad_normed_node_mid, groups)
     mid_here, mid_totals, node_mid_here, node_mid_totals = (
         lax.psum_scatter(
-            grad_normed_mid.astype(jnp.bfloat16), "chan", scatter_dimension=2, tiled=True
-        ).astype(jnp.float32),
-        lax.psum_scatter(
-            mid_terms.astype(jnp.bfloat16), "chan", scatter_dimension=2, tiled=True
-        ).astype(jnp.float32),
-        lax.psum_scatter(
-            grad_normed_node_mid.astype(jnp.bfloat16), "chan", scatter_dimension=2, tiled=True
-        ).astype(jnp.float32),
-        lax.psum_scatter(
-            node_mid_terms.astype(jnp.bfloat16), "chan", scatter_dimension=2, tiled=True
+            grad_normed_mid.astype(jnp.bfloat16), CHAN, scatter_dimension=2, tiled=True
+        ).astype(jnp.float32),
+        lax.psum_scatter(
+            mid_terms.astype(jnp.bfloat16), CHAN, scatter_dimension=2, tiled=True
+        ).astype(jnp.float32),
+        lax.psum_scatter(
+            grad_normed_node_mid.astype(jnp.bfloat16), CHAN, scatter_dimension=2, tiled=True
+        ).astype(jnp.float32),
+        lax.psum_scatter(
+            node_mid_terms.astype(jnp.bfloat16), CHAN, scatter_dimension=2, tiled=True
         ).astype(jnp.float32),
     )
     mid_extra, grad_gain_trans = norm_finish(full_mid, gain_trans, mid_here, mid_totals, chan_index)
@@ -292,19 +297,19 @@
     )
     out_here, out_totals, inc_here, inc_totals, attn_here = (
         lax.psum_scatter(
-            grad_tri_normed[0].astype(jnp.bfloat16), "chan", scatter_dimension=2, tiled=True
-        ).astype(jnp.float32),
-        lax.psum_scatter(
-            out_stats.astype(jnp.bfloat16), "chan", scatter_dimension=2, tiled=True
-        ).astype(jnp.float32),
-        lax.psum_scatter(
-            grad_tri_normed[1].astype(jnp.bfloat16), "chan", scatter_dimension=2, tiled=True
-        ).astype(jnp.float32),
-        lax.psum_scatter(
-            inc_stats.astype(jnp.bfloat16), "chan", scatter_dimension=2, tiled=True
-        ).astype(jnp.float32),
-        lax.psum_scatter(
-            attn_terms.astype(jnp.bfloat16), "chan", scatter_dimension=2, tiled=True
+            grad_tri_normed[0].astype(jnp.bfloat16), CHAN, scatter_dimension=2, tiled=True
+        ).astype(jnp.float32),
+        lax.psum_scatter(
+            out_stats.astype(jnp.bfloat16), CHAN, scatter_dimension=2, tiled=True
+        ).astype(jnp.float32),
+        lax.psum_scatter(
+            grad_tri_normed[1].astype(jnp.bfloat16), CHAN, scatter_dimension=2, tiled=True
+        ).astype(jnp.float32),
+        lax.psum_scatter(
+            inc_stats.astype(jnp.bfloat16), CHAN, scatter_dimension=2, tiled=True
+        ).astype(jnp.float32),
+        lax.psum_scatter(
+            attn_terms.astype(jnp.bfloat16), CHAN, scatter_dimension=2, tiled=True
         ).astype(jnp.float32),
     )
     grad_tri_a, gain_grad_out = norm_finish(
@@ -344,16 +349,16 @@
     )
     grad_right_out, key_grads, value_grads = (
         lax.psum_scatter(
-            right_terms.astype(jnp.bfloat16), "rows", scatter_dimension=1, tiled=True
-        ).astype(jnp.float32),
-        lax.psum_scatter(
-            key_terms.astype(jnp.bfloat16), "rows", scatter_dimension=1, tiled=True
-        ).astype(jnp.float32),
-        lax.psum_scatter(
-            value_terms.astype(jnp.bfloat16), "rows", scatter_dimension=1, tiled=True
-        ).astype(jnp.float32),
-    )
-    whole_grad_in = lax.all_gather(grad_inc_low, "rows", axis=1, tiled=True)
+            right_terms.astype(jnp.bfloat16), ROWS, scatter_dimension=1, tiled=True
+        ).astype(jnp.float32),
+        lax.psum_scatter(
+            key_terms.astype(jnp.bfloat16), ROWS, scatter_dimension=1, tiled=True
+        ).astype(jnp.float32),
+        lax.psum_scatter(
+            value_terms.astype(jnp.bfloat16), ROWS, scatter_dimension=1, tiled=True
+        ).astype(jnp.float32),
+    )
+    whole_grad_in = lax.all_gather(grad_inc_low, ROWS, axis=1, tiled=True)
     grad_left_in = jnp.einsum(
         "bihj,bkhj->bkhi", whole_grad_in, right_in, preferred_element_type=jnp.float32
     )
@@ -402,16 +407,16 @@
     node_in_terms = stat_terms(node_full, gain_node, grad_normed_node, groups)
     in_here, in_totals, node_in_here, node_in_totals = (
         lax.psum_scatter(
-            grad_normed_in.astype(jnp.bfloat16), "chan", scatter_dimension=2, tiled=True
-        ).astype(jnp.float32),
-        lax.psum_scatter(
-            in_terms.astype(jnp.bfloat16), "chan", scatter_dimension=2, tiled=True
-        ).astype(jnp.float32),
-        lax.psum_scatter(
-            grad_normed_node.astype(jnp.bfloat16), "chan", scatter_dimension=2, tiled=True
-        ).astype(jnp.float32),
-        lax.psum_scatter(
-            node_in_terms.astype(jnp.bfloat16), "chan", scatter_dimension=2, tiled=True
+            grad_normed_in.astype(jnp.bfloat16), CHAN, scatter_dimension=2, tiled=True
+        ).astype(jnp.float32),
+        lax.psum_scatter(
+            in_terms.astype(jnp.bfloat16), CHAN, scatter_dimension=2, tiled=True
+        ).astype(jnp.float32),
+        lax.psum_scatter(
+            grad_normed_node.astype(jnp.bfloat16), CHAN, scatter_dimension=2, tiled=True
+        ).astype(jnp.float32),
+        lax.psum_scatter(
+            node_in_terms.astype(jnp.bfloat16), CHAN, scatter_dimension=2, tiled=True
         ).astype(jnp.float32),
     )
     in_extra, grad_gain_pair = norm_finish(full_in, gain_pair, in_here, in_totals, chan_index)
@@ -438,7 +443,7 @@
             grad_node_in_w,
             grad_node_out_w,
         ),
-        ("dp", "rows"),
+        (DP, ROWS),
     )
     return (
         stream_out.astype(jnp.bfloat16),
@@ -463,49 +468,1229 @@
     )
 
 
+ORDER = (3, 2, 0, 1)
+IN_LEFT, IN_RIGHT, OUT_RIGHT, OUT_LEFT = range(4)
+
+group = 8
+
+
+def dot(a, b, ca=1, cb=0):
+    return lax.dot_general(a, b, (((ca,), (cb,)), ((), ())), preferred_element_type=f32)
+
+
+def sigmoid(v):
+    return 0.5 * jnp.tanh(0.5 * v) + 0.5
+
+
+def sub_norm(full):
+    mean = jnp.mean(full, axis=0, keepdims=True)
+    centered = full - mean
+    inverse = lax.rsqrt(jnp.mean(centered * centered, axis=0, keepdims=True) + epsilon)
+    return centered * inverse, inverse
+
+
+def sub_norm_back(gain, scaled, inverse, grad):
+    weighted = gain * grad
+    first = jnp.mean(weighted, axis=0, keepdims=True)
+    second = jnp.mean(weighted * scaled, axis=0, keepdims=True)
+    return inverse * (weighted - first - scaled * second)
+
+
+def gelu_both(value):
+    cdf = 0.5 * (1.0 + lax.erf(value * (0.5**0.5)))
+    density = jnp.exp(-0.5 * value * value) * (1.0 / math.sqrt(2.0 * math.pi))
+    return value * cdf, cdf + value * density
+
+
+def lane_sums(value):
+    value = sum(value[:, at : at + 128] for at in range(0, value.shape[1], 128))
+    ones = jnp.ones((8, value.shape[1]), f32)
+    sums = lax.dot_general(
+        ones,
+        value,
+        (((1,), (1,)), ((), ())),
+        precision=lax.Precision.HIGHEST,
+        preferred_element_type=f32,
+    )
+    return sums[:1]
+
+
+def place_spec():
+    return pl.BlockSpec(memory_space=pltpu.SMEM)
+
+
+def whole_spec(a):
+    zeros = (0,) * len(a.shape)
+    return pl.BlockSpec(a.shape, lambda s: zeros)
+
+
+def in_hbm(shape, dtype):
+    return pltpu.HBM(shape, dtype)
+
+
+def held(arrays):
+    return [pltpu.with_memory_space_constraint(a, pltpu.HBM) for a in arrays]
+
+
+def params(mib):
+    return pltpu.CompilerParams(vmem_limit_bytes=mib * 2**20)
+
+
+quick = pl.CostEstimate(flops=1, bytes_accessed=1, transcendentals=0)
+
+
+def pack_kernel(first_row, rows, live_rows, place_ref, *refs):
+    z, part = place_ref[0], 2 * place_ref[2] + place_ref[1]
+    sems = refs[-1]
+    outs = refs[-7:-3] if live_rows else refs[-5:-1]
+    more = outs[0].shape[0] - rows
+    copies = []
+    for m in range(4):
+        rows_of = refs[0].at[lax.bitwise_xor(z, m), pl.ds(first_row, rows)]
+        copies.append(pltpu.make_async_copy(rows_of, outs[m].at[pl.ds(0, rows)], sems.at[m]))
+    if more and not live_rows:
+        for m in range(4):
+            rows_of = refs[1].at[pl.ds(part * more, more)]
+            copies.append(pltpu.make_async_copy(rows_of, outs[m].at[pl.ds(rows, more)], sems.at[4 + m]))
+    for copy in copies:
+        copy.start()
+    if live_rows:
+        lengths, present, node, node_cot, tri_in, gate, bias, tri_out, trans_in, trans_out = refs[1:11]
+        extra, weights = refs[-3:-1]
+        quarter, width = extra.shape[2:]
+        position = lax.broadcasted_iota(jnp.int32, (1, width), 1)
+        for crop in range(4):
+            for n, ref in enumerate((node, node_cot)):
+                value = ref[crop].astype(f32)
+                extra[crop, 1 + n] = jnp.concatenate([value[:quarter], value[quarter:]], axis=1).astype(bf16)
+            there = jnp.where(position < lengths[crop], present[crop : crop + 1], 0).astype(f32)
+            extra[crop, 0] = jnp.broadcast_to(there, (quarter, width)).astype(bf16)
+        parts = [tri_in[...], gate[...]]
+        low = bias[...].astype(f32)
+        parts.append(jnp.concatenate([low, jnp.zeros((32 - low.shape[0], width), f32)], axis=0).astype(bf16))
+        parts += [tri_out[...], trans_in[...].astype(f32).T.astype(bf16), trans_out[...]]
+        count = sum(part.shape[0] for part in parts)
+        parts.append(jnp.zeros((quarter * weights.shape[0] - count, width), bf16))
+        weights[...] = jnp.concatenate(parts, axis=0).reshape(weights.shape)
+        for m in range(4):
+            outs[m][rows : rows + 3] = extra[lax.bitwise_xor(z, m)]
+            outs[m][rows + 3 :] = weights[pl.ds(place_ref[2] * (more - 3), more - 3)]
+    for copy in copies:
+        copy.wait()
+
+
+def pack(place, source, first_row, rows, weights=None, first=None):
+    _, _, quarter, width = source.shape
+    vmem = pl.BlockSpec(memory_space=pltpu.VMEM)
+    operands, specs, scratch, more = [place, *held([source])], [place_spec(), any_spec()], [], 0
+    if first is not None:
+        count = sum(a.shape[0] for a in first[4:]) + 32 - first[6].shape[0]
+        count = -(-count // (2 * quarter)) * 2
+        operands += first[:1] + held(first[1:])
+        specs += [place_spec()] + [vmem] * (len(first) - 1)
+        scratch = [pltpu.VMEM((4, 3, quarter, width), bf16), pltpu.VMEM((count, quarter, width), bf16)]
+        more = 3 + count // 2
+    elif weights is not None:
+        operands += held([weights])
+        specs.append(any_spec())
+        more = weights.shape[0] // 4
+    return pl.pallas_call(
+        functools.partial(pack_kernel, first_row, rows, first is not None),
+        in_specs=specs,
+        out_specs=[vmem] * 4,
+        out_shape=[in_hbm((rows + more, quarter, width), bf16)] * 4,
+        scratch_shapes=scratch + [pltpu.SemaphoreType.DMA((8,))],
+        compiler_params=params(24),
+        cost_estimate=quick,
+        name="pack",
+    )(*operands)
+
+
+def project_kernel(
+    place_ref, p0, p1, p2, p3, wall_ref, mask_ref, gain_ref, tri_ref, norm_ref, pair_ref, bias_ref, pc, w_s, wb_s, bs, *kept_s
+):
+    pieces = (p0, p1, p2, p3)
+    rows, quarter, width = p0.shape
+    chans = 4 * quarter
+    z = place_ref[0]
+    gain = jnp.concatenate([gain_ref[...]] * group, axis=1)
+    heads = bias_ref.shape[0]
+    tri_rows = 8 * quarter
+
+    @pl.when(pl.program_id(0) == 0)
+    def _():
+        for g in range(4):
+            w_s[g * tri_rows : (g + 1) * tri_rows] = wall_ref[lax.bitwise_xor(z, g), :tri_rows]
+            wb_s[g * 16 : (g + 1) * 16] = wall_ref[lax.bitwise_xor(z, g), 10 * quarter : 10 * quarter + 16]
+
+    for m in range(4):
+        pc[lax.bitwise_xor(z, m)] = pieces[m][...]
+
+    @pl.loop(0, rows // group)
+    def _(step):
+        first = step * group
+
+        def wide(get):
+            return jnp.concatenate([get(first + n) for n in range(group)], axis=1)
+
+        rows_in = [jnp.concatenate([pc[q, first + n] for q in range(4)], axis=0) for n in range(group)]
+        for n in range(group):
+            pair_ref[first + n] = rows_in[n]
+        scaled, _ = sub_norm(jnp.concatenate(rows_in, axis=1).astype(f32))
+        low = (scaled * gain).astype(bf16)
+        for n in range(group):
+            norm_ref[first + n] = low[:, n * width : (n + 1) * width]
+        mask = wide(lambda r: mask_ref[pl.ds(r, 1), :])
+        bias = dot(wb_s[...], low)
+        for n in range(group):
+            for g in range(4):
+                at = (first + n) * heads + g * (heads // 4)
+                bs[pl.ds(at, heads // 4), :] = bias[g * 16 : g * 16 + heads // 4, n * width : (n + 1) * width]
+        for g in range(4):
+            proj = dot(w_s[g * tri_rows : (g + 1) * tri_rows], low)
+            for k in range(4):
+                gate = proj[(2 * k) * quarter : (2 * k + 1) * quarter]
+                value = proj[(2 * k + 1) * quarter : (2 * k + 2) * quarter]
+                kept = sigmoid(gate) * value * mask
+                for n in range(group):
+                    at = (first + n) * (chans + 1) + g * quarter
+                    kept_s[ORDER[k]][pl.ds(at, quarter), :] = kept[:, n * width : (n + 1) * width]
+
+    @pl.loop(0, chans, unroll=8)
+    def _(h):
+        for k in range(4):
+            tri_ref[k, h] = kept_s[k][pl.ds(h, rows, stride=chans + 1), :].astype(bf16)
+
+    for h in range(heads):
+        bias_ref[h] = bs[pl.ds(h, rows, stride=heads), :]
+
+
+def any_spec():
+    return pl.BlockSpec(memory_space=pl.ANY)
+
+
+def project(place, pieces, wall, mask_rows, gain, heads, rows, first_row, step_rows=16):
+    _, quarter, width = pieces[0].shape
+    chans = 4 * quarter
+    start = first_row // step_rows
+    row_spec = pl.BlockSpec((step_rows, chans, width), lambda i: (i, 0, 0))
+    pair = in_hbm((rows, chans, width), bf16)
+    return pl.pallas_call(
+        project_kernel,
+        grid=(rows // step_rows,),
+        in_specs=[place_spec()]
+        + [pl.BlockSpec((step_rows, quarter, width), lambda i: (i, 0, 0))] * 4
+        + [whole_spec(wall), pl.BlockSpec((step_rows, width), lambda i: (i + start, 0)), whole_spec(gain)],
+        out_specs=[
+            pl.BlockSpec((4, chans, step_rows, width), lambda i: (0, 0, i, 0)),
+            row_spec,
+            row_spec,
+            pl.BlockSpec((heads, step_rows, width), lambda i: (0, i, 0)),
+        ],
+        out_shape=[
+            in_hbm((4, chans, rows, width), bf16),
+            pair,
+            pair,
+            jax.ShapeDtypeStruct((heads, rows, width), f32),
+        ],
+        scratch_shapes=[
+            pltpu.VMEM((4, step_rows, quarter, width), bf16),
+            pltpu.VMEM((8 * chans, chans), bf16),
+            pltpu.VMEM((64, chans), bf16),
+            pltpu.VMEM((step_rows * heads, width), f32),
+        ]
+        + [pltpu.VMEM((step_rows * (chans + 8), width), f32)] * 4,
+        compiler_params=params(40),
+        cost_estimate=quick,
+        name="project",
+    )(place, *pieces, wall, mask_rows, gain)
+
+
+def in_core_order(core, mine, far):
+    first = core == 0
+    blocks = [jnp.where(first, a, b) for a, b in zip(mine, far)]
+    return jnp.concatenate(blocks + [jnp.where(first, b, a) for a, b in zip(mine, far)], axis=0)
+
+
+def tri_forward_kernel(count, place_ref, *refs):
+    core = place_ref[1]
+    mine, far, out_ref = refs[:count], refs[count : 2 * count], refs[-1]
+    rows = out_ref.shape[2]
+
+    @pl.loop(0, out_ref.shape[1], unroll=4)
+    def _(h):
+        left = jnp.concatenate([t[OUT_LEFT, h] for t in mine], axis=0)
+        right = in_core_order(core, [t[OUT_RIGHT, h] for t in mine], [t[OUT_RIGHT, h] for t in far])
+        out_ref[0, h] = dot(left, right, 1, 1).astype(bf16)
+        left = jnp.concatenate([t[IN_LEFT, h] for t in mine + far], axis=0)
+        right = jnp.concatenate([t[IN_RIGHT, h] for t in mine + far], axis=0)
+        both = dot(left, right, 0, 0)
+        out_ref[1, h] = jnp.where(core == 0, both[:rows], both[rows:]).astype(bf16)
+
+
+def tri_forward(place, mine, far, step_h=16):
+    _, chans, rows, width = mine[0].shape
+    rows = rows * len(mine)
+    spec = pl.BlockSpec((4, step_h) + mine[0].shape[2:], lambda s: (0, s, 0, 0))
+    far_spec = pl.BlockSpec((3, step_h) + mine[0].shape[2:], lambda s: (0, s, 0, 0))
+    return pl.pallas_call(
+        functools.partial(tri_forward_kernel, len(mine)),
+        grid=(chans // step_h,),
+        in_specs=[place_spec()] + [spec] * len(mine) + [far_spec] * len(mine),
+        out_specs=pl.BlockSpec((2, step_h, rows, width), lambda s: (0, s, 0, 0)),
+        out_shape=in_hbm((2, chans, rows, width), bf16),
+        compiler_params=params(40),
+        cost_estimate=quick,
+        name="tri_forward",
+    )(place, *held(mine), *far)
+
+
+def middle_kernel(
+    fresh, place_ref, tri_ref, pair_ref, norm_ref, c0, c1, c2, c3, gain_tri_ref, gain_trans_ref, wall_ref, rest_ref, prev_ref,
+    p0, p1, p2, p3, mid_ref, gate_ref, gtri_ref, gw_out_ref,
+    gw_ref, tri_s0, tri_s1, wg_s, wto_s, wti_s, wout_s, wout_t, wti_t, wto_t, gg_trans_s, gg_tri_s,
+    cot_s, pc, po, tn0, tn1, nm, hid, gp, gb0, gb1, gs0, gs1,
+):
+    z = place_ref[0]
+    step = pl.program_id(0)
+    rows, chans, width = pair_ref.shape
+    quarter = chans // 4
+    cots, outs = (c0, c1, c2, c3), (p0, p1, p2, p3)
+    tris, tns, gbs, gss = (tri_s0, tri_s1), (tn0, tn1), (gb0, gb1), (gs0, gs1)
+    gains_at = 2 * quarter + 2 * chans
+
+    @pl.when(step == 0)
+    def _():
+        for g in range(4):
+            for d in range(2):
+                wg_s[d * chans + g * quarter : d * chans + (g + 1) * quarter] = wall_ref[
+                    lax.bitwise_xor(z, g), (8 + d) * quarter : (9 + d) * quarter
+                ]
+                wto_s[d, g * quarter : (g + 1) * quarter] = rest_ref[lax.bitwise_xor(z, g), d * quarter : (d + 1) * quarter]
+            wti_s[g * chans : (g + 1) * chans] = rest_ref[lax.bitwise_xor(z, g), 2 * quarter : 2 * quarter + chans]
+            wout_s[g * chans : (g + 1) * chans] = rest_ref[lax.bitwise_xor(z, g), 2 * quarter + chans : gains_at]
+        for f in range(4):
+            block = slice(f * chans, (f + 1) * chans)
+            wout_t[:, block] = wout_s[block].astype(f32).T.astype(bf16)
+            wti_t[:, block] = wti_s[block].astype(f32).T.astype(bf16)
+        for d in range(2):
+            wto_t[d] = wto_s[d].astype(f32).T.astype(bf16)
+        gw_ref[...] = jnp.zeros_like(gw_ref) if fresh else prev_ref[...]
+        gg_trans_s[...] = jnp.zeros_like(gg_trans_s)
+        gg_tri_s[...] = jnp.zeros_like(gg_tri_s)
+
+    @pl.loop(0, chans, unroll=8)
+    def _(h):
+        for d in range(2):
+            tris[d][pl.ds(h * (rows + 1), rows), :] = tri_ref[d, h].astype(f32)
+
+    gain_trans = jnp.concatenate([gain_trans_ref[...]] * group, axis=1)
+    gain_tri = [jnp.concatenate([gain_tri_ref[d]] * group, axis=1) for d in range(2)]
+
+    for m in range(4):
+        pc[lax.bitwise_xor(z, m)] = cots[m][...]
+
+    @pl.loop(0, rows // group)
+    def _(s2):
+        first = s2 * group
+        lanes = pl.ds(pl.multiple_of(first * width, group * width), group * width)
+
+        def wide(get):
+            return jnp.concatenate([get(first + n) for n in range(group)], axis=1)
+
+        def cut(value, n):
+            return value[:, n * width : (n + 1) * width]
+
+        inner = wide(lambda r: norm_ref[r])
+        gate = sigmoid(dot(wg_s[...], inner))
+        total = wide(lambda r: pair_ref[r]).astype(f32)
+        kept = []
+        for d in range(2):
+            tri = wide(lambda r: tris[d][pl.ds(r, chans, stride=rows + 1), :])
+            scaled, inverse = sub_norm(tri)
+            low = (scaled * gain_tri[d]).astype(bf16)
+            tns[d][:, lanes] = low
+            branch = dot(wto_s[d], low)
+            total = total + gate[d * chans : (d + 1) * chans] * branch
+            kept.append((scaled, inverse, branch))
+        scaled, inverse = sub_norm(total)
+        low = (scaled * gain_trans).astype(bf16)
+        nm[:, lanes] = low
+        cot = wide(lambda r: jnp.concatenate([pc[q, r] for q in range(4)], axis=0))
+        cot_s[:, lanes] = cot
+        acts, backs = [], []
+        for f in range(4):
+            block = slice(f * chans, (f + 1) * chans)
+            act, slope = gelu_both(dot(wti_s[block], low))
+            acts.append(act.astype(bf16))
+            backs.append((dot(wout_s[block], cot) * slope).astype(bf16))
+            hid[block, lanes] = acts[-1]
+            gp[block, lanes] = backs[-1]
+        out = (total + dot(wout_t[...], jnp.concatenate(acts, axis=0))).astype(bf16)
+        for n in range(group):
+            for q in range(4):
+                po[q, first + n] = cut(out[q * quarter : (q + 1) * quarter], n)
+        back = dot(wti_t[...], jnp.concatenate(backs, axis=0))
+        gg_trans_s[...] += back * scaled
+        grad = cot.astype(f32) + sub_norm_back(gain_trans, scaled, inverse, back)
+        for n in range(group):
+            mid_ref[first + n] = cut(grad, n).astype(bf16)
+        for d in range(2):
+            scaled, inverse, branch = kept[d]
+            sig = gate[d * chans : (d + 1) * chans]
+            grad_branch = sig * grad
+            grad_gate = (grad_branch * branch * (1.0 - sig)).astype(bf16)
+            grad_branch = grad_branch.astype(bf16)
+            for n in range(group):
+                gate_ref[first + n, d * chans : (d + 1) * chans] = cut(grad_gate, n)
+            gbs[d][:, lanes] = grad_branch
+            back = dot(wto_t[d], grad_branch)
+            gg_tri_s[d] += back * scaled
+            out = sub_norm_back(gain_tri[d], scaled, inverse, back)
+            for n in range(group):
+                gss[d][pl.ds(first + n, chans, stride=rows + 1), :] = cut(out, n)
+
+    for m in range(4):
+        outs[m][...] = po[lax.bitwise_xor(z, m)]
+    gw_out = dot(hid[...], cot_s[...], 1, 1)
+    gw_in = dot(gp[...], nm[...], 1, 1)
+    for g in range(4):
+        at = 2 * quarter
+        gw_ref[g, at : at + chans] += gw_in[g * chans : (g + 1) * chans]
+        gw_ref[g, at + chans : at + 2 * chans] += gw_out[g * chans : (g + 1) * chans]
+    for d in range(2):
+        gw_tri = dot(gbs[d][...], tns[d][...], 1, 1)
+        for g in range(4):
+            gw_ref[g, d * quarter : (d + 1) * quarter] += gw_tri[g * quarter : (g + 1) * quarter]
+
+        @pl.loop(0, chans, unroll=8)
+        def _(h):
+            gtri_ref[d, h] = gss[d][pl.ds(h * (rows + 1), rows), :].astype(bf16)
+
+    @pl.when(step == pl.num_programs(0) - 1)
+    def _():
+        for n, total in enumerate((gg_trans_s[...], gg_tri_s[0], gg_tri_s[1])):
+            row = lane_sums(total)
+            for g in range(4):
+                gw_ref[g, gains_at + n : gains_at + n + 1] += row
+        gw_out_ref[...] = gw_ref[...].astype(gw_out_ref.dtype)
+
+
+def middle(place, tri, first_row, pair, norm, cots, gain_tri, gain_trans, wall, rest, prev, step_rows=16):
+    rows, chans, width = pair.shape
+    hidden, quarter = 4 * chans, chans // 4
+    fresh = prev is None
+    sums = in_hbm((4, 2 * quarter + 2 * chans + 16, chans), f32 if fresh else bf16)
+    start = first_row // step_rows
+    row_spec = pl.BlockSpec((step_rows, chans, width), lambda s: (s, 0, 0))
+    piece_spec = pl.BlockSpec((step_rows, quarter, width), lambda s: (s, 0, 0))
+    piece = in_hbm((rows, quarter, width), bf16)
+    gate = in_hbm((rows, 2 * chans, width), bf16)
+    lanes = step_rows * width
+    operands = [place, *held([tri, pair, norm]), *cots, gain_tri, gain_trans, wall, rest]
+    operands.append(gain_tri if fresh else prev)
+    return pl.pallas_call(
+        functools.partial(middle_kernel, fresh),
+        grid=(rows // step_rows,),
+        in_specs=[place_spec(), pl.BlockSpec((2, chans, step_rows, width), lambda s: (0, 0, s + start, 0)), row_spec, row_spec]
+        + [piece_spec] * 4
+        + [whole_spec(a) for a in operands[8:]],
+        out_specs=[piece_spec] * 4
+        + [
+            row_spec,
+            pl.BlockSpec((step_rows, 2 * chans, width), lambda s: (s, 0, 0)),
+            pl.BlockSpec((2, chans, step_rows, width), lambda s: (0, 0, s, 0)),
+            whole_spec(sums),
+        ],
+        out_shape=[piece] * 4
+        + [
+            in_hbm((rows, chans, width), bf16),
+            gate,
+            jax.ShapeDtypeStruct((2, chans, rows, width), bf16),
+            sums,
+        ],
+        scratch_shapes=[pltpu.VMEM(sums.shape, f32)]
+        + [pltpu.VMEM((chans * (step_rows + 1), width), f32)] * 2
+        + [pltpu.VMEM((2 * chans, chans), bf16), pltpu.VMEM((2, chans, chans), bf16)]
+        + [pltpu.VMEM((hidden, chans), bf16)] * 2
+        + [pltpu.VMEM((chans, hidden), bf16)] * 2
+        + [
+            pltpu.VMEM((2, chans, chans), bf16),
+            pltpu.VMEM((chans, group * width), f32),
+            pltpu.VMEM((2, chans, group * width), f32),
+            pltpu.VMEM((chans, lanes), bf16),
+            pltpu.VMEM((4, step_rows, quarter, width), bf16),
+            pltpu.VMEM((4, step_rows, quarter, width), bf16),
+        ]
+        + [pltpu.VMEM((chans, lanes), bf16)] * 3
+        + [pltpu.VMEM((hidden, lanes), bf16)] * 2
+        + [pltpu.VMEM((chans, lanes), bf16)] * 2
+        + [pltpu.VMEM((chans * (step_rows + 1), width), f32)] * 2,
+        compiler_params=params(56),
+        cost_estimate=quick,
+        name="middle",
+    )(*operands)
+
+
+def tri_backward_kernel(count, place_ref, *refs):
+    core = place_ref[1]
+    mine, far, gmine, gfar = (refs[n * count : (n + 1) * count] for n in range(4))
+    out_ref = refs[-1]
+    rows = out_ref.shape[2]
+
+    def joined(a, k, h):
+        return jnp.concatenate([t[k, h] for t in a], axis=0)
+
+    @pl.loop(0, out_ref.shape[1], unroll=4)
+    def _(h):
+        right = in_core_order(core, [t[OUT_RIGHT, h] for t in mine], [t[0, h] for t in far])
+        out_ref[0, h] = dot(joined(gmine, 0, h), right).astype(bf16)
+        left = jnp.concatenate([t[OUT_LEFT, h] for t in mine] + [t[1, h] for t in far], axis=0)
+        both = dot(joined(gmine + gfar, 0, h), left, 0, 0)
+        out_ref[1, h] = jnp.where(core == 0, both[:rows], both[rows:]).astype(bf16)
+        grad = in_core_order(core, [t[1, h] for t in gmine], [t[1, h] for t in gfar])
+        out_ref[2, h] = dot(joined(mine, IN_RIGHT, h), grad, 1, 1).astype(bf16)
+        out_ref[3, h] = dot(joined(mine, IN_LEFT, h), grad).astype(bf16)
+
+
+def tri_backward(place, mine, far, gmine, gfar, step_h=16):
+    _, chans, rows, width = mine[0].shape
+    total = rows * len(mine)
+    spec = pl.BlockSpec((4, step_h, rows, width), lambda s: (0, s, 0, 0))
+    far_spec = pl.BlockSpec((2, step_h, rows, width), lambda s: (1, s, 0, 0))
+    gspec = pl.BlockSpec((2, step_h, rows, width), lambda s: (0, s, 0, 0))
+    operands = [place, *held(mine), *held(far), *gmine, *gfar]
+    return pl.pallas_call(
+        functools.partial(tri_backward_kernel, len(mine)),
+        grid=(chans // step_h,),
+        in_specs=[place_spec()] + [spec] * len(mine) + [far_spec] * len(mine) + [gspec] * (2 * len(mine)),
+        out_specs=pl.BlockSpec((4, step_h, total, width), lambda s: (0, s, 0, 0)),
+        out_shape=in_hbm((4, chans, total, width), bf16),
+        compiler_params=params(40),
+        cost_estimate=quick,
+        name="tri_backward",
+    )(*operands)
+
+
+def finish_kernel(
+    i_steps, fresh, place_ref, sum_ref, pair_ref, norm_ref, mid_ref, gate_ref, score_ref, mask_ref, gain_ref, wall_ref, prev_ref, extra_ref,
+    p0, p1, p2, p3, gw_out_ref,
+    gw_ref, s0, s1, s2_, s3, wall_t, w_s, gall, nb, po, sc_s, gg_s,
+):
+    z = place_ref[0]
+    step = pl.program_id(0)
+    rows, chans, width = pair_ref.shape
+    quarter = chans // 4
+    sums, outs = (s0, s1, s2_, s3), (p0, p1, p2, p3)
+    block_rows = wall_ref.shape[1]
+    packed = 4 * block_rows
+    heads = score_ref.shape[1]
+    here = heads // 4
+
+    @pl.when(step == 0)
+    def _():
+        for g in range(4):
+            gall[g * block_rows : (g + 1) * block_rows, :chans] = wall_ref[lax.bitwise_xor(z, g)]
+            w_s[g * 8 * quarter : (g + 1) * 8 * quarter] = wall_ref[lax.bitwise_xor(z, g), : 8 * quarter]
+        for f in range(0, packed, 128):
+            end = min(f + 128, packed)
+            wall_t[:, f:end] = gall[f:end, :chans].astype(f32).T.astype(bf16)
+        gw_ref[...] = jnp.zeros_like(gw_ref) if fresh else prev_ref[...]
+        gg_s[...] = jnp.zeros_like(gg_s)
+        sc_s[...] = jnp.zeros_like(sc_s)
+
+    @pl.when(step < i_steps)
+    def _():
+        @pl.loop(0, chans, unroll=8)
+        def _(h):
+            for k in range(4):
+                sums[k][pl.ds(h * (rows + 1), rows), :] = sum_ref[k, h].astype(f32)
+
+        gain = jnp.concatenate([gain_ref[...]] * group, axis=1)
+
+        @pl.loop(0, rows // group)
+        def _(s2):
+            first = s2 * group
+            lanes = pl.ds(pl.multiple_of(first * width, group * width), group * width)
+
+            def wide(get):
+                return jnp.concatenate([get(first + n) for n in range(group)], axis=1)
+
+            def cut(value, n):
+                return value[:, n * width : (n + 1) * width]
+
+            inner = wide(lambda r: norm_ref[r])
+            nb[:, lanes] = inner
+            mask = wide(lambda r: mask_ref[pl.ds(r, 1), :])
+            parts = []
+            for g in range(4):
+                proj = dot(w_s[g * 8 * quarter : (g + 1) * 8 * quarter], inner)
+                for k in range(4):
+                    gate = proj[(2 * k) * quarter : (2 * k + 1) * quarter]
+                    value = proj[(2 * k + 1) * quarter : (2 * k + 2) * quarter]
+                    grad = wide(lambda r: sums[k][pl.ds(g * quarter * (rows + 1) + r, quarter, stride=rows + 1), :])
+                    sig = sigmoid(gate)
+                    back = grad * mask * sig
+                    parts.append((back * value * (1.0 - sig)).astype(bf16))
+                    parts.append(back.astype(bf16))
+                for d in range(2):
+                    at = d * chans + g * quarter
+                    parts.append(wide(lambda r: gate_ref[r, at : at + quarter]))
+                for n in range(group):
+                    sc_s[g * 16 : g * 16 + here, n * width : (n + 1) * width] = score_ref[
+                        first + n, g * here : (g + 1) * here
+                    ]
+                parts.append(sc_s[g * 16 : (g + 1) * 16].astype(bf16))
+                parts.append(jnp.zeros((block_rows - 10 * quarter - 16, group * width), bf16))
+            every = jnp.concatenate(parts, axis=0)
+            gall[:, lanes] = every
+            back = dot(wall_t[...], every)
+            scaled, inverse = sub_norm(wide(lambda r: pair_ref[r]).astype(f32))
+            gg_s[...] += back * scaled
+            out = wide(lambda r: mid_ref[r]).astype(f32) + sub_norm_back(gain, scaled, inverse, back)
+            out = out.astype(bf16)
+            for n in range(group):
+                for q in range(4):
+                    po[q, first + n] = cut(out[q * quarter : (q + 1) * quarter], n)
+
+        for m in range(4):
+            outs[m][...] = po[lax.bitwise_xor(z, m)]
+        gw_ref[...] += dot(gall[...], nb[...], 1, 1)
+
+    @pl.when(step == i_steps - 1)
+    def _():
+        row = lane_sums(gg_s[...])
+        for g in range(4):
+            at = (g + 1) * block_rows - 1
+            gw_ref[at : at + 1] += row
+        gw_out_ref[...] = gw_ref[...].astype(gw_out_ref.dtype)
+
+    @pl.when(step == i_steps)
+    def _():
+        for m in range(4):
+            outs[m][: extra_ref.shape[1]] = extra_ref[m]
+
+
+def finish(place, sums, first_row, pair, norm, mid, gate, scores, mask_rows, gain, wall, prev, extra, step_rows=16):
+    rows, chans, width = pair.shape
+    quarter = chans // 4
+    heads = scores.shape[1]
+    packed = 4 * wall.shape[1]
+    i_steps = rows // step_rows
+    fresh = prev is None
+    start = first_row // step_rows
+    last = first_row + rows == mask_rows.shape[0]
+    total = in_hbm((packed, chans), bf16 if last else f32)
+
+    def at(s):
+        return jnp.minimum(s, i_steps - 1)
+
+    if fresh:
+        prev = gain
+    row_spec = pl.BlockSpec((step_rows, chans, width), lambda s: (at(s), 0, 0))
+    piece_spec = pl.BlockSpec((step_rows, quarter, width), lambda s: (s, 0, 0))
+    piece = in_hbm((rows + (extra.shape[1] if last else 0), quarter, width), bf16)
+    lanes = step_rows * width
+    return pl.pallas_call(
+        functools.partial(finish_kernel, i_steps, fresh),
+        grid=(i_steps + (1 if last else 0),),
+        in_specs=[place_spec(), pl.BlockSpec((4, chans, step_rows, width), lambda s: (0, 0, at(s) + start, 0))]
+        + [row_spec] * 3
+        + [
+            pl.BlockSpec((step_rows, 2 * chans, width), lambda s: (at(s), 0, 0)),
+            pl.BlockSpec((step_rows, heads, width), lambda s: (at(s) + start, 0, 0)),
+            pl.BlockSpec((step_rows, width), lambda s: (at(s) + start, 0)),
+        ]
+        + [whole_spec(a) for a in (gain, wall, prev, extra)],
+        out_specs=[piece_spec] * 4 + [whole_spec(total)],
+        out_shape=[piece] * 4 + [total],
+        scratch_shapes=[pltpu.VMEM((packed, chans), f32)]
+        + [pltpu.VMEM((chans * (step_rows + 1), width), f32)] * 4
+        + [
+            pltpu.VMEM((chans, packed), bf16),
+            pltpu.VMEM((8 * chans, chans), bf16),
+            pltpu.VMEM((packed, lanes), bf16),
+            pltpu.VMEM((chans, lanes), bf16),
+            pltpu.VMEM((4, step_rows, quarter, width), bf16),
+            pltpu.VMEM((64, group * width), f32),
+            pltpu.VMEM((chans, group * width), f32),
+        ],
+        compiler_params=params(56),
+        cost_estimate=quick,
+        name="finish",
+    )(place, *held([sums, pair, norm, mid, gate]), scores, mask_rows, gain, wall, prev, extra)
+
+
+def assemble_kernel(rows, count, nodes, place_ref, *refs):
+    pieces, (out_ref, *node_refs) = refs[: 4 * count], refs[4 * count : 4 * count + (3 if nodes else 1)]
+    sems, z = refs[-1], place_ref[0]
+    copies = []
+    for m in range(4):
+        crop = lax.bitwise_xor(z, m)
+        for n in range(count):
+            source, target = pieces[4 * n + m], out_ref.at[crop, pl.ds(n * rows, rows)]
+            copies.append(pltpu.make_async_copy(source.at[pl.ds(0, rows)], target, sems.at[m, n]))
+        if nodes:
+            source = pieces[4 * (count - 1) + m].at[pl.ds(rows, 2)]
+            copies.append(pltpu.make_async_copy(source, refs[-2].at[crop], sems.at[m, count]))
+    for copy in copies:
+        copy.start()
+    for copy in copies:
+        copy.wait()
+    for n, ref in enumerate(node_refs):
+        for crop in range(4):
+            value = refs[-2][crop, n]
+            half, width = value.shape[0], value.shape[1] // 2
+            ref[crop, :half] = value[:, :width]
+            ref[crop, half:] = value[:, width:]
+
+
+def assemble(place, chunks, rows, nodes):
+    _, quarter, width = chunks[0][0].shape
+    count = len(chunks)
+    vmem = pl.BlockSpec(memory_space=pltpu.VMEM)
+    shapes = [jax.ShapeDtypeStruct((4, rows * count, quarter, width), bf16)]
+    scratch = [pltpu.SemaphoreType.DMA((4, count + 1))]
+    if nodes:
+        shapes += [jax.ShapeDtypeStruct((4, 2 * quarter, width // 2), bf16)] * 2
+        scratch = [pltpu.VMEM((4, 2, quarter, width), bf16)] + scratch
+    return pl.pallas_call(
+        functools.partial(assemble_kernel, rows, count, nodes),
+        in_specs=[place_spec()] + [any_spec()] * (4 * count),
+        out_specs=[any_spec()] + [vmem] * (len(shapes) - 1),
+        out_shape=shapes,
+        scratch_shapes=scratch,
+        compiler_params=params(16),
+        cost_estimate=quick,
+        name="assemble",
+    )(place, *[piece for chunk in chunks for piece in chunk])
+
+
+def unpack_kernel(early, node_rows, place_ref, own, far, tri_in, gate, bias, tri_out, trans_in, trans_out, qkv, attn, node_in, node_out, gains, node_gains):
+    first = place_ref[1] == 0
+    own, far = own[...].astype(f32), far[...].astype(f32)
+    a, b = jnp.where(first, own[:early], far[:early]), jnp.where(first, far[:early], own[:early])
+    last = own[early:] + far[early:]
+    quarter = tri_out.shape[1]
+    chans = trans_in.shape[0]
+    half = chans + quarter + 8
+    wide = jnp.concatenate([a[:node_rows], b[:node_rows]], axis=1)
+    rest = jnp.concatenate([a[node_rows : node_rows + half], b[node_rows : node_rows + half]], axis=0)
+    for d in range(2):
+        for n in range(4):
+            at = (4 * d + n) * quarter
+            tri_in[d, n] = last[at : at + quarter]
+        gate[d] = last[(8 + d) * quarter : (9 + d) * quarter]
+        tri_out[d] = rest[d * quarter : (d + 1) * quarter]
+    bias[...] = last[10 * quarter : 10 * quarter + bias.shape[0]]
+    at = 2 * quarter
+    trans_in[...] = rest[at : at + chans].T
+    trans_out[...] = rest[at + chans : at + 2 * chans]
+    at = at + 2 * chans
+    gains[...] = jnp.concatenate([last[last.shape[0] - 1 :], rest[at : at + 7]], axis=0)
+    size = qkv.shape[1]
+    for n in range(3):
+        qkv[n] = wide[n * size : (n + 1) * size]
+    at = 3 * size
+    attn[...] = wide[at : at + size]
+    at = at + size
+    size = node_in.shape[0]
+    node_in[...] = wide[at : at + size].T
+    node_out[...] = wide[at + size : at + 2 * size]
+    at = at + 2 * size
+    node_gains[...] = wide[at : at + 8]
+
+
+def unpack(place, own, far, early, node_rows, heads):
+    chans = own.shape[1]
+    quarter, nodes = chans // 4, 2 * chans
+    shapes = [
+        (2, 4, quarter, chans), (2, quarter, chans), (heads, chans), (2, quarter, chans), (chans, chans), (chans, chans),
+        (3, nodes // 4, nodes), (nodes // 4, nodes), (nodes, nodes), (nodes, nodes), (8, chans), (8, nodes),
+    ]
+    vmem = pl.BlockSpec(memory_space=pltpu.VMEM)
+    return pl.pallas_call(
+        functools.partial(unpack_kernel, early, node_rows),
+        in_specs=[place_spec()] + [vmem] * 2,
+        out_specs=[vmem] * len(shapes),
+        out_shape=[jax.ShapeDtypeStruct(shape, f32) for shape in shapes],
+        compiler_params=params(32),
+        cost_estimate=quick,
+        name="unpack",
+    )(place, own, far)
+
+
+def node_kernel(place_ref, bias_ref, bias_far, live_ref, gain_ref, gain_mid_ref, near_w, far_w,
+                sent_ref, score_ref, gw_ref, w_all, att, gqkv):
+    z, core, x = place_ref[0], place_ref[1], place_ref[2]
+    first = core == 0
+    groups, packed, _ = gw_ref.shape
+    half_rows = bias_ref.shape[1]
+    length, nodes = 2 * half_rows, gain_ref.shape[1]
+    quarter = nodes // groups
+    fold = quarter // 2
+    count = near_w.shape[1] // 2 - fold
+    for m in range(groups):
+        for ref, side in ((near_w, core), (far_w, 1 - core)):
+            for at, other in ((0, x), (count, 1 - x)):
+                here = pl.ds(pl.multiple_of((2 * side + other) * count, count), count)
+                w_all[lax.bitwise_xor(z, m), here] = ref[m, at:at + count]
+    heads = bias_ref.shape[0]
+    head_dim = nodes // heads
+    hidden = nodes
+    scale = 1.0 / math.sqrt(head_dim)
+
+    def weight(at, size):
+        return jnp.concatenate(
+            [jnp.concatenate([w_all[g, half * packed + at:half * packed + at + size] for half in range(2)], axis=1) for g in range(groups)], axis=0)
+
+    def ordered(mine, far):
+        return jnp.concatenate([jnp.where(first, mine, far), jnp.where(first, far, mine)], axis=0)
+
+    def rows(value):
+        return jnp.where(first, value[:half_rows], value[half_rows:])
+
+    def parts(value):
+        centered = value - jnp.mean(value, axis=1, keepdims=True)
+        inverse = lax.rsqrt(jnp.mean(centered * centered, axis=1, keepdims=True) + epsilon)
+        return centered * inverse, inverse
+
+    def back(gain, scaled, inverse, grad):
+        weighted = gain * grad
+        first_mean = jnp.mean(weighted, axis=1, keepdims=True)
+        second_mean = jnp.mean(weighted * scaled, axis=1, keepdims=True)
+        return inverse * (weighted - first_mean - scaled * second_mean)
+
+    def own_half(value):
+        return jnp.where(first, value[:, :128], value[:, 128:]).astype(bf16)
+
+    def keep(at, value):
+        size = value.shape[0] // groups
+        for g in range(groups):
+            gw_ref[g, at:at + size] = own_half(value[g * size:(g + 1) * size])
+
+    def gain_row(grad, scaled):
+        return jnp.sum(grad * scaled, axis=0, keepdims=True)
+
+
+    def unfolded(ref, n):
+        rows_of = slice(2 * count + n * fold, 2 * count + (n + 1) * fold)
+        parts = [ref[lax.bitwise_xor(z, g), rows_of].astype(f32) for g in range(groups)]
+        half = parts[0].shape[1] // 2
+        return jnp.concatenate([jnp.concatenate([v[:, :half], v[:, half:]], axis=0) for v in parts], axis=1)
+
+    def sent(n, value):
+        for g in range(groups):
+            part = value[:, g * quarter:(g + 1) * quarter]
+            half = part.shape[0] // 2
+            sent_ref[lax.bitwise_xor(z, g), n] = jnp.concatenate([part[:half], part[half:]], axis=1).astype(bf16)
+
+    node_in = ordered(unfolded(near_w, 0), unfolded(far_w, 0))
+    cot = ordered(unfolded(near_w, 1), unfolded(far_w, 1)).astype(bf16)
+    scaled_in, inverse_in = parts(node_in)
+    low_in = (scaled_in * gain_ref[...]).astype(bf16)
+    q, k, v = (dot(low_in, weight(g * quarter, quarter), 1, 1).astype(bf16) for g in range(3))
+    lane = lax.broadcasted_iota(jnp.int32, (1, nodes), 1)
+    key_live = live_ref[...] > 0.5
+
+    def of_head(value, h):
+        here = (lane >= h * head_dim) & (lane < (h + 1) * head_dim)
+        return jnp.where(here, value, jnp.zeros_like(value))
+
+    def probs_of(h):
+        raw = dot(of_head(q, h), k, 1, 1) * scale + ordered(bias_ref[h], bias_far[h])
+        scores = jnp.where(key_live, raw, -1e9)
+        exps = jnp.exp(scores - jnp.max(scores, axis=1, keepdims=True))
+        return exps / jnp.sum(exps, axis=1, keepdims=True)
+
+    total = jnp.zeros((length, nodes), f32)
+    for h in range(heads):
+        probs = probs_of(h)
+        att[h] = probs
+        total = total + dot(probs.astype(bf16), of_head(v, h))
+    attn = total.astype(bf16)
+    at_a, at_i, at_o = 3 * quarter, 4 * quarter, 4 * quarter + hidden
+    mid = node_in + dot(attn, weight(at_a, quarter), 1, 1)
+    scaled_mid, inverse_mid = parts(mid)
+    low_mid = (scaled_mid * gain_mid_ref[...]).astype(bf16)
+    out = mid
+    grad = jnp.zeros((length, nodes), f32)
+    for g in range(groups):
+        w_in = jnp.concatenate([w_all[g, half * packed + at_i:half * packed + at_i + hidden] for half in range(2)], axis=1)
+        w_out = jnp.concatenate([w_all[g, half * packed + at_o:half * packed + at_o + hidden] for half in range(2)], axis=1)
+        act, slope = gelu_both(dot(low_mid, w_in, 1, 1))
+        act = act.astype(bf16)
+        out = out + dot(act, w_out)
+        grad_pre = (dot(cot, w_out, 1, 1) * slope).astype(bf16)
+        grad = grad + dot(grad_pre, w_in)
+        gi, go = dot(grad_pre, low_mid, 0, 0), dot(act, cot, 0, 0)
+        gw_ref[g, at_i:at_i + hidden] = own_half(gi)
+        gw_ref[g, at_o:at_o + hidden] = own_half(go)
+    sent(0, rows(out))
+    mid_row = gain_row(grad, scaled_mid)
+    grad_mid = cot.astype(f32) + back(gain_mid_ref[...], scaled_mid, inverse_mid, grad)
+    grad_low = grad_mid.astype(bf16)
+    keep(at_a, dot(grad_low, attn, 0, 0))
+    grad_attn = dot(grad_low, weight(at_a, quarter)).astype(bf16)
+    for g in range(3):
+        gqkv[g] = jnp.zeros((length, nodes), f32)
+    for h in range(heads):
+        probs = att[h]
+        grad_probs = dot(of_head(grad_attn, h), v, 1, 1)
+        delta = jnp.sum(probs * grad_probs, axis=1, keepdims=True)
+        scores = probs * (grad_probs - delta)
+        score_ref[:, h, :] = rows(scores)
+        scores = scores.astype(bf16)
+        gqkv[0] += dot(scores, of_head(k, h))
+        gqkv[1] += dot(scores, of_head(q, h), 0, 0)
+        gqkv[2] += dot(probs.astype(bf16), of_head(grad_attn, h), 0, 0)
+    grad = jnp.zeros((length, nodes), f32)
+    for g, factor in enumerate((scale, scale, 1.0)):
+        low = (gqkv[g] * factor).astype(bf16)
+        keep(g * quarter, dot(low, low_in, 0, 0))
+        grad = grad + dot(low, weight(g * quarter, quarter))
+    tail = jnp.concatenate([gain_row(grad, scaled_in), mid_row, jnp.zeros((14, nodes), f32)], axis=0)
+    for g in range(groups):
+        gw_ref[g, packed - 16:] = own_half(tail)
+    sent(1, rows(grad_mid + back(gain_ref[...], scaled_in, inverse_in, grad)))
+
+def node_track(place, bias, bias_far, live, gain, gain_mid, near_w, far_w, rows):
+    half_rows, length = bias.shape[1], live.shape[1]
+    nodes = gain.shape[1]
+    heads = bias.shape[0]
+    arrays = (bias, bias_far, live, gain, gain_mid, near_w, far_w)
+    shapes = [
+        jax.ShapeDtypeStruct((near_w.shape[0], 2, half_rows // 2, 128), bf16),
+        jax.ShapeDtypeStruct((half_rows, heads, length), f32),
+        jax.ShapeDtypeStruct((near_w.shape[0], rows, 128), bf16),
+    ]
+    vmem = pl.BlockSpec(memory_space=pltpu.VMEM)
+    return pl.pallas_call(
+        node_kernel,
+        in_specs=[pl.BlockSpec(memory_space=pltpu.SMEM)] + [vmem] * len(arrays),
+        out_specs=[vmem] * len(shapes),
+        out_shape=shapes,
+        scratch_shapes=[pltpu.VMEM((near_w.shape[0], 2 * near_w.shape[1], 128), bf16), pltpu.VMEM((heads, length, length), f32), pltpu.VMEM((3, length, nodes), f32)],
+        compiler_params=params(40),
+        cost_estimate=quick,
+        name="node_track",
+    )(place, *arrays)
+
+
+def shards_by_crop(
+    pair,
+    node,
+    pair_cot,
+    node_cot,
+    lengths,
+    present,
+    gain_pair,
+    w_tri_in,
+    w_out_gate,
+    gain_tri,
+    w_tri_out,
+    gain_trans,
+    w_trans_in,
+    w_trans_out,
+    w_bias,
+    gain_node,
+    w_qkv,
+    w_attn_out,
+    gain_node_trans,
+    w_node_in,
+    w_node_out,
+):
+    groups = lax.axis_size(CHAN)
+    rows_here = pair.shape[1]
+    chans = groups * pair.shape[2]
+    crop_len = pair.shape[3]
+    nodes = groups * node.shape[2]
+    heads = groups * w_bias.shape[1]
+    quarter, node_quarter = chans // groups, nodes // groups
+    z = lax.axis_index(CHAN)
+    core = lax.axis_index(DP) % 2
+    x = lax.axis_index(ROWS)
+    y = lax.axis_index(DP) // 2
+    place = jnp.stack([z, core, x, y]).astype(jnp.int32)
+    mesh_shape = (lax.axis_size(DP), lax.axis_size(ROWS), groups)
+
+    def device(d, r, c):
+        return (d * mesh_shape[1] + r) * groups + c
+
+    def home_perm(m):
+        return [
+            (device(d, r, c), device(d - d % 2 + r, d % 2, c ^ m))
+            for d in range(mesh_shape[0])
+            for r in range(mesh_shape[1])
+            for c in range(groups)
+        ]
+
+    core_pairs = [(d, d ^ 1) for d in range(mesh_shape[0])]
+    row_pairs = [(0, 1), (1, 0)]
+
+    def send_home(pieces):
+        return [
+            lax.ppermute(piece, (DP, ROWS, CHAN), home_perm(m))
+            for m, piece in enumerate(pieces)
+        ]
+
+    def to_chan(value, m):
+        return lax.ppermute(value, CHAN, [(c, c ^ m) for c in range(groups)])
+
+    def swap_core(value):
+        return lax.ppermute(value, DP, core_pairs)
+
+    def pick(value, index):
+        return lax.dynamic_index_in_dim(value, index, 0, keepdims=False)
+
+    def own_rows(value, axis):
+        return lax.dynamic_slice_in_dim(value, core * rows_here, rows_here, axis)
+
+    def packed(parts):
+        return jnp.concatenate([part.reshape(-1, chans) for part in parts])
+
+    def split(value):
+        return jnp.concatenate([value[:, :chans], value[:, chans:]])
+
+    chunk = min(32, rows_here)
+    tied = lax.optimization_barrier
+
+    def blocks(rows):
+        rows = jnp.pad(rows, ((0, -rows.shape[0] % (4 * quarter)), (0, 0)))
+        return rows.reshape(-1, quarter, chans)
+
+    def with_far(own, far, side):
+        return jnp.concatenate([jnp.where(side == 0, own, far), jnp.where(side == 0, far, own)], axis=1)
+
+    def swap_rows(value):
+        return lax.ppermute(value, ROWS, row_pairs)
+
+    node_rest = jnp.concatenate(
+        [w_qkv.transpose(0, 2, 1).reshape(-1, nodes), w_attn_out.T, w_node_in.T, w_node_out]
+    )
+    node_rest = jnp.pad(node_rest, ((0, 16), (0, 0)))
+    first_rows, pair_rows, node_rows = 10 * quarter + 32, 2 * quarter + 2 * chans, node_rest.shape[0]
+
+    def tiles(values):
+        return jnp.broadcast_to(values[..., None], values.shape + (chans,))
+
+    gains = [tiles(values) for values in (gain_pair, gain_tri, gain_trans)]
+    sent = pack(
+        place,
+        pair,
+        0,
+        chunk,
+        first=[
+            lengths,
+            present,
+            node,
+            node_cot,
+            w_tri_in.transpose(0, 1, 3, 2).reshape(-1, chans),
+            w_out_gate.transpose(0, 2, 1).reshape(-1, chans),
+            w_bias.T,
+            w_tri_out.transpose(0, 2, 1).reshape(-1, chans),
+            w_trans_in,
+            w_trans_out,
+        ],
+    )
+    sent, pair, pair_cot = tied((sent, pair, pair_cot))
+    pieces0 = send_home(sent)
+    sent = pack(place, pair, chunk, chunk)
+    sent_cots = pack(place, pair_cot, 0, chunk)
+    sent_later = pack(place, pair_cot, chunk, chunk, blocks(split(node_rest)))
+    sent, sent_cots, sent_later, gains, pieces0 = tied((sent, sent_cots, sent_later, gains, pieces0))
+    pieces1 = send_home(sent)
+    node_own = jnp.stack([piece[chunk + 1 : chunk + 3] for piece in pieces0])
+    weights = jnp.stack([piece[chunk + 3 :] for piece in pieces0]).reshape(groups, -1, chans)
+    weights = with_far(weights, swap_core(weights), core)
+    wall, rest = weights[:, :first_rows], weights[:, first_rows : first_rows + pair_rows]
+    gain, gains_mid = gains[0], gains[1:]
+    live = pieces0[0][chunk, 0].astype(jnp.float32)
+    mask_rows = own_rows(live, 0)[:, None] * live[None, :]
+    tri0, norm0, pair0, bias0 = project(place, pieces0, wall, mask_rows, gain, heads, chunk, 0)
+    tri0, pieces1, rest = tied((tri0, pieces1, rest))
+    far0 = swap_core(tri0)
+    tri1, norm1, pair1, bias1 = project(place, pieces1, wall, mask_rows, gain, heads, chunk, chunk)
+    tri1, far0, sent = tied((tri1, far0, sent_cots))
+    far1 = swap_core(tri1)
+    cots0 = send_home(sent)
+    bias = jnp.concatenate([bias0, bias1], axis=1)
+    bias, far1 = tied((bias, far1))
+    bias_far = swap_core(bias)
+    tri = tri_forward(place, (tri0, tri1), (far0, far1))
+    sent, bias_far, cots0, tri = tied((sent_later, bias_far, cots0, tri))
+    cots1 = send_home(sent)
+    norms, pairs = (norm0, norm1), (pair0, pair1)
+
+    core_round, row_round = (core, DP, core_pairs), (x, ROWS, row_pairs)
+    y_round = (y, DP, [(d, d ^ 2) for d in range(mesh_shape[0])])
+
+    def halve(value, side, axis, pairs, at=1):
+        low, high = jnp.split(value, 2, at)
+        far = lax.ppermute(jnp.where(side == 0, high, low).astype(jnp.bfloat16), axis, pairs)
+        return jnp.where(side == 0, low, high).astype(jnp.float32), far
+
+    def added(kept, far):
+        return (kept + far).astype(jnp.bfloat16)
+
+    def both(value, far, side):
+        return jnp.concatenate([jnp.where(side == 0, value, far), jnp.where(side == 0, far, value)])
+
+    def run_middle(n, cots, prev):
+        return middle(
+            place, tri, n * chunk, pairs[n], norms[n], cots, *gains_mid, wall, rest, prev
+        )
+
+    *out0, mid0, gate0, gtri0, gw_rest = run_middle(0, cots0, None)
+    out0, gtri0, cots1 = tied((out0, gtri0, cots1))
+    out0 = send_home(out0)
+    node_rest = jnp.stack([cot[chunk:] for cot in cots1]).reshape(groups, -1, chans)
+    node_rest = jnp.concatenate(
+        [node_rest, swap_rows(node_rest), node_own.reshape(groups, -1, chans)], axis=1
+    )
+    *out1, mid1, gate1, gtri1, gw_rest = run_middle(1, cots1, gw_rest)
+    gtri0, gtri1, out0, node_rest = tied((gtri0, gtri1, out0, node_rest))
+    node_rest_far = swap_core(node_rest)
+    rest_half = added(*halve(gw_rest, *core_round))
+    gtri0, gtri1, node_rest_far, rest_half = tied((gtri0, gtri1, node_rest_far, rest_half))
+    gtris = (gtri0, gtri1)
+    gtris_far = [swap_core(gtri) for gtri in gtris]
+    mids, gates = (mid0, mid1), (gate0, gate1)
+
+    node_sent, scores, gw_node = node_track(
+        place,
+        bias,
+        bias_far,
+        live[None, :],
+        gain_node[None, :],
+        gain_node_trans[None, :],
+        node_rest,
+        node_rest_far,
+        node_rows,
+    )
+    early = [gw_node, rest_half]
+    early_rows = sum(part.shape[1] for part in early)
+    early.append(jnp.zeros((groups, -early_rows % 64, chans), jnp.bfloat16))
+    early = jnp.concatenate(early, axis=1)
+    out1, gtris_far = tied((out1, gtris_far))
+    out1 = send_home(out1)
+    kept, far = halve(early, *row_round)
+    sums = tri_backward(place, (tri0, tri1), (far0, far1), gtris, gtris_far)
+
+    def run_finish(n, prev):
+        return finish(
+            place, sums, n * chunk, pairs[n], norms[n], mids[n], gates[n], scores, mask_rows, gain, wall, prev, node_sent
+        )
+
+    sums, kept, far = tied((sums, kept, far))
+    kept, far = halve(added(kept, far), *y_round)
+    *grad0, gw_first = run_finish(0, None)
+    grad0, out1, kept, far = tied((grad0, out1, kept, far))
+    grad0 = send_home(grad0)
+    *grad1, gw_first = run_finish(1, gw_first)
+    grad1, gw_first, grad0 = tied((grad1, gw_first, grad0))
+    grad1 = send_home(grad1)
+    early = added(kept, far)
+    shard = early.shape[1]
+    low = jnp.concatenate([early, gw_first.reshape(groups, -1, chans)], axis=1)
+    total = pick(low, z).astype(jnp.float32)
+    for m in range(1, groups):
+        total = total + to_chan(pick(low, z ^ m), m)
+    total = total.astype(jnp.bfloat16)
+    total, out0, out1 = tied((total, out0, out1))
+    early, late = total[:shard], total[shard:]
+    for side, axis, pairs in (y_round, row_round):
+        far = lax.ppermute(jnp.concatenate([early, late]), axis, pairs)
+        if axis != ROWS:
+            grad1, far = tied((grad1, far))
+        late = added(late.astype(jnp.float32), far[early.shape[0] :])
+        early = both(early, far[: early.shape[0]], side)
+    own = jnp.concatenate([early, late])
+    far = swap_core(own)
+    tri_in, out_gate, bias_w, tri_out, trans_in, trans_out, qkv, attn, node_in, node_out, gain_rows, node_gains = unpack(
+        place, own, far, early.shape[0], node_rows, w_bias.shape[1]
+    )
+    def xassemble(chunks):
+        rows = [jnp.concatenate([c[m][:chunk] for c in chunks]) for m in range(groups)]
+        stacked = jnp.stack(rows)
+        return jnp.stack([pick(stacked, z ^ k) for k in range(groups)])
+
+    pair_out = xassemble((out0, out1))
+    pair_grad, node_result, node_grad = assemble(place, (grad0, grad1), chunk, True)
+
+    def own_block(row, size):
+        return lax.dynamic_slice_in_dim(row, z * size, size, row.ndim - 1)
+
+    gain_rows, node_gains = own_block(gain_rows, quarter), own_block(node_gains, node_quarter)
+    return (
+        pair_out,
+        node_result,
+        pair_grad,
+        node_grad,
+        gain_rows[0],
+        tri_in.transpose(0, 1, 3, 2),
+        out_gate.transpose(0, 2, 1),
+        gain_rows[2:4],
+        tri_out.transpose(0, 2, 1),
+        gain_rows[1],
+        trans_in,
+        trans_out,
+        bias_w.T,
+        node_gains[0],
+        qkv.transpose(0, 2, 1),
+        attn.T,
+        node_gains[1],
+        node_in,
+        node_out,
+    )
+
+
 def solution(mesh):
     in_specs = (
-        P("dp", "rows", "chan", None),
-        P("dp", "rows", "chan"),
-        P("dp", "rows", "chan", None),
-        P("dp", "rows", "chan"),
-        P("dp"),
-        P("dp", None),
+        P(DP, ROWS, CHAN, None),
+        P(DP, ROWS, CHAN),
+        P(DP, ROWS, CHAN, None),
+        P(DP, ROWS, CHAN),
+        P(DP),
+        P(DP, None),
         P(),
-        P(None, None, None, "chan"),
-        P(None, None, "chan"),
+        P(None, None, None, CHAN),
+        P(None, None, CHAN),
         P(),
-        P(None, None, "chan"),
+        P(None, None, CHAN),
         P(),
-        P(None, "chan"),
-        P("chan", None),
-        P(None, "chan"),
+        P(None, CHAN),
+        P(CHAN, None),
+        P(None, CHAN),
         P(),
-        P(None, None, "chan"),
-        P(None, "chan"),
+        P(None, None, CHAN),
+        P(None, CHAN),
         P(),
-        P(None, "chan"),
-        P("chan", None),
+        P(None, CHAN),
+        P(CHAN, None),
     )
     out_specs = (
-        P("dp", "rows", "chan", None),
-        P("dp", "rows", "chan"),
-        P("dp", "rows", "chan", None),
-        P("dp", "rows", "chan"),
-        P("chan"),
-        P(None, None, None, "chan"),
-        P(None, None, "chan"),
-        P(None, "chan"),
-        P(None, None, "chan"),
-        P("chan"),
-        P(None, "chan"),
-        P("chan", None),
-        P(None, "chan"),
-        P("chan"),
-        P(None, None, "chan"),
-        P(None, "chan"),
-        P("chan"),
-        P(None, "chan"),
-        P("chan", None),
-    )
-    return jax.shard_map(shards, mesh=mesh, in_specs=in_specs, out_specs=out_specs, check_vma=False)
+        P(DP, ROWS, CHAN, None),
+        P(DP, ROWS, CHAN),
+        P(DP, ROWS, CHAN, None),
+        P(DP, ROWS, CHAN),
+        P(CHAN),
+        P(None, None, None, CHAN),
+        P(None, None, CHAN),
+        P(None, CHAN),
+        P(None, None, CHAN),
+        P(CHAN),
+        P(None, CHAN),
+        P(CHAN, None),
+        P(None, CHAN),
+        P(CHAN),
+        P(None, None, CHAN),
+        P(None, CHAN),
+        P(CHAN),
+        P(None, CHAN),
+        P(CHAN, None),
+    )
+    sizes = dict(mesh.shape)
+    by_crop = sizes[ROWS] == 2 and sizes[DP] == 4 and sizes[CHAN] == 4
+    body = shards_by_crop if by_crop else shards
+    return jax.shard_map(body, mesh=mesh, in_specs=in_specs, out_specs=out_specs, check_vma=False)

time: 2330 us -> 325 us (0.14)
  waiting for transfers between devices: 1430 us -> 91.3 us
  matrix products: 309 us -> 0 us
  local copies, waits for them, and re-layouts: 200 us -> 8.84 us
  other arithmetic: 188 us -> 13.4 us
  blocking collectives: 166 us -> 0 us
  Pallas kernels: 0 us -> 144 us
  starting transfers between devices: 2.31 us -> 63.9 us
    all_gather x8 -> x0, waiting for transfers between devices: 641 us -> none  [the longest x1 149 us: shards(): lax.all_gather(pair, 'chan', axis=2, tiled=True)]
    reduce_scatter x7 -> x0, waiting for transfers between devices: 366 us -> none  [the longest x1 147 us: shards(): lax.psum_scatter(grad_normed_mid.astype(jnp.bfloat16), 'chan', scatter_di...]
    dot_general x43 -> x0, matrix products: 309 us -> none  [the longest x1 42.3 us: shards(): jnp.einsum('bicj,cf->bifj', normed_mid, w_trans_in, preferred_element_typ...]
    unnamed x35 -> x0, waiting for transfers between devices: 309 us -> none
    pallas_call x0 -> x15, Pallas kernels: none -> 144 us  [the longest x2 45.7 us: middle(): pl.pallas_call(functools.partial(middle_kernel, fresh), grid=(rows // ste...]
    psum x2 -> x0, waiting for transfers between devices: 117 us -> none  [shards(): lax.psum((grad_gain_pair, grad_tri_in_w, grad_out_gate, grad_gain_tri, gr...]
    unnamed x286 -> x125, local copies, waits for them, and re-layouts: 120 us -> 4.78 us
    ppermute x0 -> x49, waiting for transfers between devices: none -> 91.3 us  [the longest x32 76.5 us: send_home(): lax.ppermute(piece, (DP, ROWS, CHAN), home_perm(m))]
  transfers between devices with their start and end apart: 26 -> 49, of which waited for: 17 -> 18; matrix products, arithmetic and copies ran while one was open for 24% -> 4% of each run, Pallas kernels for 0% -> 43%
where the time goes in v2:
time: 325 us; the launch traced here: 323 us
  Pallas kernels  144 us (44%)
  waiting for transfers between devices  91.3 us (28%)
  starting transfers between devices  63.9 us (20%)
  other arithmetic  13.4 us (4%)
  local copies, waits for them, and re-layouts  8.84 us (3%)
    ppermute x32, waiting for transfers between devices, send_home(): lax.ppermute(piece, (DP, ROWS, CHAN), home_perm(m))  76.5 us
    pallas_call x2, Pallas kernels, middle(): pl.pallas_call(functools.partial(middle_kernel, fresh), grid=(rows // ste...  45.7 us
    ppermute x32, starting transfers between devices, send_home(): lax.ppermute(piece, (DP, ROWS, CHAN), home_perm(m))  39.3 us
    pallas_call x2, Pallas kernels, finish(): pl.pallas_call(functools.partial(finish_kernel, i_steps, fresh), grid=(i_...  32.8 us
    pallas_call x1, Pallas kernels, tri_backward(): pl.pallas_call(functools.partial(tri_backward_kernel, len(mine)), grid=(c...  15.8 us
    pallas_call x2, Pallas kernels, project(): pl.pallas_call(project_kernel, grid=(rows // step_rows,), in_specs=[place...  13.5 us
    pallas_call x1, Pallas kernels, tri_forward(): pl.pallas_call(functools.partial(tri_forward_kernel, len(mine)), grid=(ch...  12.8 us
    pallas_call x4, Pallas kernels, pack(): pl.pallas_call(functools.partial(pack_kernel, first_row, rows, first is n...  12 us
  transfers between devices with their start and end apart: 49, of which 18 were waited for; matrix products, arithmetic and copies ran while one was open for 4% of the time, Pallas kernels for 43%

profile of v2, /device:TPU:8, one launch (start us, length us, event | category | flops | bytes accessed | tf_op | source)
XLA Modules:
  0.0 323.0 jit_solution(3324408681500519548)
XLA Ops:
  1.4 3.4 %pack.4 = (bf16[46,32,128]{2,1,0:T(8,128)(2,1)}, bf16[46,32,128]{2,1,0:T(8,128)(2,1)}, bf16[46,32,128]{2,1,0:T(8,128)(2,1)}, bf16[46,32,128]{2,1,0:T(8,128)(2,1)}) custom-call(s32[4]{0:T(128)S(1)} %pad_add_fusion.place_ref, bf16[4,64,32,128]{3,2,1,0:T(8,128)(2,1)} %refs_0_.2, s32[4]{0:T(128)S(1)} %copy-done.20, s32[4,128]{1,0:T(4,128)} %refs_2_.1, ...), custom_call_target="tpu_custom_call" | custom-call | flops 1 | bytes 1 | tf_op jit(solution)/shard_map/pack/pallas_call | solution.py:597
  6.5 3.0 collective-permute-start.2
  13.8 3.0 pack.7
  21.6 5.1 %collective-permute-done.2.p2 = bf16[46,32,128]{2,1,0:T(8,128)(2,1)S(1)} collective-permute-done((bf16[46,32,128]{2,1,0:T(8,128)(2,1)}, bf16[46,32,128]{2,1,0:T(8,128)(2,1)S(1)}, u32[]{:S(2)}, u32[]{:S(2)}) %collective-permute-start.2) | collective-permute-done | bytes 376864 | tf_op jit(solution)/shard_map/ppermute | solution.py:1433
  26.7 15.4 %collective-permute-done.3.p3 = bf16[46,32,128]{2,1,0:T(8,128)(2,1)S(1)} collective-permute-done((bf16[46,32,128]{2,1,0:T(8,128)(2,1)}, bf16[46,32,128]{2,1,0:T(8,128)(2,1)S(1)}, u32[]{:S(2)}, u32[]{:S(2)}) %collective-permute-start.3) | collective-permute-done | bytes 376864 | tf_op jit(solution)/shard_map/ppermute | solution.py:1433
  46.8 3.0 collective-permute-start.7
  50.5 6.8 %project.2 = (bf16[4,128,32,128]{3,2,1,0:T(8,128)(2,1)}, bf16[32,128,128]{2,1,0:T(8,128)(2,1)}, bf16[32,128,128]{2,1,0:T(8,128)(2,1)}, f32[8,32,128]{2,1,0:T(8,128)S(1)}) custom-call(s32[4]{0:T(128)S(1)} %pad_add_fusion.place_ref, bf16[46,32,128]{2,1,0:T(8,128)(2,1)S(1)} %collective-permute-done.p0, bf16[46,32,128]{2,1,0:T(8,128)(2,1)S(1)} %collective-permute-done.1.p1, ...), custom_call_target="tpu_custom_call" | custom-call | flops 1 | bytes 1 | tf_op jit(solution)/shard_map/project/pallas_call | solution.py:678
  58.0 3.4 %collective-permute-done.7.p2 = bf16[32,32,128]{2,1,0:T(8,128)(2,1)S(1)} collective-permute-done((bf16[32,32,128]{2,1,0:T(8,128)(2,1)}, bf16[32,32,128]{2,1,0:T(8,128)(2,1)S(1)}, u32[]{:S(2)}, u32[]{:S(2)}) %collective-permute-start.7) | collective-permute-done | bytes 262176 | tf_op jit(solution)/shard_map/ppermute | solution.py:1433
  61.4 10.5 %collective-permute-done.8.p3 = bf16[32,32,128]{2,1,0:T(8,128)(2,1)S(1)} collective-permute-done((bf16[32,32,128]{2,1,0:T(8,128)(2,1)}, bf16[32,32,128]{2,1,0:T(8,128)(2,1)S(1)}, u32[]{:S(2)}, u32[]{:S(2)}) %collective-permute-start.8) | collective-permute-done | bytes 262176 | tf_op jit(solution)/shard_map/ppermute | solution.py:1433
  71.9 3.2 %collective-permute-start.9 = (bf16[4,128,32,128]{3,2,1,0:T(8,128)(2,1)}, bf16[4,128,32,128]{3,2,1,0:T(8,128)(2,1)S(1)}, u32[]{:S(2)}, u32[]{:S(2)}) collective-permute-start(bf16[4,128,32,128]{3,2,1,0:T(8,128)(2,1)} %get-tuple-element.230.refs_0_), channel_id=1, source_target_pairs={{0,8},{8,0},{16,24},{24,16},{1,9},{9,1},{17,25},{25,17},{2,10},{10... | collective-permute-start | bytes 12582920 | tf_op jit(solution)/shard_map/ppermute | solution.py:1441
  75.2 6.8 %project.3 = (bf16[4,128,32,128]{3,2,1,0:T(8,128)(2,1)}, bf16[32,128,128]{2,1,0:T(8,128)(2,1)}, bf16[32,128,128]{2,1,0:T(8,128)(2,1)}, f32[8,32,128]{2,1,0:T(8,128)S(1)}) custom-call(s32[4]{0:T(128)S(1)} %pad_add_fusion.place_ref, bf16[32,32,128]{2,1,0:T(8,128)(2,1)S(1)} %collective-permute-done.5.p0, bf16[32,32,128]{2,1,0:T(8,128)(2,1)S(1)} %collective-permute-done.6.p1, ...), custom_call_target="tpu_custom_call" | custom-call | flops 1 | bytes 1 | tf_op jit(solution)/shard_map/project/pallas_call | solution.py:678
  90.3 12.8 %tri_forward.1.tri_ref = bf16[2,128,64,128]{3,2,1,0:T(8,128)(2,1)} custom-call(s32[4]{0:T(128)S(1)} %pad_add_fusion.place_ref, bf16[4,128,32,128]{3,2,1,0:T(8,128)(2,1)} %get-tuple-element.230.refs_0_, bf16[4,128,32,128]{3,2,1,0:T(8,128)(2,1)} %get-tuple-element.240.refs_1_, bf16[4,128,32,128]{3,2,1,0:T(8,128)(2,1)S(1)} %collective-permute-done.9.refs_2_, ...), custom_call_target="tpu_custom_call" | custom-call | flops 1 | bytes 1 | tf_op jit(solution)/shard_map/tri_forward/pallas_call | solution.py:736
  103.2 5.5 %collective-permute-done.15.c3 = bf16[32,32,128]{2,1,0:T(8,128)(2,1)S(1)} collective-permute-done((bf16[32,32,128]{2,1,0:T(8,128)(2,1)S(1)}, bf16[32,32,128]{2,1,0:T(8,128)(2,1)S(1)}, u32[]{:S(2)}, u32[]{:S(2)}) %collective-permute-start.15) | collective-permute-done | bytes 262176 | tf_op jit(solution)/shard_map/ppermute | solution.py:1433
  109.5 3.2 collective-permute-start.18
  112.9 23.1 %middle.2 = (bf16[32,32,128]{2,1,0:T(8,128)(2,1)}, bf16[32,32,128]{2,1,0:T(8,128)(2,1)}, bf16[32,32,128]{2,1,0:T(8,128)(2,1)}, bf16[32,32,128]{2,1,0:T(8,128)(2,...) custom-call(s32[4]{0:T(128)} %copy-done.15, ...), custom_call_target="tpu_custom_call" | custom-call | flops 1 | bytes 1 | tf_op jit(solution)/shard_map/middle/pallas_call | solution.py:892
  136.1 5.7 %collective-permute-done.19.c3 = bf16[45,32,128]{2,1,0:T(8,128)(2,1)S(1)} collective-permute-done((bf16[45,32,128]{2,1,0:T(8,128)(2,1)S(1)}, bf16[45,32,128]{2,1,0:T(8,128)(2,1)S(1)}, u32[]{:S(2)}, u32[]{:S(2)}) %collective-permute-start.19) | collective-permute-done | bytes 368672 | tf_op jit(solution)/shard_map/ppermute | solution.py:1433
  142.0 5.8 %collective-permute-start.24 = (bf16[4,416,128]{2,1,0:T(8,128)(2,1)S(1)}, bf16[4,416,128]{2,1,0:T(8,128)(2,1)S(1)}, u32[]{:S(2)}, u32[]{:S(2)}) collective-permute-start(bf16[4,416,128]{2,1,0:T(8,128)(2,1)S(1)} %pad_maximum_fusion.3), channel_id=1, source_target_pairs={{0,4},{4,0},{1,5},{5,1},{2,6},{6,2},{3,7},{7,3},{8,12},{12,8},{9,1... | collective-permute-start | bytes 1277960 | tf_op jit(solution)/shard_map/ppermute | solution.py:1466
  149.4 3.3 %collective-permute-start.22 = (bf16[32,32,128]{2,1,0:T(8,128)(2,1)}, bf16[32,32,128]{2,1,0:T(8,128)(2,1)S(1)}, u32[]{:S(2)}, u32[]{:S(2)}) collective-permute-start(bf16[32,32,128]{2,1,0:T(8,128)(2,1)} %get-tuple-element.284), channel_id=1, source_target_pairs={{0,2},{1,3},{2,0},{3,1},{4,10},{5,11},{6,8},{7,9},{8,6},{9,7},{10,... | collective-permute-start | bytes 786440 | tf_op jit(solution)/shard_map/ppermute | solution.py:1433
  152.9 22.6 %middle.3 = (bf16[32,32,128]{2,1,0:T(8,128)(2,1)}, bf16[32,32,128]{2,1,0:T(8,128)(2,1)}, bf16[32,32,128]{2,1,0:T(8,128)(2,1)}, bf16[32,32,128]{2,1,0:T(8,128)(2,...) custom-call(s32[4]{0:T(128)} %copy-done.15, ...), custom_call_target="tpu_custom_call" | custom-call | flops 1 | bytes 1 | tf_op jit(solution)/shard_map/middle/pallas_call | solution.py:892
  184.4 6.9 %node_track.1 = (bf16[4,2,32,128]{3,2,1,0:T(8,128)(2,1)S(1)}, f32[64,8,128]{2,1,0:T(8,128)S(1)}, bf16[4,784,128]{2,1,0:T(8,128)(2,1)S(1)}) custom-call(s32[4]{0:T(128)S(1)} %copy-done.16, f32[8,64,128]{2,1,0:T(8,128)S(1)} %pad_maximum_fusion.6.bias_ref, f32[8,64,128]{2,1,0:T(8,128)S(1)} %collective-permute-done.11.bias_far, ...), custom_call_target="tpu_custom_call" | custom-call | flops 1 | bytes 1 | tf_op jit(solution)/shard_map/node_track/pallas_call | solution.py:1368
  195.8 15.8 %tri_backward.1.sum_ref = bf16[4,128,64,128]{3,2,1,0:T(8,128)(2,1)} custom-call(s32[4]{0:T(128)S(1)} %copy-done.16, bf16[4,128,32,128]{3,2,1,0:T(8,128)(2,1)} %get-tuple-element.230.refs_0_, bf16[4,128,32,128]{3,2,1,0:T(8,128)(2,1)} %get-tuple-element.240.refs_1_, bf16[4,128,32,128]{3,2,1,0:T(8,128)(2,1)} %copy-done.1, bf16[4,128,32,128]{3,2,1,0:T(8,128)(2,1)} %copy-done.2, ...), custom_call_target="tpu_custom_call" | custom-call | flops 1 | bytes 1 | tf_op jit(solution)/shard_map/tri_backward/pallas_call | solution.py:963
  212.7 3.2 %collective-permute-start.32 = (bf16[32,32,128]{2,1,0:T(8,128)(2,1)S(1)}, bf16[32,32,128]{2,1,0:T(8,128)(2,1)S(1)}, u32[]{:S(2)}, u32[]{:S(2)}) collective-permute-start(bf16[32,32,128]{2,1,0:T(8,128)(2,1)S(1)} %copy-done.58), channel_id=1, source_target_pairs={{0,2},{1,3},{2,0},{3,1},{4,10},{5,11},{6,8},{7,9},{8,6},{9,7},{10,... | collective-permute-start | bytes 786440 | tf_op jit(solution)/shard_map/ppermute | solution.py:1433
  217.9 16.9 %finish.2 = (bf16[32,32,128]{2,1,0:T(8,128)(2,1)}, bf16[32,32,128]{2,1,0:T(8,128)(2,1)}, bf16[32,32,128]{2,1,0:T(8,128)(2,1)}, bf16[32,32,128]{2,1,0:T(8,128)(2,1)}, f32[1408,128]{1,0:T(8,128)}) custom-call(s32[4]{0:T(128)} %copy-done.15, bf16[4,128,64,128]{3,2,1,0:T(8,128)(2,1)} %tri_backward.1.sum_ref, bf16[32,128,128]{2,1,0:T(8,128)(2,1)} %get-tuple-element.255.pair_ref, ...), custom_call_target="tpu_custom_call" | custom-call | flops 1 | bytes 1 | tf_op jit(solution)/shard_map/finish/pallas_call | solution.py:1094
  234.9 3.7 %collective-permute-done.33 = bf16[32,32,128]{2,1,0:T(8,128)(2,1)S(1)} collective-permute-done((bf16[32,32,128]{2,1,0:T(8,128)(2,1)S(1)}, bf16[32,32,128]{2,1,0:T(8,128)(2,1)S(1)}, u32[]{:S(2)}, u32[]{:S(2)}) %collective-permute-start.33) | collective-permute-done | bytes 262176 | tf_op jit(solution)/shard_map/ppermute | solution.py:1433
  240.2 3.6 %collective-permute-start.37 = (bf16[32,32,128]{2,1,0:T(8,128)(2,1)}, bf16[32,32,128]{2,1,0:T(8,128)(2,1)S(1)}, u32[]{:S(2)}, u32[]{:S(2)}) collective-permute-start(bf16[32,32,128]{2,1,0:T(8,128)(2,1)} %get-tuple-element.329), channel_id=1, source_target_pairs={{0,2},{1,3},{2,0},{3,1},{4,10},{5,11},{6,8},{7,9},{8,6},{9,7},{10,... | collective-permute-start | bytes 786440 | tf_op jit(solution)/shard_map/ppermute | solution.py:1433
  243.8 15.8 %finish.3 = (bf16[34,32,128]{2,1,0:T(8,128)(2,1)}, bf16[34,32,128]{2,1,0:T(8,128)(2,1)}, bf16[34,32,128]{2,1,0:T(8,128)(2,1)}, bf16[34,32,128]{2,1,0:T(8,128)(2,1)}, bf16[1408,128]{1,0:T(8,128)(2,1)}) custom-call(s32[4]{0:T(128)} %copy-done.15, bf16[4,128,64,128]{3,2,1,0:T(8,128)(2,1)} %tri_backward.1.sum_ref, ...), custom_call_target="tpu_custom_call" | custom-call | flops 1 | bytes 1 | tf_op jit(solution)/shard_map/finish/pallas_call | solution.py:1094
  259.8 5.7 %collective-permute-done.38.refs_3_ = bf16[32,32,128]{2,1,0:T(8,128)(2,1)S(1)} collective-permute-done((bf16[32,32,128]{2,1,0:T(8,128)(2,1)}, bf16[32,32,128]{2,1,0:T(8,128)(2,1)S(1)}, u32[]{:S(2)}, u32[]{:S(2)}) %collective-permute-start.38) | collective-permute-done | bytes 262176 | tf_op jit(solution)/shard_map/ppermute | solution.py:1433
  267.2 3.8 %collective-permute-start.40 = (bf16[592,128]{1,0:T(8,128)(2,1)S(1)}, bf16[592,128]{1,0:T(8,128)(2,1)}, u32[]{:S(2)}, u32[]{:S(2)}) collective-permute-start(bf16[592,128]{1,0:T(8,128)(2,1)S(1)} %get-tuple-element.384), channel_id=1, source_target_pairs={{0,2},{1,3},{2,0},{3,1},{4,6},{5,7},{6,4},{7,5},{8,10},{9,11},{10,... | collective-permute-start | bytes 454664 | tf_op jit(solution)/shard_map/ppermute | solution.py:1438
  276.7 4.9 %collective-permute-done.40 = bf16[592,128]{1,0:T(8,128)(2,1)} collective-permute-done((bf16[592,128]{1,0:T(8,128)(2,1)S(1)}, bf16[592,128]{1,0:T(8,128)(2,1)}, u32[]{:S(2)}, u32[]{:S(2)}) %collective-permute-start.40) | collective-permute-done | bytes 151584 | tf_op jit(solution)/shard_map/ppermute | solution.py:1438
  281.6 3.7 %collective-permute-done.41 = bf16[592,128]{1,0:T(8,128)(2,1)} collective-permute-done((bf16[592,128]{1,0:T(8,128)(2,1)}, bf16[592,128]{1,0:T(8,128)(2,1)}, u32[]{:S(2)}, u32[]{:S(2)}) %collective-permute-start.41) | collective-permute-done | bytes 151584 | tf_op jit(solution)/shard_map/ppermute | solution.py:1438
  289.4 13.5 %collective-permute-done.44.refs_6_ = bf16[34,32,128]{2,1,0:T(8,128)(2,1)S(1)} collective-permute-done((bf16[34,32,128]{2,1,0:T(8,128)(2,1)}, bf16[34,32,128]{2,1,0:T(8,128)(2,1)S(1)}, u32[]{:S(2)}, u32[]{:S(2)}) %collective-permute-start.44) | collective-permute-done | bytes 278560 | tf_op jit(solution)/shard_map/ppermute | solution.py:1433
  302.9 5.3 %collective-permute-done.45.refs_7_ = bf16[34,32,128]{2,1,0:T(8,128)(2,1)S(1)} collective-permute-done((bf16[34,32,128]{2,1,0:T(8,128)(2,1)}, bf16[34,32,128]{2,1,0:T(8,128)(2,1)S(1)}, u32[]{:S(2)}, u32[]{:S(2)}) %collective-permute-start.45) | collective-permute-done | bytes 278560 | tf_op jit(solution)/shard_map/ppermute | solution.py:1433
  (264 shorter events, 72.8 us)
Async XLA Ops:
  6.5 20.3 %collective-permute-start.2 = (bf16[46,32,128]{2,1,0:T(8,128)(2,1)}, bf16[46,32,128]{2,1,0:T(8,128)(2,1)S(1)}, u32[]{:S(2)}, u32[]{:S(2)}) collective-permute-start(bf16[46,32,128]{2,1,0:T(8,128)(2,1)} %get-tuple-element.218), channel_id=1, source_target_pairs={{0,2},{1,3},{2,0},{3,1},{4,10},{5,11},{6,8},{7,9},{8,6},{9,7},{10,... | collective-permute-start | bytes 1130504 | tf_op jit(solution)/shard_map/ppermute | solution.py:1433
  9.5 32.7 %collective-permute-start.3 = (bf16[46,32,128]{2,1,0:T(8,128)(2,1)}, bf16[46,32,128]{2,1,0:T(8,128)(2,1)S(1)}, u32[]{:S(2)}, u32[]{:S(2)}) collective-permute-start(bf16[46,32,128]{2,1,0:T(8,128)(2,1)} %get-tuple-element.219), channel_id=1, source_target_pairs={{0,3},{1,2},{2,1},{3,0},{4,11},{5,10},{6,9},{7,8},{8,7},{9,6},{10,... | collective-permute-start | bytes 1130504 | tf_op jit(solution)/shard_map/ppermute | solution.py:1433
  49.8 22.1 %collective-permute-start.8 = (bf16[32,32,128]{2,1,0:T(8,128)(2,1)}, bf16[32,32,128]{2,1,0:T(8,128)(2,1)S(1)}, u32[]{:S(2)}, u32[]{:S(2)}) collective-permute-start(bf16[32,32,128]{2,1,0:T(8,128)(2,1)} %get-tuple-element.229), channel_id=1, source_target_pairs={{0,3},{1,2},{2,1},{3,0},{4,11},{5,10},{6,9},{7,8},{8,7},{9,6},{10,... | collective-permute-start | bytes 786440 | tf_op jit(solution)/shard_map/ppermute | solution.py:1433
  82.6 20.5 %collective-permute-start.12 = (bf16[32,32,128]{2,1,0:T(8,128)(2,1)S(1)}, bf16[32,32,128]{2,1,0:T(8,128)(2,1)S(1)}, u32[]{:S(2)}, u32[]{:S(2)}) collective-permute-start(bf16[32,32,128]{2,1,0:T(8,128)(2,1)S(1)} %copy-done.59), channel_id=1, source_target_pairs={{0,0},{1,1},{2,2},{3,3},{4,8},{5,9},{6,10},{7,11},{8,4},{9,5},{10,... | collective-permute-start | bytes 786440 | tf_op jit(solution)/shard_map/ppermute | solution.py:1433
  83.4 19.7 %collective-permute-start.13 = (bf16[32,32,128]{2,1,0:T(8,128)(2,1)S(1)}, bf16[32,32,128]{2,1,0:T(8,128)(2,1)S(1)}, u32[]{:S(2)}, u32[]{:S(2)}) collective-permute-start(bf16[32,32,128]{2,1,0:T(8,128)(2,1)S(1)} %copy-done.57), channel_id=1, source_target_pairs={{0,1},{1,0},{2,3},{3,2},{4,9},{5,8},{6,11},{7,10},{8,5},{9,4},{10,... | collective-permute-start | bytes 786440 | tf_op jit(solution)/shard_map/ppermute | solution.py:1433
  83.5 19.6 %collective-permute-start.14 = (bf16[32,32,128]{2,1,0:T(8,128)(2,1)S(1)}, bf16[32,32,128]{2,1,0:T(8,128)(2,1)S(1)}, u32[]{:S(2)}, u32[]{:S(2)}) collective-permute-start(bf16[32,32,128]{2,1,0:T(8,128)(2,1)S(1)} %copy-done.55), channel_id=1, source_target_pairs={{0,2},{1,3},{2,0},{3,1},{4,10},{5,11},{6,8},{7,9},{8,6},{9,7},{10,... | collective-permute-start | bytes 786440 | tf_op jit(solution)/shard_map/ppermute | solution.py:1433
  86.5 22.1 %collective-permute-start.15 = (bf16[32,32,128]{2,1,0:T(8,128)(2,1)S(1)}, bf16[32,32,128]{2,1,0:T(8,128)(2,1)S(1)}, u32[]{:S(2)}, u32[]{:S(2)}) collective-permute-start(bf16[32,32,128]{2,1,0:T(8,128)(2,1)S(1)} %copy-done.54), channel_id=1, source_target_pairs={{0,3},{1,2},{2,1},{3,0},{4,11},{5,10},{6,9},{7,8},{8,7},{9,6},{10,... | collective-permute-start | bytes 786440 | tf_op jit(solution)/shard_map/ppermute | solution.py:1433
  89.5 19.1 %collective-permute-start.11 = (f32[8,64,128]{2,1,0:T(8,128)S(1)}, f32[8,64,128]{2,1,0:T(8,128)S(1)}, u32[]{:S(2)}, u32[]{:S(2)}) collective-permute-start(f32[8,64,128]{2,1,0:T(8,128)S(1)} %pad_maximum_fusion.6.bias_ref), channel_id=1, source_target_pairs={{0,8},{8,0},{16,24},{24,16},{1,9},{9,1},{17,25},{25,17},{2,10},{10... | collective-permute-start | bytes 786440 | tf_op jit(solution)/shard_map/ppermute | solution.py:1441
  108.7 27.4 %collective-permute-start.16 = (bf16[45,32,128]{2,1,0:T(8,128)(2,1)S(1)}, bf16[45,32,128]{2,1,0:T(8,128)(2,1)S(1)}, u32[]{:S(2)}, u32[]{:S(2)}) collective-permute-start(bf16[45,32,128]{2,1,0:T(8,128)(2,1)S(1)} %copy-done.53), channel_id=1, source_target_pairs={{0,0},{1,1},{2,2},{3,3},{4,8},{5,9},{6,10},{7,11},{8,4},{9,5},{10,... | collective-permute-start | bytes 1105928 | tf_op jit(solution)/shard_map/ppermute | solution.py:1433
  109.4 26.7 %collective-permute-start.17 = (bf16[45,32,128]{2,1,0:T(8,128)(2,1)S(1)}, bf16[45,32,128]{2,1,0:T(8,128)(2,1)S(1)}, u32[]{:S(2)}, u32[]{:S(2)}) collective-permute-start(bf16[45,32,128]{2,1,0:T(8,128)(2,1)S(1)} %copy-done.52), channel_id=1, source_target_pairs={{0,1},{1,0},{2,3},{3,2},{4,9},{5,8},{6,11},{7,10},{8,5},{9,4},{10,... | collective-permute-start | bytes 1105928 | tf_op jit(solution)/shard_map/ppermute | solution.py:1433
  109.5 26.7 %collective-permute-start.18 = (bf16[45,32,128]{2,1,0:T(8,128)(2,1)S(1)}, bf16[45,32,128]{2,1,0:T(8,128)(2,1)S(1)}, u32[]{:S(2)}, u32[]{:S(2)}) collective-permute-start(bf16[45,32,128]{2,1,0:T(8,128)(2,1)S(1)} %copy-done.51), channel_id=1, source_target_pairs={{0,2},{1,3},{2,0},{3,1},{4,10},{5,11},{6,8},{7,9},{8,6},{9,7},{10,... | collective-permute-start | bytes 1105928 | tf_op jit(solution)/shard_map/ppermute | solution.py:1433
  112.7 29.2 %collective-permute-start.19 = (bf16[45,32,128]{2,1,0:T(8,128)(2,1)S(1)}, bf16[45,32,128]{2,1,0:T(8,128)(2,1)S(1)}, u32[]{:S(2)}, u32[]{:S(2)}) collective-permute-start(bf16[45,32,128]{2,1,0:T(8,128)(2,1)S(1)} %copy-done.50), channel_id=1, source_target_pairs={{0,3},{1,2},{2,1},{3,0},{4,11},{5,10},{6,9},{7,8},{8,7},{9,6},{10,... | collective-permute-start | bytes 1105928 | tf_op jit(solution)/shard_map/ppermute | solution.py:1433
  142.0 33.6 %collective-permute-start.24 = (bf16[4,416,128]{2,1,0:T(8,128)(2,1)S(1)}, bf16[4,416,128]{2,1,0:T(8,128)(2,1)S(1)}, u32[]{:S(2)}, u32[]{:S(2)}) collective-permute-start(bf16[4,416,128]{2,1,0:T(8,128)(2,1)S(1)} %pad_maximum_fusion.3), channel_id=1, source_target_pairs={{0,4},{4,0},{1,5},{5,1},{2,6},{6,2},{3,7},{7,3},{8,12},{12,8},{9,1... | collective-permute-start | bytes 1277960 | tf_op jit(solution)/shard_map/ppermute | solution.py:1466
  147.8 27.9 %collective-permute-start.20 = (bf16[32,32,128]{2,1,0:T(8,128)(2,1)}, bf16[32,32,128]{2,1,0:T(8,128)(2,1)S(1)}, u32[]{:S(2)}, u32[]{:S(2)}) collective-permute-start(bf16[32,32,128]{2,1,0:T(8,128)(2,1)} %get-tuple-element.282), channel_id=1, source_target_pairs={{0,0},{1,1},{2,2},{3,3},{4,8},{5,9},{6,10},{7,11},{8,4},{9,5},{10,... | collective-permute-start | bytes 786440 | tf_op jit(solution)/shard_map/ppermute | solution.py:1433
  149.4 26.4 %collective-permute-start.21 = (bf16[32,32,128]{2,1,0:T(8,128)(2,1)}, bf16[32,32,128]{2,1,0:T(8,128)(2,1)S(1)}, u32[]{:S(2)}, u32[]{:S(2)}) collective-permute-start(bf16[32,32,128]{2,1,0:T(8,128)(2,1)} %get-tuple-element.283), channel_id=1, source_target_pairs={{0,1},{1,0},{2,3},{3,2},{4,9},{5,8},{6,11},{7,10},{8,5},{9,4},{10,... | collective-permute-start | bytes 786440 | tf_op jit(solution)/shard_map/ppermute | solution.py:1433
  149.4 26.4 %collective-permute-start.22 = (bf16[32,32,128]{2,1,0:T(8,128)(2,1)}, bf16[32,32,128]{2,1,0:T(8,128)(2,1)S(1)}, u32[]{:S(2)}, u32[]{:S(2)}) collective-permute-start(bf16[32,32,128]{2,1,0:T(8,128)(2,1)} %get-tuple-element.284), channel_id=1, source_target_pairs={{0,2},{1,3},{2,0},{3,1},{4,10},{5,11},{6,8},{7,9},{8,6},{9,7},{10,... | collective-permute-start | bytes 786440 | tf_op jit(solution)/shard_map/ppermute | solution.py:1433
  152.6 23.9 %collective-permute-start.23 = (bf16[32,32,128]{2,1,0:T(8,128)(2,1)}, bf16[32,32,128]{2,1,0:T(8,128)(2,1)S(1)}, u32[]{:S(2)}, u32[]{:S(2)}) collective-permute-start(bf16[32,32,128]{2,1,0:T(8,128)(2,1)} %get-tuple-element.285), channel_id=1, source_target_pairs={{0,3},{1,2},{2,1},{3,0},{4,11},{5,10},{6,9},{7,8},{8,7},{9,6},{10,... | collective-permute-start | bytes 786440 | tf_op jit(solution)/shard_map/ppermute | solution.py:1433
  192.5 19.2 %collective-permute-start.29 = (bf16[4,480,128]{2,1,0:T(8,128)(2,1)S(1)}, bf16[4,480,128]{2,1,0:T(8,128)(2,1)S(1)}, u32[]{:S(2)}, u32[]{:S(2)}) collective-permute-start(bf16[4,480,128]{2,1,0:T(8,128)(2,1)S(1)} %get-tuple-element.381), channel_id=1, source_target_pairs={{0,4},{4,0},{1,5},{5,1},{2,6},{6,2},{3,7},{7,3},{8,12},{12,8},{9,1... | collective-permute-start | bytes 1474568 | tf_op jit(solution)/shard_map/ppermute | solution.py:1530
  211.7 23.2 %collective-permute-start.30 = (bf16[32,32,128]{2,1,0:T(8,128)(2,1)S(1)}, bf16[32,32,128]{2,1,0:T(8,128)(2,1)S(1)}, u32[]{:S(2)}, u32[]{:S(2)}) collective-permute-start(bf16[32,32,128]{2,1,0:T(8,128)(2,1)S(1)} %copy-done.61), channel_id=1, source_target_pairs={{0,0},{1,1},{2,2},{3,3},{4,8},{5,9},{6,10},{7,11},{8,4},{9,5},{10,... | collective-permute-start | bytes 786440 | tf_op jit(solution)/shard_map/ppermute | solution.py:1433
  212.6 22.3 %collective-permute-start.31 = (bf16[32,32,128]{2,1,0:T(8,128)(2,1)S(1)}, bf16[32,32,128]{2,1,0:T(8,128)(2,1)S(1)}, u32[]{:S(2)}, u32[]{:S(2)}) collective-permute-start(bf16[32,32,128]{2,1,0:T(8,128)(2,1)S(1)} %copy-done.60), channel_id=1, source_target_pairs={{0,1},{1,0},{2,3},{3,2},{4,9},{5,8},{6,11},{7,10},{8,5},{9,4},{10,... | collective-permute-start | bytes 786440 | tf_op jit(solution)/shard_map/ppermute | solution.py:1433
  212.7 22.2 %collective-permute-start.32 = (bf16[32,32,128]{2,1,0:T(8,128)(2,1)S(1)}, bf16[32,32,128]{2,1,0:T(8,128)(2,1)S(1)}, u32[]{:S(2)}, u32[]{:S(2)}) collective-permute-start(bf16[32,32,128]{2,1,0:T(8,128)(2,1)S(1)} %copy-done.58), channel_id=1, source_target_pairs={{0,2},{1,3},{2,0},{3,1},{4,10},{5,11},{6,8},{7,9},{8,6},{9,7},{10,... | collective-permute-start | bytes 786440 | tf_op jit(solution)/shard_map/ppermute | solution.py:1433
  215.9 22.6 %collective-permute-start.33 = (bf16[32,32,128]{2,1,0:T(8,128)(2,1)S(1)}, bf16[32,32,128]{2,1,0:T(8,128)(2,1)S(1)}, u32[]{:S(2)}, u32[]{:S(2)}) collective-permute-start(bf16[32,32,128]{2,1,0:T(8,128)(2,1)S(1)} %copy-done.56), channel_id=1, source_target_pairs={{0,3},{1,2},{2,1},{3,0},{4,11},{5,10},{6,9},{7,8},{8,7},{9,6},{10,... | collective-permute-start | bytes 786440 | tf_op jit(solution)/shard_map/ppermute | solution.py:1433
  216.3 18.5 %collective-permute-start.34 = (bf16[4,240,128]{2,1,0:T(8,128)(2,1)S(1)}, bf16[4,240,128]{2,1,0:T(8,128)(2,1)S(1)}, u32[]{:S(2)}, u32[]{:S(2)}) collective-permute-start(bf16[4,240,128]{2,1,0:T(8,128)(2,1)S(1)} %get-tuple-element.386), channel_id=1, source_target_pairs={{0,16},{8,24},{16,0},{24,8},{1,17},{9,25},{17,1},{25,9},{2,18},{10... | collective-permute-start | bytes 737288 | tf_op jit(solution)/shard_map/ppermute | solution.py:1530
  238.6 21.2 %collective-permute-start.35 = (bf16[32,32,128]{2,1,0:T(8,128)(2,1)}, bf16[32,32,128]{2,1,0:T(8,128)(2,1)S(1)}, u32[]{:S(2)}, u32[]{:S(2)}) collective-permute-start(bf16[32,32,128]{2,1,0:T(8,128)(2,1)} %get-tuple-element.327), channel_id=1, source_target_pairs={{0,0},{1,1},{2,2},{3,3},{4,8},{5,9},{6,10},{7,11},{8,4},{9,5},{10,... | collective-permute-start | bytes 786440 | tf_op jit(solution)/shard_map/ppermute | solution.py:1433
  240.2 19.6 %collective-permute-start.36 = (bf16[32,32,128]{2,1,0:T(8,128)(2,1)}, bf16[32,32,128]{2,1,0:T(8,128)(2,1)S(1)}, u32[]{:S(2)}, u32[]{:S(2)}) collective-permute-start(bf16[32,32,128]{2,1,0:T(8,128)(2,1)} %get-tuple-element.328), channel_id=1, source_target_pairs={{0,1},{1,0},{2,3},{3,2},{4,9},{5,8},{6,11},{7,10},{8,5},{9,4},{10,... | collective-permute-start | bytes 786440 | tf_op jit(solution)/shard_map/ppermute | solution.py:1433
  240.2 19.6 %collective-permute-start.37 = (bf16[32,32,128]{2,1,0:T(8,128)(2,1)}, bf16[32,32,128]{2,1,0:T(8,128)(2,1)S(1)}, u32[]{:S(2)}, u32[]{:S(2)}) collective-permute-start(bf16[32,32,128]{2,1,0:T(8,128)(2,1)} %get-tuple-element.329), channel_id=1, source_target_pairs={{0,2},{1,3},{2,0},{3,1},{4,10},{5,11},{6,8},{7,9},{8,6},{9,7},{10,... | collective-permute-start | bytes 786440 | tf_op jit(solution)/shard_map/ppermute | solution.py:1433
  243.7 21.7 %collective-permute-start.38 = (bf16[32,32,128]{2,1,0:T(8,128)(2,1)}, bf16[32,32,128]{2,1,0:T(8,128)(2,1)S(1)}, u32[]{:S(2)}, u32[]{:S(2)}) collective-permute-start(bf16[32,32,128]{2,1,0:T(8,128)(2,1)} %get-tuple-element.330), channel_id=1, source_target_pairs={{0,3},{1,2},{2,1},{3,0},{4,11},{5,10},{6,9},{7,8},{8,7},{9,6},{10,... | collective-permute-start | bytes 786440 | tf_op jit(solution)/shard_map/ppermute | solution.py:1433
  271.0 18.3 %collective-permute-start.42 = (bf16[34,32,128]{2,1,0:T(8,128)(2,1)}, bf16[34,32,128]{2,1,0:T(8,128)(2,1)S(1)}, u32[]{:S(2)}, u32[]{:S(2)}) collective-permute-start(bf16[34,32,128]{2,1,0:T(8,128)(2,1)} %get-tuple-element.352), channel_id=1, source_target_pairs={{0,0},{1,1},{2,2},{3,3},{4,8},{5,9},{6,10},{7,11},{8,4},{9,5},{10,... | collective-permute-start | bytes 835592 | tf_op jit(solution)/shard_map/ppermute | solution.py:1433
  272.7 16.6 %collective-permute-start.43 = (bf16[34,32,128]{2,1,0:T(8,128)(2,1)}, bf16[34,32,128]{2,1,0:T(8,128)(2,1)S(1)}, u32[]{:S(2)}, u32[]{:S(2)}) collective-permute-start(bf16[34,32,128]{2,1,0:T(8,128)(2,1)} %get-tuple-element.353), channel_id=1, source_target_pairs={{0,1},{1,0},{2,3},{3,2},{4,9},{5,8},{6,11},{7,10},{8,5},{9,4},{10,... | collective-permute-start | bytes 835592 | tf_op jit(solution)/shard_map/ppermute | solution.py:1433
  274.2 28.7 %collective-permute-start.44 = (bf16[34,32,128]{2,1,0:T(8,128)(2,1)}, bf16[34,32,128]{2,1,0:T(8,128)(2,1)S(1)}, u32[]{:S(2)}, u32[]{:S(2)}) collective-permute-start(bf16[34,32,128]{2,1,0:T(8,128)(2,1)} %get-tuple-element.354), channel_id=1, source_target_pairs={{0,2},{1,3},{2,0},{3,1},{4,10},{5,11},{6,8},{7,9},{8,6},{9,7},{10,... | collective-permute-start | bytes 835592 | tf_op jit(solution)/shard_map/ppermute | solution.py:1433
  281.6 26.5 %collective-permute-start.45 = (bf16[34,32,128]{2,1,0:T(8,128)(2,1)}, bf16[34,32,128]{2,1,0:T(8,128)(2,1)S(1)}, u32[]{:S(2)}, u32[]{:S(2)}) collective-permute-start(bf16[34,32,128]{2,1,0:T(8,128)(2,1)} %get-tuple-element.355), channel_id=1, source_target_pairs={{0,3},{1,2},{2,1},{3,0},{4,11},{5,10},{6,9},{7,8},{8,7},{9,6},{10,... | collective-permute-start | bytes 835592 | tf_op jit(solution)/shard_map/ppermute | solution.py:1433
  286.5 21.7 %collective-permute-start.46 = (bf16[592,128]{1,0:T(8,128)(2,1)S(1)}, bf16[592,128]{1,0:T(8,128)(2,1)S(1)}, u32[]{:S(2)}, u32[]{:S(2)}) collective-permute-start(bf16[592,128]{1,0:T(8,128)(2,1)S(1)} %fusion.13), channel_id=1, source_target_pairs={{0,16},{8,24},{16,0},{24,8},{1,17},{9,25},{17,1},{25,9},{2,18},{10... | collective-permute-start | bytes 454664 | tf_op jit(solution)/shard_map/ppermute | solution.py:1603
  (83 other events, 1752.4 us)
